TPU v7x, 32 devices: a whole 2x2x4 slice. The times are simulated.
32 devices in a mesh: pb: 8 (over z, y), col: 4 (over x, core).
Axes of the slice: x: 2, y: 2, z: 4, core: 2. Of those that a mesh axis runs over, the one named last changes fastest.
Arguments:
- queries: bfloat16 [12288, 1024], P(('pb', 'col')), may hold values from -5 to 18
- groups: bfloat16 [1024, 1024], P(('pb', 'col')), may hold values from -5 to 6
- teacher: bfloat16 [12288, 512], P(('pb', 'col')), may hold values from -60 to 410
- tile_mask: int32 [96, 4], P(('pb', 'col')), may hold values from 0 to 1, as said below
- weights: float32 [12288], P(('pb', 'col')), may hold values from 0.25 to 4
Outputs:
- query_grad: float32 [12288, 1024], P(('pb', 'col'))
- group_grad: float32 [1024, 1024], P(('pb', 'col'))
Inputs may be any that keep to these rules, and one draw needn't show every extreme that they name: `tile_mask`: every row of tiles has at least one 1; in every draw some rows of tiles are all ones.
All inputs are finite; a program needn't handle non-finite values.
Results may differ from a plain program's by a relative error of at most 0.0095.
Values may be sent and summed in bfloat16 or wider, within the bound.
No kernel may reach another device: no remote copies, remote signals or barrier semaphores. Data moves between devices by JAX's collectives and lax.ppermute only.
A program may use at most 64 MiB of HBM per device.

v0:
```python
import math

import jax
import jax.numpy as jnp
from jax import lax
from jax.sharding import PartitionSpec as P

very_negative = -1e30


def passed_along(block, axis, distance):
    devices = range(lax.axis_size(axis))
    route = [((i - distance) % len(devices), i) for i in devices]
    return lax.ppermute(block, axis, route)


def product_rows(left, right):
    return lax.dot_general(
        left, right, (((1,), (1,)), ((), ())), preferred_element_type=jnp.float32
    )


def term_rows(grads, queries):
    return lax.dot_general(
        grads, queries, (((0,), (0,)), ((), ())), preferred_element_type=jnp.float32
    )


def update_stats(scores, live_cols, row_max, row_sum):
    new_max = jnp.maximum(
        row_max, jnp.max(jnp.where(live_cols, scores, very_negative), axis=1, keepdims=True)
    )
    added = jnp.sum(jnp.where(live_cols, jnp.exp(scores - new_max), 0.0), axis=1, keepdims=True)
    return (new_max, row_sum * jnp.exp(row_max - new_max) + added)


def on_device(queries, groups, teacher, tile_mask, weights):
    score_scale = 2.0 / math.sqrt(queries.shape[1])
    own_rows = groups.shape[0]
    panel_rows = own_rows * lax.axis_size("col")
    window = teacher.shape[1]
    count_steps = window // panel_rows
    tile_rows = queries.shape[0] // tile_mask.shape[0]
    tile_cols = window // tile_mask.shape[1]
    live_mask = jnp.repeat(jnp.repeat(tile_mask, tile_rows, axis=0), tile_cols, axis=1) > 0
    taught = teacher.astype(jnp.float32)
    teach_max = jnp.max(jnp.where(live_mask, taught, -jnp.inf), axis=1, keepdims=True)
    teach_exp = jnp.where(live_mask, jnp.exp(taught - teach_max), 0.0)
    target = teach_exp / jnp.sum(teach_exp, axis=1, keepdims=True)
    row_scale = (weights * score_scale)[:, None]
    row_max = jnp.full((queries.shape[0], 1), very_negative, jnp.float32)
    row_sum = jnp.zeros((queries.shape[0], 1), jnp.float32)
    query_grad = jnp.zeros(queries.shape, jnp.float32)
    visiting = groups
    kept_rows = []
    kept_scores = []
    for cycle_step in range(count_steps):
        if cycle_step > 0:
            visiting = passed_along(visiting, "pb", 1)
        gathered = lax.all_gather(visiting, "col", axis=0, tiled=True)
        scores = product_rows(queries, gathered) * score_scale
        live_cols = live_mask[:, cycle_step * panel_rows : (cycle_step + 1) * panel_rows]
        row_max, row_sum = update_stats(scores, live_cols, row_max, row_sum)
        kept_rows.append(gathered)
        kept_scores.append(scores)
    group_grad = None
    for cycle_step in reversed(range(count_steps)):
        grad_scores = kept_scores[cycle_step]
        grad_live_cols = lax.dynamic_slice_in_dim(
            live_mask, cycle_step * panel_rows + 0, panel_rows, 1
        )
        goal = lax.dynamic_slice_in_dim(target, cycle_step * panel_rows + 0, panel_rows, 1)
        student = jnp.where(grad_live_cols, jnp.exp(grad_scores - row_max), 0.0) / row_sum
        grads = (row_scale * (student - goal)).astype(jnp.bfloat16)
        query_grad = query_grad + jnp.dot(
            grads, kept_rows[cycle_step], preferred_element_type=jnp.float32
        )
        summed = lax.psum_scatter(
            term_rows(grads, queries).astype(jnp.bfloat16), "col", scatter_dimension=0, tiled=True
        ).astype(jnp.float32)
        if group_grad is None:
            group_grad = summed
        else:
            group_grad = (
                passed_along(group_grad.astype(jnp.bfloat16), "pb", -1).astype(group_grad.dtype)
                + summed
            )
    return (query_grad, group_grad)


def solution(mesh):
    placed = (
        P(("pb", "col"), None),
        P(("pb", "col"), None),
        P(("pb", "col"), None),
        P(("pb", "col"), None),
        P(("pb", "col")),
    )
    return jax.shard_map(
        on_device,
        mesh=mesh,
        in_specs=placed,
        out_specs=(P(("pb", "col"), None), P(("pb", "col"), None)),
        check_vma=False,
    )
```

profile of v0, /device:TPU:0, one launch (start us, length us, event | category | flops | bytes accessed | tf_op | source)
XLA Modules:
  0.0 138.8 jit_solution(14129354540793993720)
XLA Ops:
  7.2 3.0 %collective-permute-start = (bf16[32,1024]{1,0:T(8,128)(2,1)}, bf16[32,1024]{1,0:T(8,128)(2,1)S(1)}, u32[]{:S(2)}, u32[]{:S(2)}) collective-permute-start(bf16[32,1024]{1,0:T(8,128)(2,1)} %param.6), channel_id=1, source_target_pairs={{28,0},{0,4},{4,8},{8,12},{12,16},{16,20},{20,24},{24,28},{29,1},{... | collective-permute-start | bytes 196616 | tf_op jit(solution)/shard_map/ppermute | solution.py:14
  10.3 6.0 %all_gather.13 = bf16[128,1024]{1,0:T(8,128)(2,1)S(1)} all-gather(bf16[32,1024]{1,0:T(8,128)(2,1)} %param.6), channel_id=1, replica_groups=mesh['pb'=8,'col'=4] {'col'}, dimensions={0}, use_global_device_ids=true | all-gather | bytes 327680 | tf_op jit(solution)/shard_map/all_gather | solution.py:60
  18.8 1.6 %collective-permute-start.1 = (bf16[32,1024]{1,0:T(8,128)(2,1)S(1)}, bf16[32,1024]{1,0:T(8,128)(2,1)S(1)}, u32[]{:S(2)}, u32[]{:S(2)}) collective-permute-start(bf16[32,1024]{1,0:T(8,128)(2,1)S(1)} %collective-permute-done), channel_id=1, source_target_pairs={{28,0},{0,4},{4,8},{8,12},{12,16},{16,20},{20,24},{24,28},{29,1},{... | collective-permute-start | bytes 196616 | tf_op jit(solution)/shard_map/ppermute | solution.py:14
  20.4 5.8 %all_gather.14 = bf16[128,1024]{1,0:T(8,128)(2,1)S(1)} all-gather(bf16[32,1024]{1,0:T(8,128)(2,1)S(1)} %collective-permute-done), channel_id=1, replica_groups=mesh['pb'=8,'col'=4] {'col'}, dimensions={0}, use_global_device_ids=true | all-gather | bytes 327680 | tf_op jit(solution)/shard_map/all_gather | solution.py:60
  26.5 1.6 %collective-permute-start.2 = (bf16[32,1024]{1,0:T(8,128)(2,1)S(1)}, bf16[32,1024]{1,0:T(8,128)(2,1)S(1)}, u32[]{:S(2)}, u32[]{:S(2)}) collective-permute-start(bf16[32,1024]{1,0:T(8,128)(2,1)S(1)} %collective-permute-done.1), channel_id=1, source_target_pairs={{28,0},{0,4},{4,8},{8,12},{12,16},{16,20},{20,24},{24,28},{29,1},{... | collective-permute-start | bytes 196616 | tf_op jit(solution)/shard_map/ppermute | solution.py:14
  28.1 5.8 %all_gather.15 = bf16[128,1024]{1,0:T(8,128)(2,1)S(1)} all-gather(bf16[32,1024]{1,0:T(8,128)(2,1)S(1)} %collective-permute-done.1), channel_id=1, replica_groups=mesh['pb'=8,'col'=4] {'col'}, dimensions={0}, use_global_device_ids=true | all-gather | bytes 327680 | tf_op jit(solution)/shard_map/all_gather | solution.py:60
  34.2 5.9 %all_gather.12 = bf16[128,1024]{1,0:T(8,128)(2,1)S(1)} all-gather(bf16[32,1024]{1,0:T(8,128)(2,1)S(1)} %collective-permute-done.2), channel_id=1, replica_groups=mesh['pb'=8,'col'=4] {'col'}, dimensions={0}, use_global_device_ids=true | all-gather | bytes 327680 | tf_op jit(solution)/shard_map/all_gather | solution.py:60
  40.9 1.0 fusion.12
  41.9 1.0 convolution_convert_fusion.3
  43.0 1.9 %convolution_convert_fusion.2 = bf16[128,1024]{1,0:T(8,128)(2,1)} fusion(bf16[384,128]{0,1:T(8,128)(2,1)} %get-tuple-element.16, bf16[384,1024]{1,0:T(8,128)(2,1)S(1)} %copy-done), kind=kOutput, calls=%fused_computation.3 | convolution fusion | flops 100794368 | bytes 1146880 | tf_op jit(solution)/shard_map/dot_general | solution.py:24
  44.9 1.3 fusion.17
  46.3 1.9 %convolution_convert_fusion.1 = bf16[128,1024]{1,0:T(8,128)(2,1)} fusion(bf16[384,128]{0,1:T(8,128)(2,1)} %get-tuple-element.15, bf16[384,1024]{1,0:T(8,128)(2,1)S(1)} %copy-done), kind=kOutput, calls=%fused_computation.2 | convolution fusion | flops 100794368 | bytes 1146880 | tf_op jit(solution)/shard_map/dot_general | solution.py:24
  48.2 2.4 %fusion.18 = f32[384,1024]{1,0:T(8,128)} fusion(bf16[384,128]{0,1:T(8,128)(2,1)} %get-tuple-element.15, bf16[128,1024]{1,0:T(8,128)(2,1)S(1)} %all_gather.14), kind=kOutput, calls=%fused_computation.48 | convolution fusion | flops 100663296 | bytes 1933312 | tf_op jit(solution)/shard_map/dot_general | solution.py:75
  50.7 12.3 %reduce-scatter.5.cloned.1.call-done = bf16[32,1024]{1,0:T(8,128)(2,1)} async-done(((bf16[128,1024]{1,0:T(8,128)(2,1)}), bf16[32,1024]{1,0:T(8,128)(2,1)}) %reduce-scatter.5.cloned.1.call-update) | async-done | bytes 65552 | tf_op jit(solution)/shard_map/reduce_scatter | solution.py:78
  63.0 4.2 %collective-permute-start.3 = (bf16[32,1024]{1,0:T(8,128)(2,1)}, bf16[32,1024]{1,0:T(8,128)(2,1)S(1)}, u32[]{:S(2)}, u32[]{:S(2)}) collective-permute-start(bf16[32,1024]{1,0:T(8,128)(2,1)} %reduce-scatter.5.cloned.1.call-done), channel_id=1, source_target_pairs={{4,0},{8,4},{12,8},{16,12},{20,16},{24,20},{28,24},{0,28},{5,1},{9... | collective-permute-start | bytes 196616 | tf_op jit(solution)/shard_map/ppermute | solution.py:14
  67.3 1.5 %fusion.19 = f32[384,1024]{1,0:T(8,128)} fusion(bf16[384,128]{0,1:T(8,128)(2,1)S(1)} %copy-done.1, bf16[128,1024]{1,0:T(8,128)(2,1)S(1)} %all_gather.13), kind=kOutput, calls=%fused_computation.49 | convolution fusion | flops 100663296 | bytes 1933312 | tf_op jit(solution)/shard_map/dot_general | solution.py:75
  68.8 16.9 %reduce-scatter.7.cloned.1.call-done = bf16[32,1024]{1,0:T(8,128)(2,1)} async-done(((bf16[128,1024]{1,0:T(8,128)(2,1)}), bf16[32,1024]{1,0:T(8,128)(2,1)}) %reduce-scatter.7.cloned.1.call-update) | async-done | bytes 65552 | tf_op jit(solution)/shard_map/reduce_scatter | solution.py:78
  86.6 4.3 %collective-permute-start.4 = (bf16[32,1024]{1,0:T(8,128)(2,1)S(1)}, bf16[32,1024]{1,0:T(8,128)(2,1)S(1)}, u32[]{:S(2)}, u32[]{:S(2)}) collective-permute-start(bf16[32,1024]{1,0:T(8,128)(2,1)S(1)} %add_convert_fusion.1), channel_id=1, source_target_pairs={{4,0},{8,4},{12,8},{16,12},{20,16},{24,20},{28,24},{0,28},{5,1},{9... | collective-permute-start | bytes 196616 | tf_op jit(solution)/shard_map/ppermute | solution.py:14
  90.9 1.0 convolution_convert_fusion
  91.9 16.3 %reduce-scatter.9.cloned.1.call-done = bf16[32,1024]{1,0:T(8,128)(2,1)} async-done(((bf16[128,1024]{1,0:T(8,128)(2,1)}), bf16[32,1024]{1,0:T(8,128)(2,1)}) %reduce-scatter.9.cloned.1.call-update) | async-done | bytes 65552 | tf_op jit(solution)/shard_map/reduce_scatter | solution.py:78
  109.1 4.3 %collective-permute-start.5 = (bf16[32,1024]{1,0:T(8,128)(2,1)S(1)}, bf16[32,1024]{1,0:T(8,128)(2,1)S(1)}, u32[]{:S(2)}, u32[]{:S(2)}) collective-permute-start(bf16[32,1024]{1,0:T(8,128)(2,1)S(1)} %add_convert_fusion), channel_id=1, source_target_pairs={{4,0},{8,4},{12,8},{16,12},{20,16},{24,20},{28,24},{0,28},{5,1},{9... | collective-permute-start | bytes 196616 | tf_op jit(solution)/shard_map/ppermute | solution.py:14
  113.4 3.4 %add_add_fusion = f32[384,1024]{1,0:T(8,128)} fusion(f32[384,1024]{1,0:T(8,128)} %fusion.19, f32[384,1024]{1,0:T(8,128)} %fusion.18, f32[384,1024]{1,0:T(8,128)S(1)} %fusion.17, bf16[384,128]{0,1:T(8,128)(2,1)S(1)} %get-tuple-element.13, bf16[128,1024]{1,0:T(8,128)(2,1)S(1)} %all_gather.12), kind=kOutput, calls=%fused_computation | convolution fusion | flops 101842944 | bytes 6651904 | tf_op jit(solution)/shard_map/dot_general | solution.py:75
  116.8 14.0 %reduce-scatter.11.cloned.1.call-done = bf16[32,1024]{1,0:T(8,128)(2,1)} async-done(((bf16[128,1024]{1,0:T(8,128)(2,1)}), bf16[32,1024]{1,0:T(8,128)(2,1)}) %reduce-scatter.11.cloned.1.call-update) | async-done | bytes 65552 | tf_op jit(solution)/shard_map/reduce_scatter | solution.py:78
  130.8 1.5 %convert_add_fusion = f32[32,1024]{1,0:T(8,128)} fusion(bf16[32,1024]{1,0:T(8,128)(2,1)} %reduce-scatter.11.cloned.1.call-done, bf16[32,1024]{1,0:T(8,128)(2,1)S(1)} %collective-permute-done.5), kind=kLoop, calls=%fused_computation.36 | loop fusion | flops 98304 | bytes 262144 | tf_op jit(solution)/shard_map/add | solution.py:85
  (37 shorter events, 6.0 us)
Async XLA Ops:
  7.2 10.4 %copy-start = (bf16[384,1024]{1,0:T(8,128)(2,1)S(1)}, bf16[384,1024]{1,0:T(8,128)(2,1)}, u32[]{:S(2)}) copy-start(bf16[384,1024]{1,0:T(8,128)(2,1)} %param.5) | copy-start | bytes 2359300
  7.2 10.9 %copy-start.2 = (bf16[384,512]{1,0:T(8,128)(2,1)S(1)}, bf16[384,512]{1,0:T(8,128)(2,1)}, u32[]{:S(2)}) copy-start(bf16[384,512]{1,0:T(8,128)(2,1)} %param.7) | copy-start | bytes 1179652
  7.2 55.8 %reduce-scatter.5.cloned.1.call-start = ((), (), s32[]{:S(2)}) async-start(), calls=%async_computation.4 | async-start | bytes 327680 | tf_op jit(solution)/shard_map/reduce_scatter | solution.py:78
  7.2 11.5 %collective-permute-start = (bf16[32,1024]{1,0:T(8,128)(2,1)}, bf16[32,1024]{1,0:T(8,128)(2,1)S(1)}, u32[]{:S(2)}, u32[]{:S(2)}) collective-permute-start(bf16[32,1024]{1,0:T(8,128)(2,1)} %param.6), channel_id=1, source_target_pairs={{28,0},{0,4},{4,8},{8,12},{12,16},{16,20},{20,24},{24,28},{29,1},{... | collective-permute-start | bytes 196616 | tf_op jit(solution)/shard_map/ppermute | solution.py:14
  18.8 7.7 %collective-permute-start.1 = (bf16[32,1024]{1,0:T(8,128)(2,1)S(1)}, bf16[32,1024]{1,0:T(8,128)(2,1)S(1)}, u32[]{:S(2)}, u32[]{:S(2)}) collective-permute-start(bf16[32,1024]{1,0:T(8,128)(2,1)S(1)} %collective-permute-done), channel_id=1, source_target_pairs={{28,0},{0,4},{4,8},{8,12},{12,16},{16,20},{20,24},{24,28},{29,1},{... | collective-permute-start | bytes 196616 | tf_op jit(solution)/shard_map/ppermute | solution.py:14
  26.5 7.7 %collective-permute-start.2 = (bf16[32,1024]{1,0:T(8,128)(2,1)S(1)}, bf16[32,1024]{1,0:T(8,128)(2,1)S(1)}, u32[]{:S(2)}, u32[]{:S(2)}) collective-permute-start(bf16[32,1024]{1,0:T(8,128)(2,1)S(1)} %collective-permute-done.1), channel_id=1, source_target_pairs={{28,0},{0,4},{4,8},{8,12},{12,16},{16,20},{20,24},{24,28},{29,1},{... | collective-permute-start | bytes 196616 | tf_op jit(solution)/shard_map/ppermute | solution.py:14
  42.9 42.8 %reduce-scatter.7.cloned.1.call-start = ((), (), s32[]{:S(2)}) async-start(), calls=%async_computation.5 | async-start | bytes 327680 | tf_op jit(solution)/shard_map/reduce_scatter | solution.py:78
  46.2 62.0 %reduce-scatter.9.cloned.1.call-start = ((), (), s32[]{:S(2)}) async-start(), calls=%async_computation.6 | async-start | bytes 327680 | tf_op jit(solution)/shard_map/reduce_scatter | solution.py:78
  46.2 21.0 %copy-start.1 = (bf16[384,128]{0,1:T(8,128)(2,1)S(1)}, bf16[384,128]{0,1:T(8,128)(2,1)}, u32[]{:S(2)}) copy-start(bf16[384,128]{0,1:T(8,128)(2,1)} %get-tuple-element.14) | copy-start | bytes 294916
  50.6 80.1 %reduce-scatter.11.cloned.1.call-start = ((), (), s32[]{:S(2)}) async-start(), calls=%async_computation.7 | async-start | bytes 327680 | tf_op jit(solution)/shard_map/reduce_scatter | solution.py:78
  63.0 22.7 %collective-permute-start.3 = (bf16[32,1024]{1,0:T(8,128)(2,1)}, bf16[32,1024]{1,0:T(8,128)(2,1)S(1)}, u32[]{:S(2)}, u32[]{:S(2)}) collective-permute-start(bf16[32,1024]{1,0:T(8,128)(2,1)} %reduce-scatter.5.cloned.1.call-done), channel_id=1, source_target_pairs={{4,0},{8,4},{12,8},{16,12},{20,16},{24,20},{28,24},{0,28},{5,1},{9... | collective-permute-start | bytes 196616 | tf_op jit(solution)/shard_map/ppermute | solution.py:14
  86.6 21.6 %collective-permute-start.4 = (bf16[32,1024]{1,0:T(8,128)(2,1)S(1)}, bf16[32,1024]{1,0:T(8,128)(2,1)S(1)}, u32[]{:S(2)}, u32[]{:S(2)}) collective-permute-start(bf16[32,1024]{1,0:T(8,128)(2,1)S(1)} %add_convert_fusion.1), channel_id=1, source_target_pairs={{4,0},{8,4},{12,8},{16,12},{20,16},{24,20},{28,24},{0,28},{5,1},{9... | collective-permute-start | bytes 196616 | tf_op jit(solution)/shard_map/ppermute | solution.py:14
  109.1 21.7 %collective-permute-start.5 = (bf16[32,1024]{1,0:T(8,128)(2,1)S(1)}, bf16[32,1024]{1,0:T(8,128)(2,1)S(1)}, u32[]{:S(2)}, u32[]{:S(2)}) collective-permute-start(bf16[32,1024]{1,0:T(8,128)(2,1)S(1)} %add_convert_fusion), channel_id=1, source_target_pairs={{4,0},{8,4},{12,8},{16,12},{20,16},{24,20},{28,24},{0,28},{5,1},{9... | collective-permute-start | bytes 196616 | tf_op jit(solution)/shard_map/ppermute | solution.py:14
Sparse Core Ops, SparseCore 0:
  43.0 19.9 reduce-scatter.4
  65.6 20.0 reduce-scatter.6
  88.2 19.9 reduce-scatter.8
  110.7 20.0 reduce-scatter.10
where the time goes:
time: 139 us
  waiting for transfers between devices  59.7 us (43%)
  blocking collectives  23.4 us (17%)
  starting transfers between devices  19.1 us (14%)
  matrix products  16.1 us (12%)
  between operations  13.9 us (10%)
  other arithmetic  6.33 us (5%)
    reduce_scatter x4, waiting for transfers between devices, on_device(): lax.psum_scatter(term_rows(grads, queries).astype(jnp.bfloat16), 'col', s...  59.6 us
    all_gather x4, blocking collectives, on_device(): gathered = lax.all_gather(visiting, 'col', axis=0, tiled=True)  23.4 us
    ppermute x6, starting transfers between devices, passed_along(): return lax.ppermute(block, axis, route)  19 us
    dot_general x4, matrix products, on_device(): jnp.dot(grads, kept_rows[cycle_step], preferred_element_type=jnp.float32)  8.65 us
    dot_general x4, matrix products, term_rows(): lax.dot_general(grads, queries, (((0,), (0,)), ((), ())), preferred_eleme...  5.87 us
  transfers between devices with their start and end apart: 10, of which 4 were waited for; matrix products, arithmetic and copies ran while one was open for 13% of the time, Pallas kernels for 0%

commit v1 on v0

v1 whole, which is shorter than its diff:
```python
import functools
import math

import jax
import jax.numpy as jnp
from jax import lax
from jax.experimental import pallas as pl
from jax.experimental.pallas import tpu as pltpu
from jax.sharding import PartitionSpec as P

very_negative = -1e30


def passed_along(block, distance):
    count = lax.axis_size("pb")
    return lax.ppermute(block, "pb", [(i, (i + distance) % count) for i in range(count)])


def swapped(block, bit):
    return lax.ppermute(block, "col", [(i, i ^ bit) for i in range(lax.axis_size("col"))])


def live_scores(values, mask_ref, row_tile, tile_cols):
    parts = []
    for col_tile in range(mask_ref.shape[1]):
        part = values[:, col_tile * tile_cols : (col_tile + 1) * tile_cols]
        parts.append(jnp.where(mask_ref[row_tile, col_tile] > 0, part, very_negative))
    return jnp.concatenate(parts, axis=1)


def softmax_rows(values):
    expon = jnp.exp(values - jnp.max(values, axis=1, keepdims=True))
    return expon * (1.0 / jnp.sum(expon, axis=1, keepdims=True))


def target_kernel(mask_ref, teacher_ref, target_ref):
    tiles, tile_count = mask_ref.shape
    tile_rows = teacher_ref.shape[0] // tiles
    tile_cols = teacher_ref.shape[1] // tile_count
    for tile in range(tiles):
        rows = slice(tile * tile_rows, (tile + 1) * tile_rows)
        taught = teacher_ref[rows, :].astype(jnp.float32)
        target_ref[rows, :] = softmax_rows(live_scores(taught, mask_ref, tile, tile_cols))


def load_window(pieces, window_ref, sems, order, own_rows, own_col):
    copies = []
    for number, (step, offset) in enumerate(order):
        count_cols = len(order) // (1 + max(s for s, _ in order))
        row = (step * count_cols + (own_col ^ offset)) * own_rows
        copies.append(
            pltpu.make_async_copy(
                pieces[number],
                window_ref.at[pl.ds(pl.multiple_of(row, own_rows), own_rows), :],
                sems.at[number],
            )
        )
    for copy in copies:
        copy.start()
    return copies


def grads_kernel(order, score_scale, mask_ref, queries_ref, target_ref, weights_ref, *refs):
    pieces = refs[: len(order)]
    grads_ref, send_ref, keep_ref, window_ref, sems = refs[len(order) :]
    own_rows = pieces[0].shape[0]
    own_col = lax.axis_index("col")
    copies = load_window(pieces, window_ref, sems, order, own_rows, own_col)
    tiles, tile_count = mask_ref.shape
    tile_rows = queries_ref.shape[0] // tiles
    tile_cols = window_ref.shape[0] // tile_count
    for copy in copies:
        copy.wait()
    for tile in range(tiles):
        rows = slice(tile * tile_rows, (tile + 1) * tile_rows)
        scores = score_scale * lax.dot_general(
            queries_ref[rows, :],
            window_ref[...],
            (((1,), (1,)), ((), ())),
            preferred_element_type=jnp.float32,
        )
        student = softmax_rows(live_scores(scores, mask_ref, tile, tile_cols))
        grads = (weights_ref[rows, :] * score_scale) * (student - target_ref[rows, :])
        grads_ref[rows, :] = grads.astype(jnp.bfloat16)
    steps, halves = send_ref.shape[:2]
    panel = 2 * halves * own_rows
    for step in range(steps):
        term = lax.dot_general(
            grads_ref[:, step * panel : (step + 1) * panel],
            queries_ref[...],
            (((0,), (0,)), ((), ())),
            preferred_element_type=jnp.float32,
        ).astype(jnp.bfloat16)
        for col in range(2 * halves):
            part = term[col * own_rows : (col + 1) * own_rows, :]
            offset = own_col ^ col

            @pl.when(offset % 2 == 1)
            def _():
                send_ref[step, offset // 2] = part

            @pl.when(offset % 2 == 0)
            def _():
                keep_ref[step, offset // 2] = part


def query_grad_kernel(order, grads_ref, *refs):
    pieces = refs[: len(order)]
    out_ref, window_ref, sems = refs[len(order) :]
    own_rows = pieces[0].shape[0]
    copies = load_window(pieces, window_ref, sems, order, own_rows, lax.axis_index("col"))
    for copy in copies:
        copy.wait()
    out_ref[...] = jnp.dot(grads_ref[...], window_ref[...], preferred_element_type=jnp.float32)


def on_device(queries, groups, teacher, tile_mask, weights):
    count_rows, width = queries.shape
    score_scale = 2.0 / math.sqrt(width)
    own_rows = groups.shape[0]
    count_cols = lax.axis_size("col")
    window = teacher.shape[1]
    steps = window // (own_rows * count_cols)
    bits = [1 << k for k in reversed(range(count_cols.bit_length() - 1))]
    vmem = pl.BlockSpec(memory_space=pltpu.VMEM)
    smem = pl.BlockSpec(memory_space=pltpu.SMEM)
    far = pl.BlockSpec(memory_space=pl.ANY)
    budget = 16 * 2**20 + 2 * window * width * 2 + 2 * count_rows * (window + width) * 4

    target = pl.pallas_call(
        target_kernel,
        out_shape=jax.ShapeDtypeStruct((count_rows, window), jnp.float32),
        in_specs=[smem, vmem],
        out_specs=vmem,
        compiler_params=pltpu.CompilerParams(vmem_limit_bytes=budget),
        cost_estimate=pl.CostEstimate(
            flops=8 * count_rows * window,
            bytes_accessed=6 * count_rows * window,
            transcendentals=count_rows * window,
        ),
    )(tile_mask, teacher)

    held = {}
    for step in reversed(range(steps)):
        held[(step, 0)] = groups if step == 0 else passed_along(groups, step)
    for bit in bits:
        for step, offset in list(held):
            held[(step, offset ^ bit)] = swapped(held[(step, offset)], bit)
    order = sorted(held)
    pieces = [held[key] for key in order]

    grads, send, keep = pl.pallas_call(
        functools.partial(grads_kernel, order, score_scale),
        out_shape=(
            jax.ShapeDtypeStruct((count_rows, window), jnp.bfloat16),
            jax.ShapeDtypeStruct((steps, count_cols // 2, own_rows, width), jnp.bfloat16),
            jax.ShapeDtypeStruct((steps, count_cols // 2, own_rows, width), jnp.bfloat16),
        ),
        in_specs=[smem, vmem, vmem, vmem] + [far] * len(pieces),
        out_specs=(vmem, vmem, vmem),
        scratch_shapes=[
            pltpu.VMEM((window, width), jnp.bfloat16),
            pltpu.SemaphoreType.DMA((len(pieces),)),
        ],
        compiler_params=pltpu.CompilerParams(vmem_limit_bytes=budget),
        cost_estimate=pl.CostEstimate(
            flops=4 * count_rows * window * width,
            bytes_accessed=2 * count_rows * width + 4 * window * width + 6 * count_rows * window,
            transcendentals=count_rows * window,
        ),
    )(tile_mask, queries, target, weights[:, None], *pieces)

    query_grad = pl.pallas_call(
        functools.partial(query_grad_kernel, order),
        out_shape=jax.ShapeDtypeStruct((count_rows, width), jnp.float32),
        in_specs=[vmem] + [far] * len(pieces),
        out_specs=vmem,
        scratch_shapes=[
            pltpu.VMEM((window, width), jnp.bfloat16),
            pltpu.SemaphoreType.DMA((len(pieces),)),
        ],
        compiler_params=pltpu.CompilerParams(vmem_limit_bytes=budget),
        cost_estimate=pl.CostEstimate(
            flops=2 * count_rows * window * width,
            bytes_accessed=4 * count_rows * width + 2 * window * width + 2 * count_rows * window,
            transcendentals=0,
        ),
    )(grads, *pieces)

    group_grad = None
    for step in reversed(range(steps)):
        total = keep[step].astype(jnp.float32) + swapped(send[step], 1).astype(jnp.float32)
        for bit in reversed(bits[:-1]):
            half = total.reshape(-1, 2, own_rows, width)
            total = half[:, 0].astype(jnp.float32) + swapped(
                half[:, 1].astype(jnp.bfloat16), bit
            ).astype(jnp.float32)
        total = total.reshape(own_rows, width)
        if step > 0:
            total = passed_along(total.astype(jnp.bfloat16), -step).astype(jnp.float32)
        group_grad = total if group_grad is None else group_grad + total
    return (query_grad, group_grad)


def solution(mesh):
    placed = (
        P(("pb", "col"), None),
        P(("pb", "col"), None),
        P(("pb", "col"), None),
        P(("pb", "col"), None),
        P(("pb", "col")),
    )
    return jax.shard_map(
        on_device,
        mesh=mesh,
        in_specs=placed,
        out_specs=(P(("pb", "col"), None), P(("pb", "col"), None)),
        check_vma=False,
    )
```

time: 139 us -> 45.7 us (0.33)
  waiting for transfers between devices: 59.7 us -> 8.32 us
  blocking collectives: 23.4 us -> 0 us
  matrix products: 16.1 us -> 0 us
  between operations: 13.9 us -> 0.81 us
  Pallas kernels: 0 us -> 9.38 us
  other arithmetic: 6.33 us -> 0.91 us
  local copies, waits for them, and re-layouts: 0.36 us -> 4.5 us
  starting transfers between devices: 19.1 us -> 21.5 us
    reduce_scatter x4 -> x0, waiting for transfers between devices: 59.6 us -> none  [on_device(): lax.psum_scatter(term_rows(grads, queries).astype(jnp.bfloat16), 'col', s...]
    all_gather x4 -> x0, blocking collectives: 23.4 us -> none  [on_device(): gathered = lax.all_gather(visiting, 'col', axis=0, tiled=True)]
    dot_general x12 -> x0, matrix products: 16.1 us -> none  [the longest x4 8.65 us: on_device(): jnp.dot(grads, kept_rows[cycle_step], preferred_element_type=jnp.float32)]
    pallas_call x0 -> x3, Pallas kernels: none -> 9.38 us  [the longest x1 5.17 us: on_device(): pl.pallas_call(functools.partial(grads_kernel, order, score_scale), out_s...]
    ppermute x6 -> x26, waiting for transfers between devices: 0.02 us -> 8.32 us  [the longest x20 5.7 us: swapped(): lax.ppermute(block, 'col', [(i, i ^ bit) for i in range(lax.axis_size('co...]
    unnamed x7 -> x8, local copies, waits for them, and re-layouts: 0.23 us -> 3.64 us
    convert_element_type x3, other arithmetic: 2.67 us -> 0.06 us  [on_device(): total = passed_along(total.astype(jnp.bfloat16), -step).astype(jnp.float32)]
    ppermute x6 -> x26, starting transfers between devices: 19 us -> 21.5 us  [the longest x20 11.1 us: swapped(): lax.ppermute(block, 'col', [(i, i ^ bit) for i in range(lax.axis_size('co...]
  transfers between devices with their start and end apart: 10 -> 26, of which waited for: 4 -> 9; matrix products, arithmetic and copies ran while one was open for 13% -> 2% of each run, Pallas kernels for 0% -> 9%
where the time goes in v1:
time: 45.7 us; the launch traced here: 45.4 us
  starting transfers between devices  21.5 us (47%)
  Pallas kernels  9.38 us (21%)
  waiting for transfers between devices  8.32 us (18%)
  local copies, waits for them, and re-layouts  4.5 us (10%)
  other arithmetic  0.91 us (2%)
  between operations  0.81 us (2%)
    ppermute x20, starting transfers between devices, swapped(): lax.ppermute(block, 'col', [(i, i ^ bit) for i in range(lax.axis_size('co...  11.1 us
    ppermute x6, starting transfers between devices, passed_along(): lax.ppermute(block, 'pb', [(i, (i + distance) % count) for i in range(cou...  10.4 us
    ppermute x20, waiting for transfers between devices, swapped(): lax.ppermute(block, 'col', [(i, i ^ bit) for i in range(lax.axis_size('co...  5.7 us
    pallas_call x1, Pallas kernels, on_device(): pl.pallas_call(functools.partial(grads_kernel, order, score_scale), out_s...  5.17 us
    unnamed x8, local copies, waits for them, and re-layouts  3.64 us
    pallas_call x1, Pallas kernels, on_device(): pl.pallas_call(functools.partial(query_grad_kernel, order), out_shape=jax...  3.37 us
    ppermute x6, waiting for transfers between devices, passed_along(): lax.ppermute(block, 'pb', [(i, (i + distance) % count) for i in range(cou...  2.62 us
  transfers between devices with their start and end apart: 26, of which 9 were waited for; matrix products, arithmetic and copies ran while one was open for 2% of the time, Pallas kernels for 9%

profile of v1, /device:TPU:0, one launch (start us, length us, event | category | flops | bytes accessed | tf_op | source)
XLA Modules:
  0.0 45.4 jit_solution(14411450390778428748)
XLA Ops:
  0.6 3.1 %collective-permute-start.7 = (bf16[32,1024]{1,0:T(8,128)(2,1)}, bf16[32,1024]{1,0:T(8,128)(2,1)S(1)}, u32[]{:S(2)}, u32[]{:S(2)}) collective-permute-start(bf16[32,1024]{1,0:T(8,128)(2,1)} %refs_0_.3), channel_id=1, source_target_pairs={{0,8},{4,12},{8,16},{12,20},{16,24},{20,28},{24,0},{28,4},{1,9},{5... | collective-permute-start | bytes 196616 | tf_op jit(solution)/shard_map/ppermute | solution.py:16
  3.7 2.5 %collective-permute-start.11 = (bf16[32,1024]{1,0:T(8,128)(2,1)}, bf16[32,1024]{1,0:T(8,128)(2,1)S(1)}, u32[]{:S(2)}, u32[]{:S(2)}) collective-permute-start(bf16[32,1024]{1,0:T(8,128)(2,1)} %refs_0_.3), channel_id=1, source_target_pairs={{0,12},{4,16},{8,20},{12,24},{16,28},{20,0},{24,4},{28,8},{1,13},{... | collective-permute-start | bytes 196616 | tf_op jit(solution)/shard_map/ppermute | solution.py:16
  6.2 1.5 %collective-permute-start.3 = (bf16[32,1024]{1,0:T(8,128)(2,1)}, bf16[32,1024]{1,0:T(8,128)(2,1)S(1)}, u32[]{:S(2)}, u32[]{:S(2)}) collective-permute-start(bf16[32,1024]{1,0:T(8,128)(2,1)} %refs_0_.3), channel_id=1, source_target_pairs={{0,4},{4,8},{8,12},{12,16},{16,20},{20,24},{24,28},{28,0},{1,5},{5... | collective-permute-start | bytes 196616 | tf_op jit(solution)/shard_map/ppermute | solution.py:16
  7.8 1.5 %collective-permute-start.1 = (bf16[32,1024]{1,0:T(8,128)(2,1)}, bf16[32,1024]{1,0:T(8,128)(2,1)S(1)}, u32[]{:S(2)}, u32[]{:S(2)}) collective-permute-start(bf16[32,1024]{1,0:T(8,128)(2,1)} %refs_0_.3), channel_id=1, source_target_pairs={{0,2},{1,3},{2,0},{3,1},{4,6},{5,7},{6,4},{7,5},{8,10},{9,11},{10,... | collective-permute-start | bytes 196616 | tf_op jit(solution)/shard_map/ppermute | solution.py:20
  9.9 2.6 %collective-permute-done.11.refs_12_ = bf16[32,1024]{1,0:T(8,128)(2,1)S(1)} collective-permute-done((bf16[32,1024]{1,0:T(8,128)(2,1)}, bf16[32,1024]{1,0:T(8,128)(2,1)S(1)}, u32[]{:S(2)}, u32[]{:S(2)}) %collective-permute-start.11) | collective-permute-done | bytes 65568 | tf_op jit(solution)/shard_map/ppermute | solution.py:16
  12.5 1.5 %collective-permute-start.13 = (bf16[32,1024]{1,0:T(8,128)(2,1)S(1)}, bf16[32,1024]{1,0:T(8,128)(2,1)S(1)}, u32[]{:S(2)}, u32[]{:S(2)}) collective-permute-start(bf16[32,1024]{1,0:T(8,128)(2,1)S(1)} %collective-permute-done.11.refs_12_), channel_id=1, source_target_pairs={{0,2},{1,3},{2,0},{3,1},{4,6},{5,7},{6,4},{7,5},{8,10},{9,11},{10,... | collective-permute-start | bytes 196616 | tf_op jit(solution)/shard_map/ppermute | solution.py:20
  14.0 0.9 %collective-permute-start.5 = (bf16[32,1024]{1,0:T(8,128)(2,1)S(1)}, bf16[32,1024]{1,0:T(8,128)(2,1)S(1)}, u32[]{:S(2)}, u32[]{:S(2)}) collective-permute-start(bf16[32,1024]{1,0:T(8,128)(2,1)S(1)} %collective-permute-done.3.refs_4_), channel_id=1, source_target_pairs={{0,2},{1,3},{2,0},{3,1},{4,6},{5,7},{6,4},{7,5},{8,10},{9,11},{10,... | collective-permute-start | bytes 196616 | tf_op jit(solution)/shard_map/ppermute | solution.py:20
  15.5 1.9 %collective-permute-done.13.refs_14_ = bf16[32,1024]{1,0:T(8,128)(2,1)S(1)} collective-permute-done((bf16[32,1024]{1,0:T(8,128)(2,1)S(1)}, bf16[32,1024]{1,0:T(8,128)(2,1)S(1)}, u32[]{:S(2)}, u32[]{:S(2)}) %collective-permute-start.13) | collective-permute-done | bytes 65568 | tf_op jit(solution)/shard_map/ppermute | solution.py:20
  17.4 0.8 %collective-permute-done.5.refs_6_ = bf16[32,1024]{1,0:T(8,128)(2,1)S(1)} collective-permute-done((bf16[32,1024]{1,0:T(8,128)(2,1)S(1)}, bf16[32,1024]{1,0:T(8,128)(2,1)S(1)}, u32[]{:S(2)}, u32[]{:S(2)}) %collective-permute-start.5) | collective-permute-done | bytes 65568 | tf_op jit(solution)/shard_map/ppermute | solution.py:20
  18.9 0.8 %broadcast_in_dim.4.weights_ref = f32[384,1]{1,0:T(8,128)S(1)} reshape(f32[384]{0:T(512)} %param.9) | data formatting | bytes 3072 | tf_op jit(solution)/shard_map/broadcast_in_dim | solution.py:171
  19.7 1.0 %copy-done = bf16[384,512]{1,0:T(8,128)(2,1)S(1)} copy-done((bf16[384,512]{1,0:T(8,128)(2,1)S(1)}, bf16[384,512]{1,0:T(8,128)(2,1)}, u32[]{:S(2)}) %copy-start) | copy-done | bytes 393240
  21.3 0.8 %shard_map.68.target_ref = f32[384,512]{1,0:T(8,128)S(1)} custom-call(s32[3,4]{1,0:T(4,128)S(1)} %copy-done.2, bf16[384,512]{1,0:T(8,128)(2,1)S(1)} %copy-done), custom_call_target="tpu_custom_call" | custom-call | flops 1572864 | bytes 1179648 | tf_op jit(solution)/shard_map/pallas_call | solution.py:130
  22.2 0.8 %copy-done.1 = bf16[32,1024]{1,0:T(8,128)(2,1)S(1)} copy-done((bf16[32,1024]{1,0:T(8,128)(2,1)S(1)}, bf16[32,1024]{1,0:T(8,128)(2,1)}, u32[]{:S(2)}) %copy-start.1) | copy-done | bytes 65560
  23.1 1.1 %copy-done.3 = bf16[384,1024]{1,0:T(8,128)(2,1)S(1)} copy-done((bf16[384,1024]{1,0:T(8,128)(2,1)S(1)}, bf16[384,1024]{1,0:T(8,128)(2,1)}, u32[]{:S(2)}) %copy-start.3) | copy-done | bytes 786456
  24.2 5.2 %shard_map.69 = (bf16[384,512]{1,0:T(8,128)(2,1)S(1)}, bf16[4,2,32,1024]{3,2,1,0:T(8,128)(2,1)S(1)}, bf16[4,2,32,1024]{3,2,1,0:T(8,128)(2,1)S(1)}) custom-call(s32[3,4]{1,0:T(4,128)S(1)} %copy-done.2, bf16[384,1024]{1,0:T(8,128)(2,1)S(1)} %copy-done.3, f32[384,512]{1,0:T(8,128)S(1)} %shard_map.68.target_ref, f32[384,1]{1,0:T(8,128)S(1)} %broadcast_in_dim.4.weights_ref, ...), custom_call_target="tpu_custom_call" | custom-call | flops 805306368 | bytes 4063232 | tf_op jit(solution)/shard_map/pallas_call | solution.py:152
  32.0 1.0 %collective-permute-start.16 = (bf16[1,32,1024]{2,1,0:T(8,128)(2,1)S(1)}, bf16[1,32,1024]{2,1,0:T(8,128)(2,1)S(1)}, u32[]{:S(2)}, u32[]{:S(2)}) collective-permute-start(bf16[1,32,1024]{2,1,0:T(8,128)(2,1)S(1)} %fusion.14), channel_id=1, source_target_pairs={{0,2},{1,3},{2,0},{3,1},{4,6},{5,7},{6,4},{7,5},{8,10},{9,11},{10,... | collective-permute-start | bytes 196616 | tf_op jit(solution)/shard_map/ppermute | solution.py:20
  32.9 1.2 %collective-permute-start.19 = (bf16[1,32,1024]{2,1,0:T(8,128)(2,1)S(1)}, bf16[1,32,1024]{2,1,0:T(8,128)(2,1)S(1)}, u32[]{:S(2)}, u32[]{:S(2)}) collective-permute-start(bf16[1,32,1024]{2,1,0:T(8,128)(2,1)S(1)} %fusion.16), channel_id=1, source_target_pairs={{0,2},{1,3},{2,0},{3,1},{4,6},{5,7},{6,4},{7,5},{8,10},{9,11},{10,... | collective-permute-start | bytes 196616 | tf_op jit(solution)/shard_map/ppermute | solution.py:20
  34.1 1.0 %collective-permute-start.22 = (bf16[1,32,1024]{2,1,0:T(8,128)(2,1)S(1)}, bf16[1,32,1024]{2,1,0:T(8,128)(2,1)S(1)}, u32[]{:S(2)}, u32[]{:S(2)}) collective-permute-start(bf16[1,32,1024]{2,1,0:T(8,128)(2,1)S(1)} %fusion.18), channel_id=1, source_target_pairs={{0,2},{1,3},{2,0},{3,1},{4,6},{5,7},{6,4},{7,5},{8,10},{9,11},{10,... | collective-permute-start | bytes 196616 | tf_op jit(solution)/shard_map/ppermute | solution.py:20
  35.1 1.2 %collective-permute-start.25 = (bf16[1,32,1024]{2,1,0:T(8,128)(2,1)S(1)}, bf16[1,32,1024]{2,1,0:T(8,128)(2,1)S(1)}, u32[]{:S(2)}, u32[]{:S(2)}) collective-permute-start(bf16[1,32,1024]{2,1,0:T(8,128)(2,1)S(1)} %fusion.19), channel_id=1, source_target_pairs={{0,2},{1,3},{2,0},{3,1},{4,6},{5,7},{6,4},{7,5},{8,10},{9,11},{10,... | collective-permute-start | bytes 196616 | tf_op jit(solution)/shard_map/ppermute | solution.py:20
  37.4 1.0 %collective-permute-done.19 = bf16[1,32,1024]{2,1,0:T(8,128)(2,1)S(1)} collective-permute-done((bf16[1,32,1024]{2,1,0:T(8,128)(2,1)S(1)}, bf16[1,32,1024]{2,1,0:T(8,128)(2,1)S(1)}, u32[]{:S(2)}, u32[]{:S(2)}) %collective-permute-start.19) | collective-permute-done | bytes 65568 | tf_op jit(solution)/shard_map/ppermute | solution.py:20
  38.4 2.0 %collective-permute-start.20 = (bf16[32,1024]{1,0:T(8,128)(2,1)S(1)}, bf16[32,1024]{1,0:T(8,128)(2,1)S(1)}, u32[]{:S(2)}, u32[]{:S(2)}) collective-permute-start(bf16[32,1024]{1,0:T(8,128)(2,1)S(1)} %fusion.15), channel_id=1, source_target_pairs={{0,24},{4,28},{8,0},{12,4},{16,8},{20,12},{24,16},{28,20},{1,25},{... | collective-permute-start | bytes 196616 | tf_op jit(solution)/shard_map/ppermute | solution.py:16
  40.4 0.9 %collective-permute-start.23 = (bf16[32,1024]{1,0:T(8,128)(2,1)S(1)}, bf16[32,1024]{1,0:T(8,128)(2,1)S(1)}, u32[]{:S(2)}, u32[]{:S(2)}) collective-permute-start(bf16[32,1024]{1,0:T(8,128)(2,1)S(1)} %fusion.17), channel_id=1, source_target_pairs={{0,28},{4,0},{8,4},{12,8},{16,12},{20,16},{24,20},{28,24},{1,29},{... | collective-permute-start | bytes 196616 | tf_op jit(solution)/shard_map/ppermute | solution.py:16
  41.3 3.4 %shard_map.70 = f32[384,1024]{1,0:T(8,128)} custom-call(bf16[384,512]{1,0:T(8,128)(2,1)S(1)} %get-tuple-element.5.grads_ref, bf16[32,1024]{1,0:T(8,128)(2,1)S(1)} %copy-done.1, bf16[32,1024]{1,0:T(8,128)(2,1)S(1)} %collective-permute-done.refs_1_, bf16[32,1024]{1,0:T(8,128)(2,1)S(1)} %collective-permute-done.1.refs_2_, ...), custom_call_target="tpu_custom_call" | custom-call | flops 402653184 | bytes 3014656 | tf_op jit(solution)/shard_map/pallas_call | solution.py:173
  44.7 0.7 %fusion.6 = f32[32,1024]{1,0:T(8,128)} fusion(f32[1,2,32,1024]{3,2,1,0:T(8,128)S(1)} %get-tuple-element.9, bf16[1,32,1024]{2,1,0:T(8,128)(2,1)S(1)} %collective-permute-done.25, bf16[32,1024]{1,0:T(8,128)(2,1)S(1)} %collective-permute-done.23, bf16[32,1024]{1,0:T(8,128)(2,1)S(1)} %collective-permute-done.20, bf16[32,1024]{1,0:T(8,128)(2,1)S(1)} %collective-permute-done.17), kind=kLoop, calls=%fused_computation.12 | loop fusion | flops 262144 | bytes 524288 | tf_op jit(solution)/shard_map/add | solution.py:201
  (50 shorter events, 6.2 us)
Async XLA Ops:
  0.6 8.6 %collective-permute-start.7 = (bf16[32,1024]{1,0:T(8,128)(2,1)}, bf16[32,1024]{1,0:T(8,128)(2,1)S(1)}, u32[]{:S(2)}, u32[]{:S(2)}) collective-permute-start(bf16[32,1024]{1,0:T(8,128)(2,1)} %refs_0_.3), channel_id=1, source_target_pairs={{0,8},{4,12},{8,16},{12,20},{16,24},{20,28},{24,0},{28,4},{1,9},{5... | collective-permute-start | bytes 196616 | tf_op jit(solution)/shard_map/ppermute | solution.py:16
  3.7 8.8 %collective-permute-start.11 = (bf16[32,1024]{1,0:T(8,128)(2,1)}, bf16[32,1024]{1,0:T(8,128)(2,1)S(1)}, u32[]{:S(2)}, u32[]{:S(2)}) collective-permute-start(bf16[32,1024]{1,0:T(8,128)(2,1)} %refs_0_.3), channel_id=1, source_target_pairs={{0,12},{4,16},{8,20},{12,24},{16,28},{20,0},{24,4},{28,8},{1,13},{... | collective-permute-start | bytes 196616 | tf_op jit(solution)/shard_map/ppermute | solution.py:16
  6.2 7.8 %collective-permute-start.3 = (bf16[32,1024]{1,0:T(8,128)(2,1)}, bf16[32,1024]{1,0:T(8,128)(2,1)S(1)}, u32[]{:S(2)}, u32[]{:S(2)}) collective-permute-start(bf16[32,1024]{1,0:T(8,128)(2,1)} %refs_0_.3), channel_id=1, source_target_pairs={{0,4},{4,8},{8,12},{12,16},{16,20},{20,24},{24,28},{28,0},{1,5},{5... | collective-permute-start | bytes 196616 | tf_op jit(solution)/shard_map/ppermute | solution.py:16
  7.8 7.1 %collective-permute-start.1 = (bf16[32,1024]{1,0:T(8,128)(2,1)}, bf16[32,1024]{1,0:T(8,128)(2,1)S(1)}, u32[]{:S(2)}, u32[]{:S(2)}) collective-permute-start(bf16[32,1024]{1,0:T(8,128)(2,1)} %refs_0_.3), channel_id=1, source_target_pairs={{0,2},{1,3},{2,0},{3,1},{4,6},{5,7},{6,4},{7,5},{8,10},{9,11},{10,... | collective-permute-start | bytes 196616 | tf_op jit(solution)/shard_map/ppermute | solution.py:20
  9.2 5.7 %collective-permute-start = (bf16[32,1024]{1,0:T(8,128)(2,1)}, bf16[32,1024]{1,0:T(8,128)(2,1)S(1)}, u32[]{:S(2)}, u32[]{:S(2)}) collective-permute-start(bf16[32,1024]{1,0:T(8,128)(2,1)} %refs_0_.3), channel_id=1, source_target_pairs={{0,1},{1,0},{2,3},{3,2},{4,5},{5,4},{6,7},{7,6},{8,9},{9,8},{10,11... | collective-permute-start | bytes 196616 | tf_op jit(solution)/shard_map/ppermute | solution.py:20
  9.3 6.2 %collective-permute-start.9 = (bf16[32,1024]{1,0:T(8,128)(2,1)S(1)}, bf16[32,1024]{1,0:T(8,128)(2,1)S(1)}, u32[]{:S(2)}, u32[]{:S(2)}) collective-permute-start(bf16[32,1024]{1,0:T(8,128)(2,1)S(1)} %collective-permute-done.7.refs_8_), channel_id=1, source_target_pairs={{0,2},{1,3},{2,0},{3,1},{4,6},{5,7},{6,4},{7,5},{8,10},{9,11},{10,... | collective-permute-start | bytes 196616 | tf_op jit(solution)/shard_map/ppermute | solution.py:20
  12.5 4.9 %collective-permute-start.13 = (bf16[32,1024]{1,0:T(8,128)(2,1)S(1)}, bf16[32,1024]{1,0:T(8,128)(2,1)S(1)}, u32[]{:S(2)}, u32[]{:S(2)}) collective-permute-start(bf16[32,1024]{1,0:T(8,128)(2,1)S(1)} %collective-permute-done.11.refs_12_), channel_id=1, source_target_pairs={{0,2},{1,3},{2,0},{3,1},{4,6},{5,7},{6,4},{7,5},{8,10},{9,11},{10,... | collective-permute-start | bytes 196616 | tf_op jit(solution)/shard_map/ppermute | solution.py:20
  14.0 4.3 %collective-permute-start.5 = (bf16[32,1024]{1,0:T(8,128)(2,1)S(1)}, bf16[32,1024]{1,0:T(8,128)(2,1)S(1)}, u32[]{:S(2)}, u32[]{:S(2)}) collective-permute-start(bf16[32,1024]{1,0:T(8,128)(2,1)S(1)} %collective-permute-done.3.refs_4_), channel_id=1, source_target_pairs={{0,2},{1,3},{2,0},{3,1},{4,6},{5,7},{6,4},{7,5},{8,10},{9,11},{10,... | collective-permute-start | bytes 196616 | tf_op jit(solution)/shard_map/ppermute | solution.py:20
  14.9 3.4 %collective-permute-start.12 = (bf16[32,1024]{1,0:T(8,128)(2,1)S(1)}, bf16[32,1024]{1,0:T(8,128)(2,1)S(1)}, u32[]{:S(2)}, u32[]{:S(2)}) collective-permute-start(bf16[32,1024]{1,0:T(8,128)(2,1)S(1)} %collective-permute-done.11.refs_12_), channel_id=1, source_target_pairs={{0,1},{1,0},{2,3},{3,2},{4,5},{5,4},{6,7},{7,6},{8,9},{9,8},{10,11... | collective-permute-start | bytes 196616 | tf_op jit(solution)/shard_map/ppermute | solution.py:20
  14.9 3.9 %collective-permute-start.4 = (bf16[32,1024]{1,0:T(8,128)(2,1)S(1)}, bf16[32,1024]{1,0:T(8,128)(2,1)S(1)}, u32[]{:S(2)}, u32[]{:S(2)}) collective-permute-start(bf16[32,1024]{1,0:T(8,128)(2,1)S(1)} %collective-permute-done.3.refs_4_), channel_id=1, source_target_pairs={{0,1},{1,0},{2,3},{3,2},{4,5},{5,4},{6,7},{7,6},{8,9},{9,8},{10,11... | collective-permute-start | bytes 196616 | tf_op jit(solution)/shard_map/ppermute | solution.py:20
  15.4 6.8 %collective-permute-start.8 = (bf16[32,1024]{1,0:T(8,128)(2,1)S(1)}, bf16[32,1024]{1,0:T(8,128)(2,1)S(1)}, u32[]{:S(2)}, u32[]{:S(2)}) collective-permute-start(bf16[32,1024]{1,0:T(8,128)(2,1)S(1)} %collective-permute-done.7.refs_8_), channel_id=1, source_target_pairs={{0,1},{1,0},{2,3},{3,2},{4,5},{5,4},{6,7},{7,6},{8,9},{9,8},{10,11... | collective-permute-start | bytes 196616 | tf_op jit(solution)/shard_map/ppermute | solution.py:20
  17.4 4.8 %collective-permute-start.2 = (bf16[32,1024]{1,0:T(8,128)(2,1)S(1)}, bf16[32,1024]{1,0:T(8,128)(2,1)S(1)}, u32[]{:S(2)}, u32[]{:S(2)}) collective-permute-start(bf16[32,1024]{1,0:T(8,128)(2,1)S(1)} %collective-permute-done.1.refs_2_), channel_id=1, source_target_pairs={{0,1},{1,0},{2,3},{3,2},{4,5},{5,4},{6,7},{7,6},{8,9},{9,8},{10,11... | collective-permute-start | bytes 196616 | tf_op jit(solution)/shard_map/ppermute | solution.py:20
  18.3 3.9 %collective-permute-start.10 = (bf16[32,1024]{1,0:T(8,128)(2,1)S(1)}, bf16[32,1024]{1,0:T(8,128)(2,1)S(1)}, u32[]{:S(2)}, u32[]{:S(2)}) collective-permute-start(bf16[32,1024]{1,0:T(8,128)(2,1)S(1)} %collective-permute-done.9.refs_10_), channel_id=1, source_target_pairs={{0,1},{1,0},{2,3},{3,2},{4,5},{5,4},{6,7},{7,6},{8,9},{9,8},{10,11... | collective-permute-start | bytes 196616 | tf_op jit(solution)/shard_map/ppermute | solution.py:20
  18.3 3.9 %collective-permute-start.14 = (bf16[32,1024]{1,0:T(8,128)(2,1)S(1)}, bf16[32,1024]{1,0:T(8,128)(2,1)S(1)}, u32[]{:S(2)}, u32[]{:S(2)}) collective-permute-start(bf16[32,1024]{1,0:T(8,128)(2,1)S(1)} %collective-permute-done.13.refs_14_), channel_id=1, source_target_pairs={{0,1},{1,0},{2,3},{3,2},{4,5},{5,4},{6,7},{7,6},{8,9},{9,8},{10,11... | collective-permute-start | bytes 196616 | tf_op jit(solution)/shard_map/ppermute | solution.py:20
  18.8 3.4 %collective-permute-start.6 = (bf16[32,1024]{1,0:T(8,128)(2,1)S(1)}, bf16[32,1024]{1,0:T(8,128)(2,1)S(1)}, u32[]{:S(2)}, u32[]{:S(2)}) collective-permute-start(bf16[32,1024]{1,0:T(8,128)(2,1)S(1)} %collective-permute-done.5.refs_6_), channel_id=1, source_target_pairs={{0,1},{1,0},{2,3},{3,2},{4,5},{5,4},{6,7},{7,6},{8,9},{9,8},{10,11... | collective-permute-start | bytes 196616 | tf_op jit(solution)/shard_map/ppermute | solution.py:20
  29.4 1.5 %collective-permute-start.15 = (bf16[2,32,1024]{2,1,0:T(8,128)(2,1)S(1)}, bf16[2,32,1024]{2,1,0:T(8,128)(2,1)S(1)}, u32[]{:S(2)}, u32[]{:S(2)}) collective-permute-start(bf16[2,32,1024]{2,1,0:T(8,128)(2,1)S(1)} %get-tuple-element.12), channel_id=1, source_target_pairs={{0,1},{1,0},{2,3},{3,2},{4,5},{5,4},{6,7},{7,6},{8,9},{9,8},{10,11... | collective-permute-start | bytes 393224 | tf_op jit(solution)/shard_map/ppermute | solution.py:20
  30.0 1.4 %collective-permute-start.21 = (bf16[2,32,1024]{2,1,0:T(8,128)(2,1)S(1)}, bf16[2,32,1024]{2,1,0:T(8,128)(2,1)S(1)}, u32[]{:S(2)}, u32[]{:S(2)}) collective-permute-start(bf16[2,32,1024]{2,1,0:T(8,128)(2,1)S(1)} %get-tuple-element.14), channel_id=1, source_target_pairs={{0,1},{1,0},{2,3},{3,2},{4,5},{5,4},{6,7},{7,6},{8,9},{9,8},{10,11... | collective-permute-start | bytes 393224 | tf_op jit(solution)/shard_map/ppermute | solution.py:20
  32.0 5.0 %collective-permute-start.16 = (bf16[1,32,1024]{2,1,0:T(8,128)(2,1)S(1)}, bf16[1,32,1024]{2,1,0:T(8,128)(2,1)S(1)}, u32[]{:S(2)}, u32[]{:S(2)}) collective-permute-start(bf16[1,32,1024]{2,1,0:T(8,128)(2,1)S(1)} %fusion.14), channel_id=1, source_target_pairs={{0,2},{1,3},{2,0},{3,1},{4,6},{5,7},{6,4},{7,5},{8,10},{9,11},{10,... | collective-permute-start | bytes 196616 | tf_op jit(solution)/shard_map/ppermute | solution.py:20
  32.9 5.4 %collective-permute-start.19 = (bf16[1,32,1024]{2,1,0:T(8,128)(2,1)S(1)}, bf16[1,32,1024]{2,1,0:T(8,128)(2,1)S(1)}, u32[]{:S(2)}, u32[]{:S(2)}) collective-permute-start(bf16[1,32,1024]{2,1,0:T(8,128)(2,1)S(1)} %fusion.16), channel_id=1, source_target_pairs={{0,2},{1,3},{2,0},{3,1},{4,6},{5,7},{6,4},{7,5},{8,10},{9,11},{10,... | collective-permute-start | bytes 196616 | tf_op jit(solution)/shard_map/ppermute | solution.py:20
  34.1 6.2 %collective-permute-start.22 = (bf16[1,32,1024]{2,1,0:T(8,128)(2,1)S(1)}, bf16[1,32,1024]{2,1,0:T(8,128)(2,1)S(1)}, u32[]{:S(2)}, u32[]{:S(2)}) collective-permute-start(bf16[1,32,1024]{2,1,0:T(8,128)(2,1)S(1)} %fusion.18), channel_id=1, source_target_pairs={{0,2},{1,3},{2,0},{3,1},{4,6},{5,7},{6,4},{7,5},{8,10},{9,11},{10,... | collective-permute-start | bytes 196616 | tf_op jit(solution)/shard_map/ppermute | solution.py:20
  35.1 9.6 %collective-permute-start.25 = (bf16[1,32,1024]{2,1,0:T(8,128)(2,1)S(1)}, bf16[1,32,1024]{2,1,0:T(8,128)(2,1)S(1)}, u32[]{:S(2)}, u32[]{:S(2)}) collective-permute-start(bf16[1,32,1024]{2,1,0:T(8,128)(2,1)S(1)} %fusion.19), channel_id=1, source_target_pairs={{0,2},{1,3},{2,0},{3,1},{4,6},{5,7},{6,4},{7,5},{8,10},{9,11},{10,... | collective-permute-start | bytes 196616 | tf_op jit(solution)/shard_map/ppermute | solution.py:20
  37.0 7.7 %collective-permute-start.17 = (bf16[32,1024]{1,0:T(8,128)(2,1)S(1)}, bf16[32,1024]{1,0:T(8,128)(2,1)S(1)}, u32[]{:S(2)}, u32[]{:S(2)}) collective-permute-start(bf16[32,1024]{1,0:T(8,128)(2,1)S(1)} %fusion.13), channel_id=1, source_target_pairs={{0,20},{4,24},{8,28},{12,0},{16,4},{20,8},{24,12},{28,16},{1,21},{... | collective-permute-start | bytes 196616 | tf_op jit(solution)/shard_map/ppermute | solution.py:16
  38.4 6.3 %collective-permute-start.20 = (bf16[32,1024]{1,0:T(8,128)(2,1)S(1)}, bf16[32,1024]{1,0:T(8,128)(2,1)S(1)}, u32[]{:S(2)}, u32[]{:S(2)}) collective-permute-start(bf16[32,1024]{1,0:T(8,128)(2,1)S(1)} %fusion.15), channel_id=1, source_target_pairs={{0,24},{4,28},{8,0},{12,4},{16,8},{20,12},{24,16},{28,20},{1,25},{... | collective-permute-start | bytes 196616 | tf_op jit(solution)/shard_map/ppermute | solution.py:16
  40.4 4.3 %collective-permute-start.23 = (bf16[32,1024]{1,0:T(8,128)(2,1)S(1)}, bf16[32,1024]{1,0:T(8,128)(2,1)S(1)}, u32[]{:S(2)}, u32[]{:S(2)}) collective-permute-start(bf16[32,1024]{1,0:T(8,128)(2,1)S(1)} %fusion.17), channel_id=1, source_target_pairs={{0,28},{4,0},{8,4},{12,8},{16,12},{20,16},{24,20},{28,24},{1,29},{... | collective-permute-start | bytes 196616 | tf_op jit(solution)/shard_map/ppermute | solution.py:16
  (6 other events, 6.4 us)

commit v2 on v0

v2 whole, which is shorter than its diff:
```python
import functools
import math

import jax
import jax.numpy as jnp
from jax import lax
from jax.experimental import pallas as pl
from jax.experimental.pallas import tpu as pltpu
from jax.sharding import PartitionSpec as P

very_negative = -1e30


def moved_to(block, target):
    count_cols = lax.axis_size("col")
    pairs = []
    for p in range(lax.axis_size("pb")):
        for c in range(count_cols):
            q, d = target(p, c)
            pairs.append((p * count_cols + c, q * count_cols + d))
    return lax.ppermute(block, ("pb", "col"), pairs)


def swapped(block, bits):
    return moved_to(block, lambda p, c: (p, c ^ bits))


def softmax_cols(blocks):
    top = functools.reduce(jnp.maximum, [jnp.max(block, axis=0, keepdims=True) for block in blocks])
    blocks = [jnp.exp(block - top) for block in blocks]
    total = functools.reduce(jnp.add, [jnp.sum(block, axis=0, keepdims=True) for block in blocks])
    scale = 1.0 / total
    return [block * scale for block in blocks]


def piece_col(number, slot_steps, count_cols, own_rows):
    slot, offset = divmod(number, count_cols)
    own_step = slot_steps(lax.axis_index("pb"))[slot]
    own_col = lax.axis_index("col")
    return pl.multiple_of((own_step * count_cols + (own_col ^ offset)) * own_rows, own_rows)


def target_kernel(
    slot_steps, count_cols, score_scale, own_rows, mask_ref, weights_ref, teacher_ref, queries_ref,
    target_ref, live_ref, factor_ref, flat_ref,
):
    del queries_ref
    window, count_rows = target_ref.shape
    tiles, tile_count = mask_ref.shape
    tile_rows, tile_cols = count_rows // tiles, window // tile_count
    factor_ref[...] = weights_ref[...] * score_scale
    for tile in range(tiles):
        rows = slice(tile * tile_rows, (tile + 1) * tile_rows)
        taught = teacher_ref[rows, :].astype(jnp.float32).T
        blocks = []
        for col in range(tile_count):
            part = taught[col * tile_cols : (col + 1) * tile_cols, :]
            blocks.append(jnp.where(mask_ref[tile, col] > 0, part, very_negative))
        for col, block in enumerate(softmax_cols(blocks)):
            flat_ref[col * tile_cols : (col + 1) * tile_cols, rows] = block
    for number in range(window // own_rows):
        col = piece_col(number, slot_steps, count_cols, own_rows)
        target_ref[number * own_rows : (number + 1) * own_rows, :] = flat_ref[pl.ds(col, own_rows), :]
        for tile in range(tiles):
            live = mask_ref[tile, col // tile_cols].astype(jnp.float32)
            live_ref[number : number + 1, tile * tile_rows : (tile + 1) * tile_rows] = jnp.full(
                (1, tile_rows), live, jnp.float32
            )


def grads_kernel(score_scale, queries_ref, target_ref, live_ref, factor_ref, *refs):
    grads_ref, window_ref, send_ref, keep_ref, scores_ref = refs[-5:]
    pieces = refs[:-5]
    halves, own_rows = pieces[0].shape[:2]
    count_rows = grads_ref.shape[1]
    lanes = 128 if count_rows % 128 == 0 else count_rows
    for number in range(len(pieces) * halves):
        slot, offset = divmod(number, 2 * halves)
        window_ref[number * own_rows : (number + 1) * own_rows, :] = pieces[2 * slot + offset % 2][offset // 2]
    scores_ref[...] = score_scale * lax.dot_general(
        window_ref[...],
        queries_ref[...],
        (((1,), (1,)), ((), ())),
        preferred_element_type=jnp.float32,
    )
    for first in range(0, count_rows, lanes):
        rows = slice(first, first + lanes)
        blocks = []
        for number in range(len(pieces) * halves):
            part = scores_ref[number * own_rows : (number + 1) * own_rows, rows]
            blocks.append(jnp.where(live_ref[number : number + 1, rows] > 0, part, very_negative))
        factor = factor_ref[:, rows]
        for number, student in enumerate(softmax_cols(blocks)):
            cols = slice(number * own_rows, (number + 1) * own_rows)
            grads_ref[cols, rows] = (factor * (student - target_ref[cols, rows])).astype(jnp.bfloat16)
    slots = send_ref.shape[0]
    panel = 2 * halves * own_rows
    for slot in reversed(range(slots)):
        term = jnp.dot(
            grads_ref[slot * panel : (slot + 1) * panel, :],
            queries_ref[...],
            preferred_element_type=jnp.float32,
        ).astype(jnp.bfloat16)
        for half in range(halves):
            keep_ref[slot, half] = term[2 * half * own_rows : (2 * half + 1) * own_rows, :]
            send_ref[slot, half] = term[(2 * half + 1) * own_rows : (2 * half + 2) * own_rows, :]


def query_grad_kernel(grads_ref, window_ref, out_ref, part_ref, sems):
    count_rows = out_ref.shape[0]
    rows = part_ref.shape[1]
    copies = []
    for tile in range(count_rows // rows):
        part_ref[tile] = lax.dot_general(
            grads_ref[:, tile * rows : (tile + 1) * rows],
            window_ref[...],
            (((0,), (0,)), ((), ())),
            preferred_element_type=jnp.float32,
        )
        copy = pltpu.make_async_copy(
            part_ref.at[tile], out_ref.at[tile * rows : (tile + 1) * rows, :], sems.at[tile]
        )
        copy.start()
        copies.append(copy)
    for copy in copies:
        copy.wait()


def on_device(queries, groups, teacher, tile_mask, weights):
    count_rows, width = queries.shape
    score_scale = 2.0 / math.sqrt(width)
    own_rows = groups.shape[0]
    count_pb, count_cols = lax.axis_size("pb"), lax.axis_size("col")
    window = teacher.shape[1]
    steps = window // (own_rows * count_cols)
    tiles = tile_mask.shape[0]
    evens = range(0, count_cols, 2)
    vmem = pl.BlockSpec(memory_space=pltpu.VMEM)
    smem = pl.BlockSpec(memory_space=pltpu.SMEM)
    far = pl.BlockSpec(memory_space=pltpu.HBM)
    budget = 8 * 2**20 + 6 * window * width * 2 + 2 * count_rows * (window + width) * 4
    params = pltpu.CompilerParams(vmem_limit_bytes=min(budget, 50 * 2**20))

    def slot_steps(p):
        return (0, 2, 3 - 2 * (p % 2), 1 + 2 * (p % 2))

    def own(offset):
        return lambda p, c: (p, c ^ offset)

    def ahead(offset):
        return lambda p, c: ((p + 2) % count_pb, c ^ offset)

    def across(offset):
        return lambda p, c: ((p + 1 + 2 * (p % 2)) % count_pb, c ^ offset)

    def beside(p, c):
        return (p ^ 1, c)

    def reverse(move):
        back = {move(p, c): (p, c) for p in range(count_pb) for c in range(count_cols)}
        return lambda p, c: back[(p, c)]

    def joined(parts):
        return jnp.stack(parts)

    second = joined([moved_to(groups, ahead(offset)) for offset in evens])
    thirds = [moved_to(groups, across(offset)) for offset in evens]
    firsts = [groups] + [moved_to(groups, own(offset)) for offset in evens[1:]]
    fourth = moved_to(second, beside)

    teacher, queries, _ = lax.optimization_barrier((teacher, queries, second))
    target, live, factor = pl.pallas_call(
        functools.partial(target_kernel, slot_steps, count_cols, score_scale, own_rows),
        out_shape=(
            jax.ShapeDtypeStruct((window, count_rows), jnp.float32),
            jax.ShapeDtypeStruct((window // own_rows, count_rows), jnp.float32),
            jax.ShapeDtypeStruct((1, count_rows), jnp.float32),
        ),
        in_specs=[smem, vmem, vmem, vmem],
        out_specs=(vmem,) * 3,
        scratch_shapes=[pltpu.VMEM((window, count_rows), jnp.float32)],
        compiler_params=params,
        cost_estimate=pl.CostEstimate(
            flops=8 * count_rows * window,
            bytes_accessed=6 * count_rows * (window + width),
            transcendentals=count_rows * window,
        ),
    )(tile_mask, weights[None, :], teacher, queries)
    thirds, target = lax.optimization_barrier((thirds, target))
    firsts, target = lax.optimization_barrier((firsts, target))
    fourth, target = lax.optimization_barrier((fourth, target))
    first, third = joined(firsts), joined(thirds)
    held = [first, second, third, fourth]
    pieces = []
    for block in held:
        pieces += [block, moved_to(block, own(1))]

    grads, gathered, send, keep = pl.pallas_call(
        functools.partial(grads_kernel, score_scale),
        out_shape=(
            jax.ShapeDtypeStruct((window, count_rows), jnp.bfloat16),
            jax.ShapeDtypeStruct((window, width), jnp.bfloat16),
            jax.ShapeDtypeStruct((steps, count_cols // 2, own_rows, width), jnp.bfloat16),
            jax.ShapeDtypeStruct((steps, count_cols // 2, own_rows, width), jnp.bfloat16),
        ),
        in_specs=[vmem] * (4 + len(pieces)),
        out_specs=(vmem,) * 4,
        scratch_shapes=[pltpu.VMEM((window, count_rows), jnp.float32)],
        compiler_params=params,
        cost_estimate=pl.CostEstimate(
            flops=4 * count_rows * window * width,
            bytes_accessed=2 * count_rows * width + 4 * window * width + 6 * count_rows * window,
            transcendentals=count_rows * window,
        ),
    )(queries, target, live, factor, *pieces)

    rows = count_rows // tiles
    query_grad = pl.pallas_call(
        query_grad_kernel,
        out_shape=jax.ShapeDtypeStruct((count_rows, width), jnp.float32),
        in_specs=[vmem, vmem],
        out_specs=far,
        scratch_shapes=[
            pltpu.VMEM((tiles, rows, width), jnp.float32),
            pltpu.SemaphoreType.DMA((tiles,)),
        ],
        compiler_params=params,
        cost_estimate=pl.CostEstimate(
            flops=2 * count_rows * window * width,
            bytes_accessed=4 * count_rows * width + 2 * window * width + 2 * count_rows * window,
            transcendentals=0,
        ),
    )(grads, gathered)

    sums = []
    for slot in range(steps):
        other = swapped(send[slot], 1)
        sums.append(keep[slot].astype(jnp.float32) + other.astype(jnp.float32))

    def arrived(block, move):
        return moved_to(block.astype(jnp.bfloat16), move).astype(jnp.float32)

    sums[1] = sums[1] + arrived(sums[3], beside)
    moves = ((2, across), (1, ahead), (0, own))
    group_grad = sums[0][0]
    for slot, move in moves:
        for offset in evens:
            if slot > 0 or offset > 0:
                group_grad = group_grad + arrived(sums[slot][offset // 2], reverse(move(offset)))
    return (query_grad, group_grad)


def solution(mesh):
    placed = (
        P(("pb", "col"), None),
        P(("pb", "col"), None),
        P(("pb", "col"), None),
        P(("pb", "col"), None),
        P(("pb", "col")),
    )
    return jax.shard_map(
        on_device,
        mesh=mesh,
        in_specs=placed,
        out_specs=(P(("pb", "col"), None), P(("pb", "col"), None)),
        check_vma=False,
    )
```

time: 139 us -> 41.1 us (0.30)
  waiting for transfers between devices: 59.7 us -> 6.46 us
  blocking collectives: 23.4 us -> 0 us
  matrix products: 16.1 us -> 0 us
  between operations: 13.9 us -> 0.78 us
  starting transfers between devices: 19.1 us -> 23.9 us
  other arithmetic: 6.33 us -> 1.77 us
  Pallas kernels: 0 us -> 4.27 us
  local copies, waits for them, and re-layouts: 0.36 us -> 3.56 us
    reduce_scatter x4 -> x0, waiting for transfers between devices: 59.6 us -> none  [on_device(): lax.psum_scatter(term_rows(grads, queries).astype(jnp.bfloat16), 'col', s...]
    all_gather x4 -> x0, blocking collectives: 23.4 us -> none  [on_device(): gathered = lax.all_gather(visiting, 'col', axis=0, tiled=True)]
    dot_general x12 -> x0, matrix products: 16.1 us -> none  [the longest x4 8.65 us: on_device(): jnp.dot(grads, kept_rows[cycle_step], preferred_element_type=jnp.float32)]
    ppermute x6 -> x20, waiting for transfers between devices: 0.02 us -> 6.46 us  [moved_to(): return lax.ppermute(block, ('pb', 'col'), pairs)]
    ppermute x6 -> x20, starting transfers between devices: 19 us -> 23.9 us  [moved_to(): return lax.ppermute(block, ('pb', 'col'), pairs)]
    pallas_call x0 -> x3, Pallas kernels: none -> 4.27 us  [the longest x1 1.76 us: on_device(): pl.pallas_call(functools.partial(grads_kernel, score_scale), out_shape=(j...]
    convert_element_type x3 -> x0, other arithmetic: 2.67 us -> none  [the longest x2 1.72 us: on_device(): group_grad.astype(jnp.bfloat16)]
    unnamed x7 -> x8, local copies, waits for them, and re-layouts: 0.23 us -> 2.81 us
  transfers between devices with their start and end apart: 10 -> 20, of which waited for: 4 -> 10; matrix products, arithmetic and copies ran while one was open for 13% -> 4% of each run, Pallas kernels for 0% -> 6%
where the time goes in v2:
time: 41.1 us; the launch traced here: 40.8 us
  starting transfers between devices  23.9 us (58%)
  waiting for transfers between devices  6.46 us (16%)
  Pallas kernels  4.27 us (10%)
  local copies, waits for them, and re-layouts  3.56 us (9%)
  other arithmetic  1.77 us (4%)
  between operations  0.78 us (2%)
    ppermute x20, starting transfers between devices, moved_to(): return lax.ppermute(block, ('pb', 'col'), pairs)  23.9 us
    ppermute x20, waiting for transfers between devices, moved_to(): return lax.ppermute(block, ('pb', 'col'), pairs)  6.46 us
    unnamed x8, local copies, waits for them, and re-layouts  2.81 us
    pallas_call x1, Pallas kernels, on_device(): pl.pallas_call(functools.partial(grads_kernel, score_scale), out_shape=(j...  1.76 us
    pallas_call x1, Pallas kernels, on_device(): pl.pallas_call(query_grad_kernel, out_shape=jax.ShapeDtypeStruct((count_r...  1.5 us
    pallas_call x1, Pallas kernels, on_device(): pl.pallas_call(functools.partial(target_kernel, slot_steps, count_cols, s...  1.01 us
    another operation x3, other arithmetic, joined(): return jnp.stack(parts)  0.88 us
  transfers between devices with their start and end apart: 20, of which 10 were waited for; matrix products, arithmetic and copies ran while one was open for 4% of the time, Pallas kernels for 6%

profile of v2, /device:TPU:0, one launch (start us, length us, event | category | flops | bytes accessed | tf_op | source)
XLA Modules:
  0.0 40.8 jit_solution(14183334916114059879)
XLA Ops:
  0.6 4.0 %collective-permute-start.1 = (bf16[32,1024]{1,0:T(8,128)(2,1)}, bf16[32,1024]{1,0:T(8,128)(2,1)S(1)}, u32[]{:S(2)}, u32[]{:S(2)}) collective-permute-start(bf16[32,1024]{1,0:T(8,128)(2,1)} %param.6), channel_id=1, source_target_pairs={{0,10},{1,11},{2,8},{3,9},{4,14},{5,15},{6,12},{7,13},{8,18},{9,19... | collective-permute-start | bytes 196616 | tf_op jit(solution)/shard_map/ppermute | solution.py:21
  4.6 1.6 %collective-permute-start = (bf16[32,1024]{1,0:T(8,128)(2,1)}, bf16[32,1024]{1,0:T(8,128)(2,1)S(1)}, u32[]{:S(2)}, u32[]{:S(2)}) collective-permute-start(bf16[32,1024]{1,0:T(8,128)(2,1)} %param.6), channel_id=1, source_target_pairs={{0,8},{1,9},{2,10},{3,11},{4,12},{5,13},{6,14},{7,15},{8,16},{9,17... | collective-permute-start | bytes 196616 | tf_op jit(solution)/shard_map/ppermute | solution.py:21
  6.2 1.5 %collective-permute-start.4 = (bf16[32,1024]{1,0:T(8,128)(2,1)}, bf16[32,1024]{1,0:T(8,128)(2,1)S(1)}, u32[]{:S(2)}, u32[]{:S(2)}) collective-permute-start(bf16[32,1024]{1,0:T(8,128)(2,1)} %param.6), channel_id=1, source_target_pairs={{0,4},{1,5},{2,6},{3,7},{4,16},{5,17},{6,18},{7,19},{8,12},{9,13},... | collective-permute-start | bytes 196616 | tf_op jit(solution)/shard_map/ppermute | solution.py:21
  7.7 0.5 %collective-permute-start.3 = (bf16[32,1024]{1,0:T(8,128)(2,1)}, bf16[32,1024]{1,0:T(8,128)(2,1)S(1)}, u32[]{:S(2)}, u32[]{:S(2)}) collective-permute-start(bf16[32,1024]{1,0:T(8,128)(2,1)} %param.6), channel_id=1, source_target_pairs={{0,2},{1,3},{2,0},{3,1},{4,6},{5,7},{6,4},{7,5},{8,10},{9,11},{10,... | collective-permute-start | bytes 196616 | tf_op jit(solution)/shard_map/ppermute | solution.py:21
  8.3 2.1 %collective-permute-start.5 = (bf16[32,1024]{1,0:T(8,128)(2,1)}, bf16[32,1024]{1,0:T(8,128)(2,1)S(1)}, u32[]{:S(2)}, u32[]{:S(2)}) collective-permute-start(bf16[32,1024]{1,0:T(8,128)(2,1)} %param.6), channel_id=1, source_target_pairs={{0,6},{1,7},{2,4},{3,5},{4,18},{5,19},{6,16},{7,17},{8,14},{9,15},... | collective-permute-start | bytes 196616 | tf_op jit(solution)/shard_map/ppermute | solution.py:21
  10.4 0.7 %broadcast_in_dim.3.weights_ref = f32[1,384]{1,0:T(1,128)S(1)} reshape(f32[384]{0:T(512)} %param.9) | data formatting | bytes 3072 | tf_op jit(solution)/shard_map/broadcast_in_dim | solution.py:188
  11.2 2.1 %collective-permute-start.2 = (bf16[2,32,1024]{2,1,0:T(8,128)(2,1)S(1)}, bf16[2,32,1024]{2,1,0:T(8,128)(2,1)S(1)}, u32[]{:S(2)}, u32[]{:S(2)}) collective-permute-start(bf16[2,32,1024]{2,1,0:T(8,128)(2,1)S(1)} %pad_maximum_fusion.refs_2_), channel_id=1, source_target_pairs={{0,4},{1,5},{2,6},{3,7},{4,0},{5,1},{6,2},{7,3},{8,12},{9,13},{10,... | collective-permute-start | bytes 393224 | tf_op jit(solution)/shard_map/ppermute | solution.py:21
  13.2 1.1 %copy-done = bf16[384,1024]{1,0:T(8,128)(2,1)S(1)} copy-done((bf16[384,1024]{1,0:T(8,128)(2,1)S(1)}, bf16[384,1024]{1,0:T(8,128)(2,1)}, u32[]{:S(2)}) %copy-start) | copy-done | bytes 786456
  14.4 1.0 %copy-done.2 = bf16[384,512]{1,0:T(8,128)(2,1)S(1)} copy-done((bf16[384,512]{1,0:T(8,128)(2,1)S(1)}, bf16[384,512]{1,0:T(8,128)(2,1)}, u32[]{:S(2)}) %copy-start.2) | copy-done | bytes 393240
  15.4 0.7 %copy-done.3 = s32[3,4]{1,0:T(4,128)S(1)} copy-done((s32[3,4]{1,0:T(4,128)S(1)}, s32[3,4]{1,0:T(4,128)}, u32[]{:S(2)}) %copy-start.3) | copy-done | bytes 72
  16.0 1.0 %shard_map.68 = (f32[512,384]{1,0:T(8,128)S(1)}, f32[16,384]{1,0:T(8,128)S(1)}, f32[1,384]{1,0:T(1,128)S(1)}) custom-call(s32[3,4]{1,0:T(4,128)S(1)} %copy-done.3, f32[1,384]{1,0:T(1,128)S(1)} %broadcast_in_dim.3.weights_ref, bf16[384,512]{1,0:T(8,128)(2,1)S(1)} %copy-done.2, bf16[384,1024]{1,0:T(8,128)(2,1)S(1)} %copy-done), custom_call_target="tpu_custom_call" | custom-call | flops 1572864 | bytes 3538944 | tf_op jit(solution)/shard_map/pallas_call | solution.py:172
  17.4 0.9 %pad_maximum_fusion.1.refs_0_ = bf16[2,32,1024]{2,1,0:T(8,128)(2,1)S(1)} fusion(bf16[1,32,1024]{2,1,0:T(8,128)(2,1)S(1)} %bitcast.51, bf16[1,32,1024]{2,1,0:T(8,128)(2,1)} %bitcast.48), kind=kLoop, calls=%fused_computation.16 | loop fusion | flops 65536 | bytes 262144 | tf_op jit(solution)/shard_map/stack | solution.py:164
  18.3 0.6 %collective-permute-start.8 = (bf16[2,32,1024]{2,1,0:T(8,128)(2,1)S(1)}, bf16[2,32,1024]{2,1,0:T(8,128)(2,1)S(1)}, u32[]{:S(2)}, u32[]{:S(2)}) collective-permute-start(bf16[2,32,1024]{2,1,0:T(8,128)(2,1)S(1)} %pad_maximum_fusion.2.refs_4_), channel_id=1, source_target_pairs={{0,1},{1,0},{2,3},{3,2},{4,5},{5,4},{6,7},{7,6},{8,9},{9,8},{10,11... | collective-permute-start | bytes 393224 | tf_op jit(solution)/shard_map/ppermute | solution.py:21
  19.9 0.9 %collective-permute-done.9.refs_7_ = bf16[2,32,1024]{2,1,0:T(8,128)(2,1)S(1)} collective-permute-done((bf16[2,32,1024]{2,1,0:T(8,128)(2,1)S(1)}, bf16[2,32,1024]{2,1,0:T(8,128)(2,1)S(1)}, u32[]{:S(2)}, u32[]{:S(2)}) %collective-permute-start.9) | collective-permute-done | bytes 131104 | tf_op jit(solution)/shard_map/ppermute | solution.py:21
  20.8 1.8 %shard_map.69 = (bf16[512,384]{1,0:T(8,128)(2,1)S(1)}, bf16[512,1024]{1,0:T(8,128)(2,1)S(1)}, bf16[4,2,32,1024]{3,2,1,0:T(8,128)(2,1)S(1)}, bf16[4,2,32,1024]{3,2,1,0:T(8,128)(2,1)S(1)}) custom-call(bf16[384,1024]{1,0:T(8,128)(2,1)S(1)} %copy-done.1, f32[512,384]{1,0:T(8,128)S(1)} %get-tuple-element.24.target_ref, f32[16,384]{1,0:T(8,128)S(1)} %get-tuple-element.25.live_ref, ...), custom_call_target="tpu_custom_call" | custom-call | flops 805306368 | bytes 4063232 | tf_op jit(solution)/shard_map/pallas_call | solution.py:198
  24.6 1.1 %collective-permute-start.19 = (bf16[32,1024]{1,0:T(8,128)(2,1)S(1)}, bf16[32,1024]{1,0:T(8,128)(2,1)S(1)}, u32[]{:S(2)}, u32[]{:S(2)}) collective-permute-start(bf16[32,1024]{1,0:T(8,128)(2,1)S(1)} %fusion.9), channel_id=1, source_target_pairs={{0,2},{1,3},{2,0},{3,1},{4,6},{5,7},{6,4},{7,5},{8,10},{9,11},{10,... | collective-permute-start | bytes 196616 | tf_op jit(solution)/shard_map/ppermute | solution.py:21
  25.7 3.1 %collective-permute-start.12 = (bf16[32,1024]{1,0:T(8,128)(2,1)S(1)}, bf16[32,1024]{1,0:T(8,128)(2,1)S(1)}, u32[]{:S(2)}, u32[]{:S(2)}) collective-permute-start(bf16[32,1024]{1,0:T(8,128)(2,1)S(1)} %get-tuple-element.43), channel_id=1, source_target_pairs={{0,20},{1,21},{2,22},{3,23},{4,0},{5,1},{6,2},{7,3},{8,28},{9,29},... | collective-permute-start | bytes 196616 | tf_op jit(solution)/shard_map/ppermute | solution.py:21
  28.8 1.4 %collective-permute-start.13 = (bf16[32,1024]{1,0:T(8,128)(2,1)S(1)}, bf16[32,1024]{1,0:T(8,128)(2,1)S(1)}, u32[]{:S(2)}, u32[]{:S(2)}) collective-permute-start(bf16[32,1024]{1,0:T(8,128)(2,1)S(1)} %get-tuple-element.44), channel_id=1, source_target_pairs={{0,22},{1,23},{2,20},{3,21},{4,2},{5,3},{6,0},{7,1},{8,30},{9,31},... | collective-permute-start | bytes 196616 | tf_op jit(solution)/shard_map/ppermute | solution.py:21
  30.2 1.5 %collective-permute-done.16 = bf16[2,32,1024]{2,1,0:T(8,128)(2,1)S(1)} collective-permute-done((bf16[2,32,1024]{2,1,0:T(8,128)(2,1)S(1)}, bf16[2,32,1024]{2,1,0:T(8,128)(2,1)S(1)}, u32[]{:S(2)}, u32[]{:S(2)}) %collective-permute-start.16) | collective-permute-done | bytes 131104 | tf_op jit(solution)/shard_map/ppermute | solution.py:21
  31.8 3.1 %collective-permute-start.17 = (bf16[32,1024]{1,0:T(8,128)(2,1)S(1)}, bf16[32,1024]{1,0:T(8,128)(2,1)S(1)}, u32[]{:S(2)}, u32[]{:S(2)}) collective-permute-start(bf16[32,1024]{1,0:T(8,128)(2,1)S(1)} %get-tuple-element.45), channel_id=1, source_target_pairs={{0,24},{1,25},{2,26},{3,27},{4,28},{5,29},{6,30},{7,31},{8,0},{9,1... | collective-permute-start | bytes 196616 | tf_op jit(solution)/shard_map/ppermute | solution.py:21
  34.9 1.6 %collective-permute-start.18 = (bf16[32,1024]{1,0:T(8,128)(2,1)S(1)}, bf16[32,1024]{1,0:T(8,128)(2,1)S(1)}, u32[]{:S(2)}, u32[]{:S(2)}) collective-permute-start(bf16[32,1024]{1,0:T(8,128)(2,1)S(1)} %get-tuple-element.46), channel_id=1, source_target_pairs={{0,26},{1,27},{2,24},{3,25},{4,30},{5,31},{6,28},{7,29},{8,2},{9,3... | collective-permute-start | bytes 196616 | tf_op jit(solution)/shard_map/ppermute | solution.py:21
  36.5 1.5 %shard_map.70 = f32[384,1024]{1,0:T(8,128)} custom-call(bf16[512,384]{1,0:T(8,128)(2,1)S(1)} %get-tuple-element.32.grads_ref, bf16[512,1024]{1,0:T(8,128)(2,1)S(1)} %get-tuple-element.33.window_ref), custom_call_target="tpu_custom_call" | custom-call | flops 402653184 | bytes 3014656 | tf_op jit(solution)/shard_map/pallas_call | solution.py:218
  38.1 2.0 %collective-permute-done.18 = bf16[32,1024]{1,0:T(8,128)(2,1)S(1)} collective-permute-done((bf16[32,1024]{1,0:T(8,128)(2,1)S(1)}, bf16[32,1024]{1,0:T(8,128)(2,1)S(1)}, u32[]{:S(2)}, u32[]{:S(2)}) %collective-permute-start.18) | collective-permute-done | bytes 65568 | tf_op jit(solution)/shard_map/ppermute | solution.py:21
  40.1 0.7 %fusion.8 = f32[32,1024]{1,0:T(8,128)} fusion(f32[2,32,1024]{2,1,0:T(8,128)S(1)} %get-tuple-element.38, bf16[32,1024]{1,0:T(8,128)(2,1)S(1)} %collective-permute-done.19, bf16[32,1024]{1,0:T(8,128)(2,1)S(1)} %collective-permute-done.18, bf16[32,1024]{1,0:T(8,128)(2,1)S(1)} %collective-permute-done.17, bf16[32,1024]{1,0:T(8,128)(2,1)S(1)} %collective-permute-done.13, ...), kind=kLoop, calls=%fused_computation.14 | loop fusion | flops 327680 | bytes 589824 | tf_op jit(solution)/shard_map/add | solution.py:249
  (38 shorter events, 3.7 us)
Async XLA Ops:
  0.6 10.4 %collective-permute-start.1 = (bf16[32,1024]{1,0:T(8,128)(2,1)}, bf16[32,1024]{1,0:T(8,128)(2,1)S(1)}, u32[]{:S(2)}, u32[]{:S(2)}) collective-permute-start(bf16[32,1024]{1,0:T(8,128)(2,1)} %param.6), channel_id=1, source_target_pairs={{0,10},{1,11},{2,8},{3,9},{4,14},{5,15},{6,12},{7,13},{8,18},{9,19... | collective-permute-start | bytes 196616 | tf_op jit(solution)/shard_map/ppermute | solution.py:21
  4.6 6.4 %collective-permute-start = (bf16[32,1024]{1,0:T(8,128)(2,1)}, bf16[32,1024]{1,0:T(8,128)(2,1)S(1)}, u32[]{:S(2)}, u32[]{:S(2)}) collective-permute-start(bf16[32,1024]{1,0:T(8,128)(2,1)} %param.6), channel_id=1, source_target_pairs={{0,8},{1,9},{2,10},{3,11},{4,12},{5,13},{6,14},{7,15},{8,16},{9,17... | collective-permute-start | bytes 196616 | tf_op jit(solution)/shard_map/ppermute | solution.py:21
  6.2 10.9 %collective-permute-start.4 = (bf16[32,1024]{1,0:T(8,128)(2,1)}, bf16[32,1024]{1,0:T(8,128)(2,1)S(1)}, u32[]{:S(2)}, u32[]{:S(2)}) collective-permute-start(bf16[32,1024]{1,0:T(8,128)(2,1)} %param.6), channel_id=1, source_target_pairs={{0,4},{1,5},{2,6},{3,7},{4,16},{5,17},{6,18},{7,19},{8,12},{9,13},... | collective-permute-start | bytes 196616 | tf_op jit(solution)/shard_map/ppermute | solution.py:21
  7.7 9.7 %collective-permute-start.3 = (bf16[32,1024]{1,0:T(8,128)(2,1)}, bf16[32,1024]{1,0:T(8,128)(2,1)S(1)}, u32[]{:S(2)}, u32[]{:S(2)}) collective-permute-start(bf16[32,1024]{1,0:T(8,128)(2,1)} %param.6), channel_id=1, source_target_pairs={{0,2},{1,3},{2,0},{3,1},{4,6},{5,7},{6,4},{7,5},{8,10},{9,11},{10,... | collective-permute-start | bytes 196616 | tf_op jit(solution)/shard_map/ppermute | solution.py:21
  8.3 9.1 %collective-permute-start.5 = (bf16[32,1024]{1,0:T(8,128)(2,1)}, bf16[32,1024]{1,0:T(8,128)(2,1)S(1)}, u32[]{:S(2)}, u32[]{:S(2)}) collective-permute-start(bf16[32,1024]{1,0:T(8,128)(2,1)} %param.6), channel_id=1, source_target_pairs={{0,6},{1,7},{2,4},{3,5},{4,18},{5,19},{6,16},{7,17},{8,14},{9,15},... | collective-permute-start | bytes 196616 | tf_op jit(solution)/shard_map/ppermute | solution.py:21
  11.1 8.4 %collective-permute-start.7 = (bf16[2,32,1024]{2,1,0:T(8,128)(2,1)S(1)}, bf16[2,32,1024]{2,1,0:T(8,128)(2,1)S(1)}, u32[]{:S(2)}, u32[]{:S(2)}) collective-permute-start(bf16[2,32,1024]{2,1,0:T(8,128)(2,1)S(1)} %pad_maximum_fusion.refs_2_), channel_id=1, source_target_pairs={{0,1},{1,0},{2,3},{3,2},{4,5},{5,4},{6,7},{7,6},{8,9},{9,8},{10,11... | collective-permute-start | bytes 393224 | tf_op jit(solution)/shard_map/ppermute | solution.py:21
  11.2 8.3 %collective-permute-start.2 = (bf16[2,32,1024]{2,1,0:T(8,128)(2,1)S(1)}, bf16[2,32,1024]{2,1,0:T(8,128)(2,1)S(1)}, u32[]{:S(2)}, u32[]{:S(2)}) collective-permute-start(bf16[2,32,1024]{2,1,0:T(8,128)(2,1)S(1)} %pad_maximum_fusion.refs_2_), channel_id=1, source_target_pairs={{0,4},{1,5},{2,6},{3,7},{4,0},{5,1},{6,2},{7,3},{8,12},{9,13},{10,... | collective-permute-start | bytes 393224 | tf_op jit(solution)/shard_map/ppermute | solution.py:21
  13.2 1.1 %copy-start = (bf16[384,1024]{1,0:T(8,128)(2,1)S(1)}, bf16[384,1024]{1,0:T(8,128)(2,1)}, u32[]{:S(2)}) copy-start(bf16[384,1024]{1,0:T(8,128)(2,1)} %queries_ref.1) | copy-start | bytes 2359300
  14.4 1.0 %copy-start.2 = (bf16[384,512]{1,0:T(8,128)(2,1)S(1)}, bf16[384,512]{1,0:T(8,128)(2,1)}, u32[]{:S(2)}) copy-start(bf16[384,512]{1,0:T(8,128)(2,1)} %teacher_ref) | copy-start | bytes 1179652
  15.4 0.7 %copy-start.3 = (s32[3,4]{1,0:T(4,128)S(1)}, s32[3,4]{1,0:T(4,128)}, u32[]{:S(2)}) copy-start(s32[3,4]{1,0:T(4,128)} %mask_ref.1) | copy-start | bytes 148
  16.0 4.7 %copy-start.1 = (bf16[384,1024]{1,0:T(8,128)(2,1)S(1)}, bf16[384,1024]{1,0:T(8,128)(2,1)}, u32[]{:S(2)}) copy-start(bf16[384,1024]{1,0:T(8,128)(2,1)} %queries_ref.1) | copy-start | bytes 2359300
  18.2 1.4 %collective-permute-start.6 = (bf16[2,32,1024]{2,1,0:T(8,128)(2,1)S(1)}, bf16[2,32,1024]{2,1,0:T(8,128)(2,1)S(1)}, u32[]{:S(2)}, u32[]{:S(2)}) collective-permute-start(bf16[2,32,1024]{2,1,0:T(8,128)(2,1)S(1)} %pad_maximum_fusion.1.refs_0_), channel_id=1, source_target_pairs={{0,1},{1,0},{2,3},{3,2},{4,5},{5,4},{6,7},{7,6},{8,9},{9,8},{10,11... | collective-permute-start | bytes 393224 | tf_op jit(solution)/shard_map/ppermute | solution.py:21
  18.3 1.5 %collective-permute-start.8 = (bf16[2,32,1024]{2,1,0:T(8,128)(2,1)S(1)}, bf16[2,32,1024]{2,1,0:T(8,128)(2,1)S(1)}, u32[]{:S(2)}, u32[]{:S(2)}) collective-permute-start(bf16[2,32,1024]{2,1,0:T(8,128)(2,1)S(1)} %pad_maximum_fusion.2.refs_4_), channel_id=1, source_target_pairs={{0,1},{1,0},{2,3},{3,2},{4,5},{5,4},{6,7},{7,6},{8,9},{9,8},{10,11... | collective-permute-start | bytes 393224 | tf_op jit(solution)/shard_map/ppermute | solution.py:21
  19.4 1.3 %collective-permute-start.9 = (bf16[2,32,1024]{2,1,0:T(8,128)(2,1)S(1)}, bf16[2,32,1024]{2,1,0:T(8,128)(2,1)S(1)}, u32[]{:S(2)}, u32[]{:S(2)}) collective-permute-start(bf16[2,32,1024]{2,1,0:T(8,128)(2,1)S(1)} %collective-permute-done.2.refs_6_), channel_id=1, source_target_pairs={{0,1},{1,0},{2,3},{3,2},{4,5},{5,4},{6,7},{7,6},{8,9},{9,8},{10,11... | collective-permute-start | bytes 393224 | tf_op jit(solution)/shard_map/ppermute | solution.py:21
  22.6 1.4 %collective-permute-start.11 = (bf16[2,32,1024]{2,1,0:T(8,128)(2,1)S(1)}, bf16[2,32,1024]{2,1,0:T(8,128)(2,1)S(1)}, u32[]{:S(2)}, u32[]{:S(2)}) collective-permute-start(bf16[2,32,1024]{2,1,0:T(8,128)(2,1)S(1)} %get-tuple-element.39), channel_id=1, source_target_pairs={{0,1},{1,0},{2,3},{3,2},{4,5},{5,4},{6,7},{7,6},{8,9},{9,8},{10,11... | collective-permute-start | bytes 393224 | tf_op jit(solution)/shard_map/ppermute | solution.py:21
  22.8 1.4 %collective-permute-start.15 = (bf16[2,32,1024]{2,1,0:T(8,128)(2,1)S(1)}, bf16[2,32,1024]{2,1,0:T(8,128)(2,1)S(1)}, u32[]{:S(2)}, u32[]{:S(2)}) collective-permute-start(bf16[2,32,1024]{2,1,0:T(8,128)(2,1)S(1)} %get-tuple-element.40), channel_id=1, source_target_pairs={{0,1},{1,0},{2,3},{3,2},{4,5},{5,4},{6,7},{7,6},{8,9},{9,8},{10,11... | collective-permute-start | bytes 393224 | tf_op jit(solution)/shard_map/ppermute | solution.py:21
  23.2 1.3 %collective-permute-start.10 = (bf16[2,32,1024]{2,1,0:T(8,128)(2,1)S(1)}, bf16[2,32,1024]{2,1,0:T(8,128)(2,1)S(1)}, u32[]{:S(2)}, u32[]{:S(2)}) collective-permute-start(bf16[2,32,1024]{2,1,0:T(8,128)(2,1)S(1)} %get-tuple-element.42), channel_id=1, source_target_pairs={{0,1},{1,0},{2,3},{3,2},{4,5},{5,4},{6,7},{7,6},{8,9},{9,8},{10,11... | collective-permute-start | bytes 393224 | tf_op jit(solution)/shard_map/ppermute | solution.py:21
  23.3 6.9 %collective-permute-start.14 = (bf16[2,32,1024]{2,1,0:T(8,128)(2,1)S(1)}, bf16[2,32,1024]{2,1,0:T(8,128)(2,1)S(1)}, u32[]{:S(2)}, u32[]{:S(2)}) collective-permute-start(bf16[2,32,1024]{2,1,0:T(8,128)(2,1)S(1)} %get-tuple-element.41), channel_id=1, source_target_pairs={{0,1},{1,0},{2,3},{3,2},{4,5},{5,4},{6,7},{7,6},{8,9},{9,8},{10,11... | collective-permute-start | bytes 393224 | tf_op jit(solution)/shard_map/ppermute | solution.py:21
  24.6 13.4 %collective-permute-start.19 = (bf16[32,1024]{1,0:T(8,128)(2,1)S(1)}, bf16[32,1024]{1,0:T(8,128)(2,1)S(1)}, u32[]{:S(2)}, u32[]{:S(2)}) collective-permute-start(bf16[32,1024]{1,0:T(8,128)(2,1)S(1)} %fusion.9), channel_id=1, source_target_pairs={{0,2},{1,3},{2,0},{3,1},{4,6},{5,7},{6,4},{7,5},{8,10},{9,11},{10,... | collective-permute-start | bytes 196616 | tf_op jit(solution)/shard_map/ppermute | solution.py:21
  25.7 6.0 %collective-permute-start.16 = (bf16[2,32,1024]{2,1,0:T(8,128)(2,1)S(1)}, bf16[2,32,1024]{2,1,0:T(8,128)(2,1)S(1)}, u32[]{:S(2)}, u32[]{:S(2)}) collective-permute-start(bf16[2,32,1024]{2,1,0:T(8,128)(2,1)S(1)} %get-tuple-element.37), channel_id=1, source_target_pairs={{0,4},{1,5},{2,6},{3,7},{4,0},{5,1},{6,2},{7,3},{8,12},{9,13},{10,... | collective-permute-start | bytes 393224 | tf_op jit(solution)/shard_map/ppermute | solution.py:21
  25.7 12.3 %collective-permute-start.12 = (bf16[32,1024]{1,0:T(8,128)(2,1)S(1)}, bf16[32,1024]{1,0:T(8,128)(2,1)S(1)}, u32[]{:S(2)}, u32[]{:S(2)}) collective-permute-start(bf16[32,1024]{1,0:T(8,128)(2,1)S(1)} %get-tuple-element.43), channel_id=1, source_target_pairs={{0,20},{1,21},{2,22},{3,23},{4,0},{5,1},{6,2},{7,3},{8,28},{9,29},... | collective-permute-start | bytes 196616 | tf_op jit(solution)/shard_map/ppermute | solution.py:21
  28.8 9.2 %collective-permute-start.13 = (bf16[32,1024]{1,0:T(8,128)(2,1)S(1)}, bf16[32,1024]{1,0:T(8,128)(2,1)S(1)}, u32[]{:S(2)}, u32[]{:S(2)}) collective-permute-start(bf16[32,1024]{1,0:T(8,128)(2,1)S(1)} %get-tuple-element.44), channel_id=1, source_target_pairs={{0,22},{1,23},{2,20},{3,21},{4,2},{5,3},{6,0},{7,1},{8,30},{9,31},... | collective-permute-start | bytes 196616 | tf_op jit(solution)/shard_map/ppermute | solution.py:21
  31.8 6.2 %collective-permute-start.17 = (bf16[32,1024]{1,0:T(8,128)(2,1)S(1)}, bf16[32,1024]{1,0:T(8,128)(2,1)S(1)}, u32[]{:S(2)}, u32[]{:S(2)}) collective-permute-start(bf16[32,1024]{1,0:T(8,128)(2,1)S(1)} %get-tuple-element.45), channel_id=1, source_target_pairs={{0,24},{1,25},{2,26},{3,27},{4,28},{5,29},{6,30},{7,31},{8,0},{9,1... | collective-permute-start | bytes 196616 | tf_op jit(solution)/shard_map/ppermute | solution.py:21
  34.9 5.2 %collective-permute-start.18 = (bf16[32,1024]{1,0:T(8,128)(2,1)S(1)}, bf16[32,1024]{1,0:T(8,128)(2,1)S(1)}, u32[]{:S(2)}, u32[]{:S(2)}) collective-permute-start(bf16[32,1024]{1,0:T(8,128)(2,1)S(1)} %get-tuple-element.46), channel_id=1, source_target_pairs={{0,26},{1,27},{2,24},{3,25},{4,30},{5,31},{6,28},{7,29},{8,2},{9,3... | collective-permute-start | bytes 196616 | tf_op jit(solution)/shard_map/ppermute | solution.py:21

commit v3 on v2

--- a/solution.py
+++ b/solution.py
@@ -40,38 +40,31 @@
     return pl.multiple_of((own_step * count_cols + (own_col ^ offset)) * own_rows, own_rows)
 
 
-def target_kernel(
-    slot_steps, count_cols, score_scale, own_rows, mask_ref, weights_ref, teacher_ref, queries_ref,
-    target_ref, live_ref, factor_ref, flat_ref,
-):
-    del queries_ref
+def target_kernel(slot_steps, count_cols, own_rows, mask_ref, packed_ref, target_ref, flat_ref):
     window, count_rows = target_ref.shape
+    width = packed_ref.shape[1] - window
     tiles, tile_count = mask_ref.shape
     tile_rows, tile_cols = count_rows // tiles, window // tile_count
-    factor_ref[...] = weights_ref[...] * score_scale
     for tile in range(tiles):
         rows = slice(tile * tile_rows, (tile + 1) * tile_rows)
-        taught = teacher_ref[rows, :].astype(jnp.float32).T
-        blocks = []
+        taught = packed_ref[rows, width:].astype(jnp.float32).T
+        lives, blocks = [], []
         for col in range(tile_count):
             part = taught[col * tile_cols : (col + 1) * tile_cols, :]
-            blocks.append(jnp.where(mask_ref[tile, col] > 0, part, very_negative))
+            live = jnp.broadcast_to(mask_ref[tile : tile + 1, col : col + 1], part.shape) > 0
+            lives.append(live)
+            blocks.append(jnp.where(live, part, very_negative))
         for col, block in enumerate(softmax_cols(blocks)):
-            flat_ref[col * tile_cols : (col + 1) * tile_cols, rows] = block
-    for number in range(window // own_rows):
-        col = piece_col(number, slot_steps, count_cols, own_rows)
-        target_ref[number * own_rows : (number + 1) * own_rows, :] = flat_ref[pl.ds(col, own_rows), :]
-        for tile in range(tiles):
-            live = mask_ref[tile, col // tile_cols].astype(jnp.float32)
-            live_ref[number : number + 1, tile * tile_rows : (tile + 1) * tile_rows] = jnp.full(
-                (1, tile_rows), live, jnp.float32
-            )
-
-
-def grads_kernel(score_scale, queries_ref, target_ref, live_ref, factor_ref, *refs):
+            flat_ref[col * tile_cols : (col + 1) * tile_cols, :] = jnp.where(lives[col], block, -1.0)
+        for number in range(window // own_rows):
+            col = piece_col(number, slot_steps, count_cols, own_rows)
+            target_ref[number * own_rows : (number + 1) * own_rows, rows] = flat_ref[pl.ds(col, own_rows), :]
+
+
+def grads_kernel(score_scale, packed_ref, target_ref, weights_ref, *refs):
     grads_ref, window_ref, send_ref, keep_ref, scores_ref = refs[-5:]
     pieces = refs[:-5]
-    halves, own_rows = pieces[0].shape[:2]
+    halves, own_rows, width = pieces[0].shape
     count_rows = grads_ref.shape[1]
     lanes = 128 if count_rows % 128 == 0 else count_rows
     for number in range(len(pieces) * halves):
@@ -79,26 +72,22 @@
         window_ref[number * own_rows : (number + 1) * own_rows, :] = pieces[2 * slot + offset % 2][offset // 2]
     scores_ref[...] = score_scale * lax.dot_general(
         window_ref[...],
-        queries_ref[...],
+        packed_ref[:count_rows, :width],
         (((1,), (1,)), ((), ())),
         preferred_element_type=jnp.float32,
     )
     for first in range(0, count_rows, lanes):
         rows = slice(first, first + lanes)
-        blocks = []
-        for number in range(len(pieces) * halves):
-            part = scores_ref[number * own_rows : (number + 1) * own_rows, rows]
-            blocks.append(jnp.where(live_ref[number : number + 1, rows] > 0, part, very_negative))
-        factor = factor_ref[:, rows]
-        for number, student in enumerate(softmax_cols(blocks)):
-            cols = slice(number * own_rows, (number + 1) * own_rows)
-            grads_ref[cols, rows] = (factor * (student - target_ref[cols, rows])).astype(jnp.bfloat16)
+        target = target_ref[:, rows]
+        (student,) = softmax_cols([jnp.where(target >= 0, scores_ref[:, rows], very_negative)])
+        factor = weights_ref[:, rows] * score_scale
+        grads_ref[:, rows] = (factor * (student - jnp.maximum(target, 0.0))).astype(jnp.bfloat16)
     slots = send_ref.shape[0]
     panel = 2 * halves * own_rows
     for slot in reversed(range(slots)):
         term = jnp.dot(
             grads_ref[slot * panel : (slot + 1) * panel, :],
-            queries_ref[...],
+            packed_ref[:count_rows, :width],
             preferred_element_type=jnp.float32,
         ).astype(jnp.bfloat16)
         for half in range(halves):
@@ -136,7 +125,6 @@
     tiles = tile_mask.shape[0]
     evens = range(0, count_cols, 2)
     vmem = pl.BlockSpec(memory_space=pltpu.VMEM)
-    smem = pl.BlockSpec(memory_space=pltpu.SMEM)
     far = pl.BlockSpec(memory_space=pltpu.HBM)
     budget = 8 * 2**20 + 6 * window * width * 2 + 2 * count_rows * (window + width) * 4
     params = pltpu.CompilerParams(vmem_limit_bytes=min(budget, 50 * 2**20))
@@ -160,39 +148,40 @@
         back = {move(p, c): (p, c) for p in range(count_pb) for c in range(count_cols)}
         return lambda p, c: back[(p, c)]
 
-    def joined(parts):
-        return jnp.stack(parts)
-
-    second = joined([moved_to(groups, ahead(offset)) for offset in evens])
-    thirds = [moved_to(groups, across(offset)) for offset in evens]
-    firsts = [groups] + [moved_to(groups, own(offset)) for offset in evens[1:]]
-    fourth = moved_to(second, beside)
-
-    teacher, queries, _ = lax.optimization_barrier((teacher, queries, second))
-    target, live, factor = pl.pallas_call(
-        functools.partial(target_kernel, slot_steps, count_cols, score_scale, own_rows),
-        out_shape=(
-            jax.ShapeDtypeStruct((window, count_rows), jnp.float32),
-            jax.ShapeDtypeStruct((window // own_rows, count_rows), jnp.float32),
-            jax.ShapeDtypeStruct((1, count_rows), jnp.float32),
-        ),
-        in_specs=[smem, vmem, vmem, vmem],
-        out_specs=(vmem,) * 3,
-        scratch_shapes=[pltpu.VMEM((window, count_rows), jnp.float32)],
+    def after(value, *others):
+        return lax.optimization_barrier((value, *others))[0]
+
+    seconds = [moved_to(groups, ahead(offset)) for offset in evens]
+    third = moved_to(groups, across(0))
+    packed = jnp.concatenate(
+        [
+            jnp.concatenate([queries, teacher], axis=1),
+            jnp.pad(groups, ((0, 0), (0, window))),
+        ],
+        axis=0,
+    )
+    seconds = [after(seconds[0], packed)] + seconds[1:]
+    fourths = [moved_to(block, beside) for block in seconds]
+    late_packed = after(packed, fourths[0])
+    target = pl.pallas_call(
+        functools.partial(target_kernel, slot_steps, count_cols, own_rows),
+        out_shape=jax.ShapeDtypeStruct((window, count_rows), jnp.float32),
+        in_specs=[vmem, vmem],
+        out_specs=vmem,
+        scratch_shapes=[pltpu.VMEM((window, count_rows // tiles), jnp.float32)],
         compiler_params=params,
         cost_estimate=pl.CostEstimate(
             flops=8 * count_rows * window,
-            bytes_accessed=6 * count_rows * (window + width),
+            bytes_accessed=6 * count_rows * window,
             transcendentals=count_rows * window,
         ),
-    )(tile_mask, weights[None, :], teacher, queries)
-    thirds, target = lax.optimization_barrier((thirds, target))
-    firsts, target = lax.optimization_barrier((firsts, target))
-    fourth, target = lax.optimization_barrier((fourth, target))
-    first, third = joined(firsts), joined(thirds)
-    held = [first, second, third, fourth]
+    )(tile_mask, late_packed)
+    near_groups = after(groups, seconds[0])
+    firsts = [near_groups] + [moved_to(near_groups, own(offset)) for offset in evens[1:]]
+    thirds = [third] + [moved_to(third, own(offset)) for offset in evens[1:]]
     pieces = []
-    for block in held:
+    for blocks in (firsts, seconds, thirds, fourths):
+        block = jnp.stack(blocks)
         pieces += [block, moved_to(block, own(1))]
 
     grads, gathered, send, keep = pl.pallas_call(
@@ -203,7 +192,7 @@
             jax.ShapeDtypeStruct((steps, count_cols // 2, own_rows, width), jnp.bfloat16),
             jax.ShapeDtypeStruct((steps, count_cols // 2, own_rows, width), jnp.bfloat16),
         ),
-        in_specs=[vmem] * (4 + len(pieces)),
+        in_specs=[vmem] * (3 + len(pieces)),
         out_specs=(vmem,) * 4,
         scratch_shapes=[pltpu.VMEM((window, count_rows), jnp.float32)],
         compiler_params=params,
@@ -212,7 +201,7 @@
             bytes_accessed=2 * count_rows * width + 4 * window * width + 6 * count_rows * window,
             transcendentals=count_rows * window,
         ),
-    )(queries, target, live, factor, *pieces)
+    )(packed, target, weights[None, :], *pieces)
 
     rows = count_rows // tiles
     query_grad = pl.pallas_call(
@@ -232,21 +221,26 @@
         ),
     )(grads, gathered)
 
-    sums = []
-    for slot in range(steps):
-        other = swapped(send[slot], 1)
-        sums.append(keep[slot].astype(jnp.float32) + other.astype(jnp.float32))
-
     def arrived(block, move):
         return moved_to(block.astype(jnp.bfloat16), move).astype(jnp.float32)
 
-    sums[1] = sums[1] + arrived(sums[3], beside)
-    moves = ((2, across), (1, ahead), (0, own))
-    group_grad = sums[0][0]
-    for slot, move in moves:
-        for offset in evens:
-            if slot > 0 or offset > 0:
-                group_grad = group_grad + arrived(sums[slot][offset // 2], reverse(move(offset)))
+    sums = {}
+    last = None
+    for slot in (3, 2, 1, 0):
+        other = moved_to(send[slot], own(1))
+        if last is not None:
+            other = after(other, last)
+        last = keep[slot].astype(jnp.float32) + other.astype(jnp.float32)
+        sums[slot] = [last[offset // 2] for offset in evens]
+    third = sums[2][0]
+    for offset in evens[1:]:
+        third = third + arrived(sums[2][offset // 2], own(offset))
+    seconds = [part + arrived(fourth, beside) for part, fourth in zip(sums[1], sums[3])]
+    group_grad = sums[0][0] + arrived(third, reverse(across(0)))
+    for offset in evens:
+        group_grad = group_grad + arrived(seconds[offset // 2], reverse(ahead(offset)))
+    for offset in evens[1:]:
+        group_grad = group_grad + arrived(sums[0][offset // 2], own(offset))
     return (query_grad, group_grad)
 
 

time: 41.1 us -> 38.1 us (0.927)
  local copies, waits for them, and re-layouts: 3.56 us -> 0.08 us
  waiting for transfers between devices: 6.46 us -> 7.81 us
  starting transfers between devices: 23.9 us -> 23.2 us
  other arithmetic: 1.77 us -> 2.31 us
  Pallas kernels: 4.27 us -> 3.75 us
    unnamed x8 -> x6, local copies, waits for them, and re-layouts: 2.81 us -> 0.01 us
    concatenate x0 -> x1, other arithmetic: none -> 1.37 us  [on_device(): jnp.concatenate([jnp.concatenate([queries, teacher], axis=1), jnp.pad(gro...]
    ppermute x20 -> x22, waiting for transfers between devices: 6.46 us -> 7.81 us  [moved_to(): return lax.ppermute(block, ('pb', 'col'), pairs)]
    another operation x5, other arithmetic: 1.06 us -> 0.12 us  [the longest x3 0.88 us: joined(): return jnp.stack(parts)]
    ppermute x20 -> x22, starting transfers between devices: 23.9 us -> 23.2 us  [moved_to(): return lax.ppermute(block, ('pb', 'col'), pairs)]
    broadcast_in_dim x1, local copies, waits for them, and re-layouts: 0.68 us -> 0.01 us  [on_device(): weights[None, :]]
    pallas_call x1, Pallas kernels: 1.01 us -> 0.49 us  [on_device(): pl.pallas_call(functools.partial(target_kernel, slot_steps, count_cols, o...]
  transfers between devices with their start and end apart: 20 -> 22, of which waited for: 10 -> 9; matrix products, arithmetic and copies ran while one was open for 4% -> 4% of each run, Pallas kernels for 6% -> 5%
where the time goes in v3:
time: 38.1 us; the launch traced here: 38 us
  starting transfers between devices  23.2 us (61%)
  waiting for transfers between devices  7.81 us (20%)
  Pallas kernels  3.75 us (10%)
  other arithmetic  2.31 us (6%)
  between operations  0.84 us (2%)
    ppermute x22, starting transfers between devices, moved_to(): return lax.ppermute(block, ('pb', 'col'), pairs)  23.2 us
    ppermute x22, waiting for transfers between devices, moved_to(): return lax.ppermute(block, ('pb', 'col'), pairs)  7.81 us
    pallas_call x1, Pallas kernels, on_device(): pl.pallas_call(functools.partial(grads_kernel, score_scale), out_shape=(j...  1.76 us
    pallas_call x1, Pallas kernels, on_device(): pl.pallas_call(query_grad_kernel, out_shape=jax.ShapeDtypeStruct((count_r...  1.5 us
    concatenate x1, other arithmetic, on_device(): jnp.concatenate([jnp.concatenate([queries, teacher], axis=1), jnp.pad(gro...  1.37 us
  transfers between devices with their start and end apart: 22, of which 9 were waited for; matrix products, arithmetic and copies ran while one was open for 4% of the time, Pallas kernels for 5%

profile of v3, /device:TPU:0, one launch (start us, length us, event | category | flops | bytes accessed | tf_op | source)
XLA Modules:
  0.0 38.0 jit_solution(9987717087659690874)
XLA Ops:
  0.7 3.1 %collective-permute-start = (bf16[32,1024]{1,0:T(8,128)(2,1)}, bf16[32,1024]{1,0:T(8,128)(2,1)S(1)}, u32[]{:S(2)}, u32[]{:S(2)}) collective-permute-start(bf16[32,1024]{1,0:T(8,128)(2,1)} %param.6), channel_id=1, source_target_pairs={{0,8},{1,9},{2,10},{3,11},{4,12},{5,13},{6,14},{7,15},{8,16},{9,17... | collective-permute-start | bytes 196616 | tf_op jit(solution)/shard_map/ppermute | solution.py:21
  3.7 1.5 %collective-permute-start.6 = (bf16[32,1024]{1,0:T(8,128)(2,1)}, bf16[32,1024]{1,0:T(8,128)(2,1)S(1)}, u32[]{:S(2)}, u32[]{:S(2)}) collective-permute-start(bf16[32,1024]{1,0:T(8,128)(2,1)} %param.6), channel_id=1, source_target_pairs={{0,4},{1,5},{2,6},{3,7},{4,16},{5,17},{6,18},{7,19},{8,12},{9,13},... | collective-permute-start | bytes 196616 | tf_op jit(solution)/shard_map/ppermute | solution.py:21
  5.3 2.5 %collective-permute-start.4 = (bf16[32,1024]{1,0:T(8,128)(2,1)}, bf16[32,1024]{1,0:T(8,128)(2,1)S(1)}, u32[]{:S(2)}, u32[]{:S(2)}) collective-permute-start(bf16[32,1024]{1,0:T(8,128)(2,1)} %param.6), channel_id=1, source_target_pairs={{0,10},{1,11},{2,8},{3,9},{4,14},{5,15},{6,12},{7,13},{8,18},{9,19... | collective-permute-start | bytes 196616 | tf_op jit(solution)/shard_map/ppermute | solution.py:21
  7.8 1.4 %fusion.1.packed_ref = bf16[416,1536]{1,0:T(8,128)(2,1)S(1)} fusion(bf16[32,1024]{1,0:T(8,128)(2,1)} %param.6, bf16[384,512]{1,0:T(8,128)(2,1)} %param.7, bf16[384,1024]{1,0:T(8,128)(2,1)} %param.5), kind=kLoop, calls=%fused_computation.2 | loop fusion | flops 5111808 | bytes 2523136 | tf_op jit(solution)/shard_map/concatenate | solution.py:156
  9.1 1.3 %collective-permute-start.1 = (bf16[32,1024]{1,0:T(8,128)(2,1)S(1)}, bf16[32,1024]{1,0:T(8,128)(2,1)S(1)}, u32[]{:S(2)}, u32[]{:S(2)}) collective-permute-start(bf16[32,1024]{1,0:T(8,128)(2,1)S(1)} %collective-permute-done), channel_id=1, source_target_pairs={{0,4},{1,5},{2,6},{3,7},{4,0},{5,1},{6,2},{7,3},{8,12},{9,13},{10,... | collective-permute-start | bytes 196616 | tf_op jit(solution)/shard_map/ppermute | solution.py:21
  10.4 1.5 %collective-permute-start.2 = (bf16[32,1024]{1,0:T(8,128)(2,1)S(1)}, bf16[32,1024]{1,0:T(8,128)(2,1)S(1)}, u32[]{:S(2)}, u32[]{:S(2)}) collective-permute-start(bf16[32,1024]{1,0:T(8,128)(2,1)S(1)} %copy-done.1), channel_id=1, source_target_pairs={{0,2},{1,3},{2,0},{3,1},{4,6},{5,7},{6,4},{7,5},{8,10},{9,11},{10,... | collective-permute-start | bytes 196616 | tf_op jit(solution)/shard_map/ppermute | solution.py:21
  11.9 2.1 %collective-permute-start.7 = (bf16[32,1024]{1,0:T(8,128)(2,1)S(1)}, bf16[32,1024]{1,0:T(8,128)(2,1)S(1)}, u32[]{:S(2)}, u32[]{:S(2)}) collective-permute-start(bf16[32,1024]{1,0:T(8,128)(2,1)S(1)} %collective-permute-done.6), channel_id=1, source_target_pairs={{0,2},{1,3},{2,0},{3,1},{4,6},{5,7},{6,4},{7,5},{8,10},{9,11},{10,... | collective-permute-start | bytes 196616 | tf_op jit(solution)/shard_map/ppermute | solution.py:21
  14.2 1.1 %collective-permute-start.9 = (bf16[32,1024]{1,0:T(8,128)(2,1)S(1)}, bf16[32,1024]{1,0:T(8,128)(2,1)S(1)}, u32[]{:S(2)}, u32[]{:S(2)}) collective-permute-start(bf16[32,1024]{1,0:T(8,128)(2,1)S(1)} %collective-permute-done.4), channel_id=1, source_target_pairs={{0,4},{1,5},{2,6},{3,7},{4,0},{5,1},{6,2},{7,3},{8,12},{9,13},{10,... | collective-permute-start | bytes 196616 | tf_op jit(solution)/shard_map/ppermute | solution.py:21
  15.2 1.1 %collective-permute-done.7 = bf16[32,1024]{1,0:T(8,128)(2,1)S(1)} collective-permute-done((bf16[32,1024]{1,0:T(8,128)(2,1)S(1)}, bf16[32,1024]{1,0:T(8,128)(2,1)S(1)}, u32[]{:S(2)}, u32[]{:S(2)}) %collective-permute-start.7) | collective-permute-done | bytes 65568 | tf_op jit(solution)/shard_map/ppermute | solution.py:21
  16.4 2.3 %collective-permute-done.9 = bf16[32,1024]{1,0:T(8,128)(2,1)S(1)} collective-permute-done((bf16[32,1024]{1,0:T(8,128)(2,1)S(1)}, bf16[32,1024]{1,0:T(8,128)(2,1)S(1)}, u32[]{:S(2)}, u32[]{:S(2)}) %collective-permute-start.9) | collective-permute-done | bytes 65568 | tf_op jit(solution)/shard_map/ppermute | solution.py:21
  18.8 0.5 %collective-permute-start.3 = (bf16[2,32,1024]{2,1,0:T(8,128)(2,1)S(1)}, bf16[2,32,1024]{2,1,0:T(8,128)(2,1)S(1)}, u32[]{:S(2)}, u32[]{:S(2)}) collective-permute-start(bf16[2,32,1024]{2,1,0:T(8,128)(2,1)S(1)} %pad_maximum_fusion.refs_0_), channel_id=1, source_target_pairs={{0,1},{1,0},{2,3},{3,2},{4,5},{5,4},{6,7},{7,6},{8,9},{9,8},{10,11... | collective-permute-start | bytes 393224 | tf_op jit(solution)/shard_map/ppermute | solution.py:21
  19.4 0.5 %shard_map.68.target_ref = f32[512,384]{1,0:T(8,128)S(1)} custom-call(s32[3,4]{1,0:T(4,128)S(1)} %copy-done, bf16[416,1536]{1,0:T(8,128)(2,1)S(1)} %fusion.1.packed_ref), custom_call_target="tpu_custom_call" | custom-call | flops 1572864 | bytes 1179648 | tf_op jit(solution)/shard_map/pallas_call | solution.py:166
  20.4 1.8 %shard_map.69 = (bf16[512,384]{1,0:T(8,128)(2,1)S(1)}, bf16[512,1024]{1,0:T(8,128)(2,1)S(1)}, bf16[4,2,32,1024]{3,2,1,0:T(8,128)(2,1)S(1)}, bf16[4,2,32,1024]{3,2,1,0:T(8,128)(2,1)S(1)}) custom-call(bf16[416,1536]{1,0:T(8,128)(2,1)S(1)} %fusion.1.packed_ref, f32[512,384]{1,0:T(8,128)S(1)} %shard_map.68.target_ref, f32[1,384]{1,0:T(1,128)S(1)} %broadcast_in_dim.3.weights_ref, ...), custom_call_target="tpu_custom_call" | custom-call | flops 805306368 | bytes 4063232 | tf_op jit(solution)/shard_map/pallas_call | solution.py:187
  22.2 0.4 %collective-permute-start.13 = (bf16[2,32,1024]{2,1,0:T(8,128)(2,1)S(1)}, bf16[2,32,1024]{2,1,0:T(8,128)(2,1)S(1)}, u32[]{:S(2)}, u32[]{:S(2)}) collective-permute-start(bf16[2,32,1024]{2,1,0:T(8,128)(2,1)S(1)} %get-tuple-element.25), channel_id=1, source_target_pairs={{0,1},{1,0},{2,3},{3,2},{4,5},{5,4},{6,7},{7,6},{8,9},{9,8},{10,11... | collective-permute-start | bytes 393224 | tf_op jit(solution)/shard_map/ppermute | solution.py:21
  24.0 0.8 %collective-permute-start.15 = (bf16[32,1024]{1,0:T(8,128)(2,1)S(1)}, bf16[32,1024]{1,0:T(8,128)(2,1)S(1)}, u32[]{:S(2)}, u32[]{:S(2)}) collective-permute-start(bf16[32,1024]{1,0:T(8,128)(2,1)S(1)} %fusion.12), channel_id=1, source_target_pairs={{0,2},{1,3},{2,0},{3,1},{4,6},{5,7},{6,4},{7,5},{8,10},{9,11},{10,... | collective-permute-start | bytes 196616 | tf_op jit(solution)/shard_map/ppermute | solution.py:21
  24.8 1.8 %collective-permute-start.17 = (bf16[32,1024]{1,0:T(8,128)(2,1)S(1)}, bf16[32,1024]{1,0:T(8,128)(2,1)S(1)}, u32[]{:S(2)}, u32[]{:S(2)}) collective-permute-start(bf16[32,1024]{1,0:T(8,128)(2,1)S(1)} %get-tuple-element.30), channel_id=1, source_target_pairs={{0,4},{1,5},{2,6},{3,7},{4,0},{5,1},{6,2},{7,3},{8,12},{9,13},{10,... | collective-permute-start | bytes 196616 | tf_op jit(solution)/shard_map/ppermute | solution.py:21
  27.0 1.4 %collective-permute-start.21 = (bf16[32,1024]{1,0:T(8,128)(2,1)S(1)}, bf16[32,1024]{1,0:T(8,128)(2,1)S(1)}, u32[]{:S(2)}, u32[]{:S(2)}) collective-permute-start(bf16[32,1024]{1,0:T(8,128)(2,1)S(1)} %fusion.13), channel_id=1, source_target_pairs={{0,2},{1,3},{2,0},{3,1},{4,6},{5,7},{6,4},{7,5},{8,10},{9,11},{10,... | collective-permute-start | bytes 196616 | tf_op jit(solution)/shard_map/ppermute | solution.py:21
  28.4 1.3 %collective-permute-start.16 = (bf16[32,1024]{1,0:T(8,128)(2,1)S(1)}, bf16[32,1024]{1,0:T(8,128)(2,1)S(1)}, u32[]{:S(2)}, u32[]{:S(2)}) collective-permute-start(bf16[32,1024]{1,0:T(8,128)(2,1)S(1)} %fusion.7), channel_id=1, source_target_pairs={{0,20},{1,21},{2,22},{3,23},{4,0},{5,1},{6,2},{7,3},{8,28},{9,29},... | collective-permute-start | bytes 196616 | tf_op jit(solution)/shard_map/ppermute | solution.py:21
  29.7 1.8 %collective-permute-done.19 = bf16[32,1024]{1,0:T(8,128)(2,1)S(1)} collective-permute-done((bf16[32,1024]{1,0:T(8,128)(2,1)S(1)}, bf16[32,1024]{1,0:T(8,128)(2,1)S(1)}, u32[]{:S(2)}, u32[]{:S(2)}) %collective-permute-start.19) | collective-permute-done | bytes 65568 | tf_op jit(solution)/shard_map/ppermute | solution.py:21
  31.6 0.5 %collective-permute-start.18 = (bf16[32,1024]{1,0:T(8,128)(2,1)S(1)}, bf16[32,1024]{1,0:T(8,128)(2,1)S(1)}, u32[]{:S(2)}, u32[]{:S(2)}) collective-permute-start(bf16[32,1024]{1,0:T(8,128)(2,1)S(1)} %get-tuple-element.28), channel_id=1, source_target_pairs={{0,24},{1,25},{2,26},{3,27},{4,28},{5,29},{6,30},{7,31},{8,0},{9,1... | collective-permute-start | bytes 196616 | tf_op jit(solution)/shard_map/ppermute | solution.py:21
  32.1 2.2 %collective-permute-start.20 = (bf16[32,1024]{1,0:T(8,128)(2,1)S(1)}, bf16[32,1024]{1,0:T(8,128)(2,1)S(1)}, u32[]{:S(2)}, u32[]{:S(2)}) collective-permute-start(bf16[32,1024]{1,0:T(8,128)(2,1)S(1)} %get-tuple-element.29), channel_id=1, source_target_pairs={{0,26},{1,27},{2,24},{3,25},{4,30},{5,31},{6,28},{7,29},{8,2},{9,3... | collective-permute-start | bytes 196616 | tf_op jit(solution)/shard_map/ppermute | solution.py:21
  34.3 1.5 %shard_map.70 = f32[384,1024]{1,0:T(8,128)} custom-call(bf16[512,384]{1,0:T(8,128)(2,1)S(1)} %get-tuple-element.15.grads_ref, bf16[512,1024]{1,0:T(8,128)(2,1)S(1)} %get-tuple-element.16.window_ref), custom_call_target="tpu_custom_call" | custom-call | flops 402653184 | bytes 3014656 | tf_op jit(solution)/shard_map/pallas_call | solution.py:207
  35.9 1.4 %collective-permute-done.20 = bf16[32,1024]{1,0:T(8,128)(2,1)S(1)} collective-permute-done((bf16[32,1024]{1,0:T(8,128)(2,1)S(1)}, bf16[32,1024]{1,0:T(8,128)(2,1)S(1)}, u32[]{:S(2)}, u32[]{:S(2)}) %collective-permute-start.20) | collective-permute-done | bytes 65568 | tf_op jit(solution)/shard_map/ppermute | solution.py:21
  37.3 0.7 %fusion.11 = f32[32,1024]{1,0:T(8,128)} fusion(f32[2,32,1024]{2,1,0:T(8,128)S(1)} %convert_add_fusion.3, bf16[32,1024]{1,0:T(8,128)(2,1)S(1)} %collective-permute-done.21, bf16[32,1024]{1,0:T(8,128)(2,1)S(1)} %collective-permute-done.20, bf16[32,1024]{1,0:T(8,128)(2,1)S(1)} %collective-permute-done.18, bf16[32,1024]{1,0:T(8,128)(2,1)S(1)} %collective-permute-done.16), kind=kLoop, calls=%fused_computation.22 | loop fusion | flops 262144 | bytes 524288 | tf_op jit(solution)/shard_map/add | solution.py:243
  (45 shorter events, 2.7 us)
Async XLA Ops:
  0.6 18.7 %copy-start.2 = (f32[384]{0:T(512)S(1)}, f32[384]{0:T(512)}, u32[]{:S(2)}) copy-start(f32[384]{0:T(512)} %param.9) | copy-start | bytes 4612
  0.7 18.7 %copy-start = (s32[3,4]{1,0:T(4,128)S(1)}, s32[3,4]{1,0:T(4,128)}, u32[]{:S(2)}) copy-start(s32[3,4]{1,0:T(4,128)} %mask_ref.1) | copy-start | bytes 148
  0.7 8.5 %collective-permute-start = (bf16[32,1024]{1,0:T(8,128)(2,1)}, bf16[32,1024]{1,0:T(8,128)(2,1)S(1)}, u32[]{:S(2)}, u32[]{:S(2)}) collective-permute-start(bf16[32,1024]{1,0:T(8,128)(2,1)} %param.6), channel_id=1, source_target_pairs={{0,8},{1,9},{2,10},{3,11},{4,12},{5,13},{6,14},{7,15},{8,16},{9,17... | collective-permute-start | bytes 196616 | tf_op jit(solution)/shard_map/ppermute | solution.py:21
  3.7 8.2 %collective-permute-start.6 = (bf16[32,1024]{1,0:T(8,128)(2,1)}, bf16[32,1024]{1,0:T(8,128)(2,1)S(1)}, u32[]{:S(2)}, u32[]{:S(2)}) collective-permute-start(bf16[32,1024]{1,0:T(8,128)(2,1)} %param.6), channel_id=1, source_target_pairs={{0,4},{1,5},{2,6},{3,7},{4,16},{5,17},{6,18},{7,19},{8,12},{9,13},... | collective-permute-start | bytes 196616 | tf_op jit(solution)/shard_map/ppermute | solution.py:21
  5.3 8.8 %collective-permute-start.4 = (bf16[32,1024]{1,0:T(8,128)(2,1)}, bf16[32,1024]{1,0:T(8,128)(2,1)S(1)}, u32[]{:S(2)}, u32[]{:S(2)}) collective-permute-start(bf16[32,1024]{1,0:T(8,128)(2,1)} %param.6), channel_id=1, source_target_pairs={{0,10},{1,11},{2,8},{3,9},{4,14},{5,15},{6,12},{7,13},{8,18},{9,19... | collective-permute-start | bytes 196616 | tf_op jit(solution)/shard_map/ppermute | solution.py:21
  9.1 9.5 %collective-permute-start.1 = (bf16[32,1024]{1,0:T(8,128)(2,1)S(1)}, bf16[32,1024]{1,0:T(8,128)(2,1)S(1)}, u32[]{:S(2)}, u32[]{:S(2)}) collective-permute-start(bf16[32,1024]{1,0:T(8,128)(2,1)S(1)} %collective-permute-done), channel_id=1, source_target_pairs={{0,4},{1,5},{2,6},{3,7},{4,0},{5,1},{6,2},{7,3},{8,12},{9,13},{10,... | collective-permute-start | bytes 196616 | tf_op jit(solution)/shard_map/ppermute | solution.py:21
  10.4 8.3 %collective-permute-start.2 = (bf16[32,1024]{1,0:T(8,128)(2,1)S(1)}, bf16[32,1024]{1,0:T(8,128)(2,1)S(1)}, u32[]{:S(2)}, u32[]{:S(2)}) collective-permute-start(bf16[32,1024]{1,0:T(8,128)(2,1)S(1)} %copy-done.1), channel_id=1, source_target_pairs={{0,2},{1,3},{2,0},{3,1},{4,6},{5,7},{6,4},{7,5},{8,10},{9,11},{10,... | collective-permute-start | bytes 196616 | tf_op jit(solution)/shard_map/ppermute | solution.py:21
  11.9 4.4 %collective-permute-start.7 = (bf16[32,1024]{1,0:T(8,128)(2,1)S(1)}, bf16[32,1024]{1,0:T(8,128)(2,1)S(1)}, u32[]{:S(2)}, u32[]{:S(2)}) collective-permute-start(bf16[32,1024]{1,0:T(8,128)(2,1)S(1)} %collective-permute-done.6), channel_id=1, source_target_pairs={{0,2},{1,3},{2,0},{3,1},{4,6},{5,7},{6,4},{7,5},{8,10},{9,11},{10,... | collective-permute-start | bytes 196616 | tf_op jit(solution)/shard_map/ppermute | solution.py:21
  14.1 5.8 %collective-permute-start.5 = (bf16[2,32,1024]{2,1,0:T(8,128)(2,1)S(1)}, bf16[2,32,1024]{2,1,0:T(8,128)(2,1)S(1)}, u32[]{:S(2)}, u32[]{:S(2)}) collective-permute-start(bf16[2,32,1024]{2,1,0:T(8,128)(2,1)S(1)} %pad_maximum_fusion.1.refs_2_), channel_id=1, source_target_pairs={{0,1},{1,0},{2,3},{3,2},{4,5},{5,4},{6,7},{7,6},{8,9},{9,8},{10,11... | collective-permute-start | bytes 393224 | tf_op jit(solution)/shard_map/ppermute | solution.py:21
  14.2 4.5 %collective-permute-start.9 = (bf16[32,1024]{1,0:T(8,128)(2,1)S(1)}, bf16[32,1024]{1,0:T(8,128)(2,1)S(1)}, u32[]{:S(2)}, u32[]{:S(2)}) collective-permute-start(bf16[32,1024]{1,0:T(8,128)(2,1)S(1)} %collective-permute-done.4), channel_id=1, source_target_pairs={{0,4},{1,5},{2,6},{3,7},{4,0},{5,1},{6,2},{7,3},{8,12},{9,13},{10,... | collective-permute-start | bytes 196616 | tf_op jit(solution)/shard_map/ppermute | solution.py:21
  16.3 3.6 %collective-permute-start.8 = (bf16[2,32,1024]{2,1,0:T(8,128)(2,1)S(1)}, bf16[2,32,1024]{2,1,0:T(8,128)(2,1)S(1)}, u32[]{:S(2)}, u32[]{:S(2)}) collective-permute-start(bf16[2,32,1024]{2,1,0:T(8,128)(2,1)S(1)} %pad_maximum_fusion.2.refs_4_), channel_id=1, source_target_pairs={{0,1},{1,0},{2,3},{3,2},{4,5},{5,4},{6,7},{7,6},{8,9},{9,8},{10,11... | collective-permute-start | bytes 393224 | tf_op jit(solution)/shard_map/ppermute | solution.py:21
  18.7 1.4 %collective-permute-start.10 = (bf16[2,32,1024]{2,1,0:T(8,128)(2,1)S(1)}, bf16[2,32,1024]{2,1,0:T(8,128)(2,1)S(1)}, u32[]{:S(2)}, u32[]{:S(2)}) collective-permute-start(bf16[2,32,1024]{2,1,0:T(8,128)(2,1)S(1)} %pad_maximum_fusion.3.refs_6_), channel_id=1, source_target_pairs={{0,1},{1,0},{2,3},{3,2},{4,5},{5,4},{6,7},{7,6},{8,9},{9,8},{10,11... | collective-permute-start | bytes 393224 | tf_op jit(solution)/shard_map/ppermute | solution.py:21
  18.8 1.5 %collective-permute-start.3 = (bf16[2,32,1024]{2,1,0:T(8,128)(2,1)S(1)}, bf16[2,32,1024]{2,1,0:T(8,128)(2,1)S(1)}, u32[]{:S(2)}, u32[]{:S(2)}) collective-permute-start(bf16[2,32,1024]{2,1,0:T(8,128)(2,1)S(1)} %pad_maximum_fusion.refs_0_), channel_id=1, source_target_pairs={{0,1},{1,0},{2,3},{3,2},{4,5},{5,4},{6,7},{7,6},{8,9},{9,8},{10,11... | collective-permute-start | bytes 393224 | tf_op jit(solution)/shard_map/ppermute | solution.py:21
  22.2 1.4 %collective-permute-start.13 = (bf16[2,32,1024]{2,1,0:T(8,128)(2,1)S(1)}, bf16[2,32,1024]{2,1,0:T(8,128)(2,1)S(1)}, u32[]{:S(2)}, u32[]{:S(2)}) collective-permute-start(bf16[2,32,1024]{2,1,0:T(8,128)(2,1)S(1)} %get-tuple-element.25), channel_id=1, source_target_pairs={{0,1},{1,0},{2,3},{3,2},{4,5},{5,4},{6,7},{7,6},{8,9},{9,8},{10,11... | collective-permute-start | bytes 393224 | tf_op jit(solution)/shard_map/ppermute | solution.py:21
  22.6 1.3 %collective-permute-start.14 = (bf16[2,32,1024]{2,1,0:T(8,128)(2,1)S(1)}, bf16[2,32,1024]{2,1,0:T(8,128)(2,1)S(1)}, u32[]{:S(2)}, u32[]{:S(2)}) collective-permute-start(bf16[2,32,1024]{2,1,0:T(8,128)(2,1)S(1)} %get-tuple-element.24), channel_id=1, source_target_pairs={{0,1},{1,0},{2,3},{3,2},{4,5},{5,4},{6,7},{7,6},{8,9},{9,8},{10,11... | collective-permute-start | bytes 393224 | tf_op jit(solution)/shard_map/ppermute | solution.py:21
  22.7 4.2 %collective-permute-start.12 = (bf16[2,32,1024]{2,1,0:T(8,128)(2,1)S(1)}, bf16[2,32,1024]{2,1,0:T(8,128)(2,1)S(1)}, u32[]{:S(2)}, u32[]{:S(2)}) collective-permute-start(bf16[2,32,1024]{2,1,0:T(8,128)(2,1)S(1)} %get-tuple-element.26), channel_id=1, source_target_pairs={{0,1},{1,0},{2,3},{3,2},{4,5},{5,4},{6,7},{7,6},{8,9},{9,8},{10,11... | collective-permute-start | bytes 393224 | tf_op jit(solution)/shard_map/ppermute | solution.py:21
  23.1 3.9 %collective-permute-start.11 = (bf16[2,32,1024]{2,1,0:T(8,128)(2,1)S(1)}, bf16[2,32,1024]{2,1,0:T(8,128)(2,1)S(1)}, u32[]{:S(2)}, u32[]{:S(2)}) collective-permute-start(bf16[2,32,1024]{2,1,0:T(8,128)(2,1)S(1)} %get-tuple-element.27), channel_id=1, source_target_pairs={{0,1},{1,0},{2,3},{3,2},{4,5},{5,4},{6,7},{7,6},{8,9},{9,8},{10,11... | collective-permute-start | bytes 393224 | tf_op jit(solution)/shard_map/ppermute | solution.py:21
  24.0 4.4 %collective-permute-start.15 = (bf16[32,1024]{1,0:T(8,128)(2,1)S(1)}, bf16[32,1024]{1,0:T(8,128)(2,1)S(1)}, u32[]{:S(2)}, u32[]{:S(2)}) collective-permute-start(bf16[32,1024]{1,0:T(8,128)(2,1)S(1)} %fusion.12), channel_id=1, source_target_pairs={{0,2},{1,3},{2,0},{3,1},{4,6},{5,7},{6,4},{7,5},{8,10},{9,11},{10,... | collective-permute-start | bytes 196616 | tf_op jit(solution)/shard_map/ppermute | solution.py:21
  24.8 4.9 %collective-permute-start.17 = (bf16[32,1024]{1,0:T(8,128)(2,1)S(1)}, bf16[32,1024]{1,0:T(8,128)(2,1)S(1)}, u32[]{:S(2)}, u32[]{:S(2)}) collective-permute-start(bf16[32,1024]{1,0:T(8,128)(2,1)S(1)} %get-tuple-element.30), channel_id=1, source_target_pairs={{0,4},{1,5},{2,6},{3,7},{4,0},{5,1},{6,2},{7,3},{8,12},{9,13},{10,... | collective-permute-start | bytes 196616 | tf_op jit(solution)/shard_map/ppermute | solution.py:21
  26.7 4.9 %collective-permute-start.19 = (bf16[32,1024]{1,0:T(8,128)(2,1)S(1)}, bf16[32,1024]{1,0:T(8,128)(2,1)S(1)}, u32[]{:S(2)}, u32[]{:S(2)}) collective-permute-start(bf16[32,1024]{1,0:T(8,128)(2,1)S(1)} %get-tuple-element.31), channel_id=1, source_target_pairs={{0,4},{1,5},{2,6},{3,7},{4,0},{5,1},{6,2},{7,3},{8,12},{9,13},{10,... | collective-permute-start | bytes 196616 | tf_op jit(solution)/shard_map/ppermute | solution.py:21
  27.0 8.8 %collective-permute-start.21 = (bf16[32,1024]{1,0:T(8,128)(2,1)S(1)}, bf16[32,1024]{1,0:T(8,128)(2,1)S(1)}, u32[]{:S(2)}, u32[]{:S(2)}) collective-permute-start(bf16[32,1024]{1,0:T(8,128)(2,1)S(1)} %fusion.13), channel_id=1, source_target_pairs={{0,2},{1,3},{2,0},{3,1},{4,6},{5,7},{6,4},{7,5},{8,10},{9,11},{10,... | collective-permute-start | bytes 196616 | tf_op jit(solution)/shard_map/ppermute | solution.py:21
  28.4 7.4 %collective-permute-start.16 = (bf16[32,1024]{1,0:T(8,128)(2,1)S(1)}, bf16[32,1024]{1,0:T(8,128)(2,1)S(1)}, u32[]{:S(2)}, u32[]{:S(2)}) collective-permute-start(bf16[32,1024]{1,0:T(8,128)(2,1)S(1)} %fusion.7), channel_id=1, source_target_pairs={{0,20},{1,21},{2,22},{3,23},{4,0},{5,1},{6,2},{7,3},{8,28},{9,29},... | collective-permute-start | bytes 196616 | tf_op jit(solution)/shard_map/ppermute | solution.py:21
  31.6 4.3 %collective-permute-start.18 = (bf16[32,1024]{1,0:T(8,128)(2,1)S(1)}, bf16[32,1024]{1,0:T(8,128)(2,1)S(1)}, u32[]{:S(2)}, u32[]{:S(2)}) collective-permute-start(bf16[32,1024]{1,0:T(8,128)(2,1)S(1)} %get-tuple-element.28), channel_id=1, source_target_pairs={{0,24},{1,25},{2,26},{3,27},{4,28},{5,29},{6,30},{7,31},{8,0},{9,1... | collective-permute-start | bytes 196616 | tf_op jit(solution)/shard_map/ppermute | solution.py:21
  32.1 5.2 %collective-permute-start.20 = (bf16[32,1024]{1,0:T(8,128)(2,1)S(1)}, bf16[32,1024]{1,0:T(8,128)(2,1)S(1)}, u32[]{:S(2)}, u32[]{:S(2)}) collective-permute-start(bf16[32,1024]{1,0:T(8,128)(2,1)S(1)} %get-tuple-element.29), channel_id=1, source_target_pairs={{0,26},{1,27},{2,24},{3,25},{4,30},{5,31},{6,28},{7,29},{8,2},{9,3... | collective-permute-start | bytes 196616 | tf_op jit(solution)/shard_map/ppermute | solution.py:21
  (1 other events, 9.8 us)

commit v4 on v3

--- a/solution.py
+++ b/solution.py
@@ -61,15 +61,17 @@
             target_ref[number * own_rows : (number + 1) * own_rows, rows] = flat_ref[pl.ds(col, own_rows), :]
 
 
-def grads_kernel(score_scale, packed_ref, target_ref, weights_ref, *refs):
+def grads_kernel(score_scale, places, packed_ref, target_ref, weights_ref, *refs):
     grads_ref, window_ref, send_ref, keep_ref, scores_ref = refs[-5:]
     pieces = refs[:-5]
-    halves, own_rows, width = pieces[0].shape
+    own_rows, width = pieces[0].shape[1:]
     count_rows = grads_ref.shape[1]
     lanes = 128 if count_rows % 128 == 0 else count_rows
-    for number in range(len(pieces) * halves):
+    slots, halves = send_ref.shape[:2]
+    for number in range(slots * 2 * halves):
         slot, offset = divmod(number, 2 * halves)
-        window_ref[number * own_rows : (number + 1) * own_rows, :] = pieces[2 * slot + offset % 2][offset // 2]
+        index, place = places[slot]
+        window_ref[number * own_rows : (number + 1) * own_rows, :] = pieces[index + offset % 2][place + offset // 2]
     scores_ref[...] = score_scale * lax.dot_general(
         window_ref[...],
         packed_ref[:count_rows, :width],
@@ -82,7 +84,6 @@
         (student,) = softmax_cols([jnp.where(target >= 0, scores_ref[:, rows], very_negative)])
         factor = weights_ref[:, rows] * score_scale
         grads_ref[:, rows] = (factor * (student - jnp.maximum(target, 0.0))).astype(jnp.bfloat16)
-    slots = send_ref.shape[0]
     panel = 2 * halves * own_rows
     for slot in reversed(range(slots)):
         term = jnp.dot(
@@ -179,13 +180,16 @@
     near_groups = after(groups, seconds[0])
     firsts = [near_groups] + [moved_to(near_groups, own(offset)) for offset in evens[1:]]
     thirds = [third] + [moved_to(third, own(offset)) for offset in evens[1:]]
-    pieces = []
-    for blocks in (firsts, seconds, thirds, fourths):
-        block = jnp.stack(blocks)
+    blocks = (firsts, seconds, thirds, fourths)
+    pieces, places = [], {}
+    for together in ((0, 1), (2, 3)):
+        block = jnp.stack([part for slot in together for part in blocks[slot]])
+        for place, slot in enumerate(together):
+            places[slot] = (len(pieces), place * len(evens))
         pieces += [block, moved_to(block, own(1))]
 
     grads, gathered, send, keep = pl.pallas_call(
-        functools.partial(grads_kernel, score_scale),
+        functools.partial(grads_kernel, score_scale, places),
         out_shape=(
             jax.ShapeDtypeStruct((window, count_rows), jnp.bfloat16),
             jax.ShapeDtypeStruct((window, width), jnp.bfloat16),

time: 38.1 us -> 37.7 us (0.990)
  starting transfers between devices: 23.2 us -> 22.8 us
    ppermute x22 -> x20, starting transfers between devices: 23.2 us -> 22.8 us  [moved_to(): return lax.ppermute(block, ('pb', 'col'), pairs)]
    ppermute x22 -> x20, waiting for transfers between devices: 7.81 us -> 7.76 us  [moved_to(): return lax.ppermute(block, ('pb', 'col'), pairs)]
  transfers between devices with their start and end apart: 22 -> 20, of which waited for: 9 -> 8; matrix products, arithmetic and copies ran while one was open for 4% -> 4% of each run, Pallas kernels for 5% -> 5%
where the time goes in v4:
time: 37.7 us; the launch traced here: 37.6 us
  starting transfers between devices  22.8 us (60%)
  waiting for transfers between devices  7.76 us (21%)
  Pallas kernels  3.75 us (10%)
  other arithmetic  2.32 us (6%)
  between operations  0.84 us (2%)
    ppermute x20, starting transfers between devices, moved_to(): return lax.ppermute(block, ('pb', 'col'), pairs)  22.8 us
    ppermute x20, waiting for transfers between devices, moved_to(): return lax.ppermute(block, ('pb', 'col'), pairs)  7.76 us
    pallas_call x1, Pallas kernels, on_device(): pl.pallas_call(functools.partial(grads_kernel, score_scale, places), out_...  1.76 us
    pallas_call x1, Pallas kernels, on_device(): pl.pallas_call(query_grad_kernel, out_shape=jax.ShapeDtypeStruct((count_r...  1.5 us
    concatenate x1, other arithmetic, on_device(): jnp.concatenate([jnp.concatenate([queries, teacher], axis=1), jnp.pad(gro...  1.37 us
  transfers between devices with their start and end apart: 20, of which 8 were waited for; matrix products, arithmetic and copies ran while one was open for 4% of the time, Pallas kernels for 5%

profile of v4, /device:TPU:0, one launch (start us, length us, event | category | flops | bytes accessed | tf_op | source)
XLA Modules:
  0.0 37.6 jit_solution(15207066512184151152)
XLA Ops:
  0.7 3.1 %collective-permute-start = (bf16[32,1024]{1,0:T(8,128)(2,1)}, bf16[32,1024]{1,0:T(8,128)(2,1)S(1)}, u32[]{:S(2)}, u32[]{:S(2)}) collective-permute-start(bf16[32,1024]{1,0:T(8,128)(2,1)} %param.6), channel_id=1, source_target_pairs={{0,8},{1,9},{2,10},{3,11},{4,12},{5,13},{6,14},{7,15},{8,16},{9,17... | collective-permute-start | bytes 196616 | tf_op jit(solution)/shard_map/ppermute | solution.py:21
  3.7 1.5 %collective-permute-start.5 = (bf16[32,1024]{1,0:T(8,128)(2,1)}, bf16[32,1024]{1,0:T(8,128)(2,1)S(1)}, u32[]{:S(2)}, u32[]{:S(2)}) collective-permute-start(bf16[32,1024]{1,0:T(8,128)(2,1)} %param.6), channel_id=1, source_target_pairs={{0,4},{1,5},{2,6},{3,7},{4,16},{5,17},{6,18},{7,19},{8,12},{9,13},... | collective-permute-start | bytes 196616 | tf_op jit(solution)/shard_map/ppermute | solution.py:21
  5.3 2.5 %collective-permute-start.3 = (bf16[32,1024]{1,0:T(8,128)(2,1)}, bf16[32,1024]{1,0:T(8,128)(2,1)S(1)}, u32[]{:S(2)}, u32[]{:S(2)}) collective-permute-start(bf16[32,1024]{1,0:T(8,128)(2,1)} %param.6), channel_id=1, source_target_pairs={{0,10},{1,11},{2,8},{3,9},{4,14},{5,15},{6,12},{7,13},{8,18},{9,19... | collective-permute-start | bytes 196616 | tf_op jit(solution)/shard_map/ppermute | solution.py:21
  7.8 1.4 %fusion.1.packed_ref = bf16[416,1536]{1,0:T(8,128)(2,1)S(1)} fusion(bf16[32,1024]{1,0:T(8,128)(2,1)} %param.6, bf16[384,512]{1,0:T(8,128)(2,1)} %param.7, bf16[384,1024]{1,0:T(8,128)(2,1)} %param.5), kind=kLoop, calls=%fused_computation.2 | loop fusion | flops 5111808 | bytes 2523136 | tf_op jit(solution)/shard_map/concatenate | solution.py:157
  9.2 0.8 %collective-permute-start.2 = (bf16[32,1024]{1,0:T(8,128)(2,1)S(1)}, bf16[32,1024]{1,0:T(8,128)(2,1)S(1)}, u32[]{:S(2)}, u32[]{:S(2)}) collective-permute-start(bf16[32,1024]{1,0:T(8,128)(2,1)S(1)} %copy-done.1), channel_id=1, source_target_pairs={{0,2},{1,3},{2,0},{3,1},{4,6},{5,7},{6,4},{7,5},{8,10},{9,11},{10,... | collective-permute-start | bytes 196616 | tf_op jit(solution)/shard_map/ppermute | solution.py:21
  9.9 2.0 %collective-permute-start.1 = (bf16[32,1024]{1,0:T(8,128)(2,1)S(1)}, bf16[32,1024]{1,0:T(8,128)(2,1)S(1)}, u32[]{:S(2)}, u32[]{:S(2)}) collective-permute-start(bf16[32,1024]{1,0:T(8,128)(2,1)S(1)} %collective-permute-done), channel_id=1, source_target_pairs={{0,4},{1,5},{2,6},{3,7},{4,0},{5,1},{6,2},{7,3},{8,12},{9,13},{10,... | collective-permute-start | bytes 196616 | tf_op jit(solution)/shard_map/ppermute | solution.py:21
  11.9 2.1 %collective-permute-start.6 = (bf16[32,1024]{1,0:T(8,128)(2,1)S(1)}, bf16[32,1024]{1,0:T(8,128)(2,1)S(1)}, u32[]{:S(2)}, u32[]{:S(2)}) collective-permute-start(bf16[32,1024]{1,0:T(8,128)(2,1)S(1)} %collective-permute-done.5), channel_id=1, source_target_pairs={{0,2},{1,3},{2,0},{3,1},{4,6},{5,7},{6,4},{7,5},{8,10},{9,11},{10,... | collective-permute-start | bytes 196616 | tf_op jit(solution)/shard_map/ppermute | solution.py:21
  14.0 1.0 %collective-permute-start.7 = (bf16[32,1024]{1,0:T(8,128)(2,1)S(1)}, bf16[32,1024]{1,0:T(8,128)(2,1)S(1)}, u32[]{:S(2)}, u32[]{:S(2)}) collective-permute-start(bf16[32,1024]{1,0:T(8,128)(2,1)S(1)} %collective-permute-done.3), channel_id=1, source_target_pairs={{0,4},{1,5},{2,6},{3,7},{4,0},{5,1},{6,2},{7,3},{8,12},{9,13},{10,... | collective-permute-start | bytes 196616 | tf_op jit(solution)/shard_map/ppermute | solution.py:21
  15.2 1.1 %collective-permute-done.6 = bf16[32,1024]{1,0:T(8,128)(2,1)S(1)} collective-permute-done((bf16[32,1024]{1,0:T(8,128)(2,1)S(1)}, bf16[32,1024]{1,0:T(8,128)(2,1)S(1)}, u32[]{:S(2)}, u32[]{:S(2)}) %collective-permute-start.6) | collective-permute-done | bytes 65568 | tf_op jit(solution)/shard_map/ppermute | solution.py:21
  16.3 2.0 %collective-permute-done.7 = bf16[32,1024]{1,0:T(8,128)(2,1)S(1)} collective-permute-done((bf16[32,1024]{1,0:T(8,128)(2,1)S(1)}, bf16[32,1024]{1,0:T(8,128)(2,1)S(1)}, u32[]{:S(2)}, u32[]{:S(2)}) %collective-permute-start.7) | collective-permute-done | bytes 65568 | tf_op jit(solution)/shard_map/ppermute | solution.py:21
  18.4 0.5 %shard_map.68.target_ref = f32[512,384]{1,0:T(8,128)S(1)} custom-call(s32[3,4]{1,0:T(4,128)S(1)} %copy-done, bf16[416,1536]{1,0:T(8,128)(2,1)S(1)} %fusion.1.packed_ref), custom_call_target="tpu_custom_call" | custom-call | flops 1572864 | bytes 1179648 | tf_op jit(solution)/shard_map/pallas_call | solution.py:167
  19.0 1.0 %collective-permute-done.8.refs_3_ = bf16[4,32,1024]{2,1,0:T(8,128)(2,1)S(1)} collective-permute-done((bf16[4,32,1024]{2,1,0:T(8,128)(2,1)S(1)}, bf16[4,32,1024]{2,1,0:T(8,128)(2,1)S(1)}, u32[]{:S(2)}, u32[]{:S(2)}) %collective-permute-start.8) | collective-permute-done | bytes 262176 | tf_op jit(solution)/shard_map/ppermute | solution.py:21
  19.9 1.8 %shard_map.69 = (bf16[512,384]{1,0:T(8,128)(2,1)S(1)}, bf16[512,1024]{1,0:T(8,128)(2,1)S(1)}, bf16[4,2,32,1024]{3,2,1,0:T(8,128)(2,1)S(1)}, bf16[4,2,32,1024]{3,2,1,0:T(8,128)(2,1)S(1)}) custom-call(bf16[416,1536]{1,0:T(8,128)(2,1)S(1)} %fusion.1.packed_ref, f32[512,384]{1,0:T(8,128)S(1)} %shard_map.68.target_ref, f32[1,384]{1,0:T(1,128)S(1)} %broadcast_in_dim.3.weights_ref, ...), custom_call_target="tpu_custom_call" | custom-call | flops 805306368 | bytes 4063232 | tf_op jit(solution)/shard_map/pallas_call | solution.py:191
  22.5 0.4 %collective-permute-start.9 = (bf16[2,32,1024]{2,1,0:T(8,128)(2,1)S(1)}, bf16[2,32,1024]{2,1,0:T(8,128)(2,1)S(1)}, u32[]{:S(2)}, u32[]{:S(2)}) collective-permute-start(bf16[2,32,1024]{2,1,0:T(8,128)(2,1)S(1)} %get-tuple-element.27), channel_id=1, source_target_pairs={{0,1},{1,0},{2,3},{3,2},{4,5},{5,4},{6,7},{7,6},{8,9},{9,8},{10,11... | collective-permute-start | bytes 393224 | tf_op jit(solution)/shard_map/ppermute | solution.py:21
  23.4 0.6 %collective-permute-start.13 = (bf16[32,1024]{1,0:T(8,128)(2,1)S(1)}, bf16[32,1024]{1,0:T(8,128)(2,1)S(1)}, u32[]{:S(2)}, u32[]{:S(2)}) collective-permute-start(bf16[32,1024]{1,0:T(8,128)(2,1)S(1)} %fusion.12), channel_id=1, source_target_pairs={{0,2},{1,3},{2,0},{3,1},{4,6},{5,7},{6,4},{7,5},{8,10},{9,11},{10,... | collective-permute-start | bytes 196616 | tf_op jit(solution)/shard_map/ppermute | solution.py:21
  24.0 2.1 %collective-permute-start.15 = (bf16[32,1024]{1,0:T(8,128)(2,1)S(1)}, bf16[32,1024]{1,0:T(8,128)(2,1)S(1)}, u32[]{:S(2)}, u32[]{:S(2)}) collective-permute-start(bf16[32,1024]{1,0:T(8,128)(2,1)S(1)} %get-tuple-element.30), channel_id=1, source_target_pairs={{0,4},{1,5},{2,6},{3,7},{4,0},{5,1},{6,2},{7,3},{8,12},{9,13},{10,... | collective-permute-start | bytes 196616 | tf_op jit(solution)/shard_map/ppermute | solution.py:21
  26.3 1.5 %collective-permute-start.19 = (bf16[32,1024]{1,0:T(8,128)(2,1)S(1)}, bf16[32,1024]{1,0:T(8,128)(2,1)S(1)}, u32[]{:S(2)}, u32[]{:S(2)}) collective-permute-start(bf16[32,1024]{1,0:T(8,128)(2,1)S(1)} %fusion.13), channel_id=1, source_target_pairs={{0,2},{1,3},{2,0},{3,1},{4,6},{5,7},{6,4},{7,5},{8,10},{9,11},{10,... | collective-permute-start | bytes 196616 | tf_op jit(solution)/shard_map/ppermute | solution.py:21
  27.8 1.3 %collective-permute-start.14 = (bf16[32,1024]{1,0:T(8,128)(2,1)S(1)}, bf16[32,1024]{1,0:T(8,128)(2,1)S(1)}, u32[]{:S(2)}, u32[]{:S(2)}) collective-permute-start(bf16[32,1024]{1,0:T(8,128)(2,1)S(1)} %fusion.7), channel_id=1, source_target_pairs={{0,20},{1,21},{2,22},{3,23},{4,0},{5,1},{6,2},{7,3},{8,28},{9,29},... | collective-permute-start | bytes 196616 | tf_op jit(solution)/shard_map/ppermute | solution.py:21
  29.2 1.6 %collective-permute-done.17 = bf16[32,1024]{1,0:T(8,128)(2,1)S(1)} collective-permute-done((bf16[32,1024]{1,0:T(8,128)(2,1)S(1)}, bf16[32,1024]{1,0:T(8,128)(2,1)S(1)}, u32[]{:S(2)}, u32[]{:S(2)}) %collective-permute-start.17) | collective-permute-done | bytes 65568 | tf_op jit(solution)/shard_map/ppermute | solution.py:21
  30.8 0.9 %collective-permute-start.16 = (bf16[32,1024]{1,0:T(8,128)(2,1)S(1)}, bf16[32,1024]{1,0:T(8,128)(2,1)S(1)}, u32[]{:S(2)}, u32[]{:S(2)}) collective-permute-start(bf16[32,1024]{1,0:T(8,128)(2,1)S(1)} %get-tuple-element.28), channel_id=1, source_target_pairs={{0,24},{1,25},{2,26},{3,27},{4,28},{5,29},{6,30},{7,31},{8,0},{9,1... | collective-permute-start | bytes 196616 | tf_op jit(solution)/shard_map/ppermute | solution.py:21
  31.7 2.1 %collective-permute-start.18 = (bf16[32,1024]{1,0:T(8,128)(2,1)S(1)}, bf16[32,1024]{1,0:T(8,128)(2,1)S(1)}, u32[]{:S(2)}, u32[]{:S(2)}) collective-permute-start(bf16[32,1024]{1,0:T(8,128)(2,1)S(1)} %get-tuple-element.29), channel_id=1, source_target_pairs={{0,26},{1,27},{2,24},{3,25},{4,30},{5,31},{6,28},{7,29},{8,2},{9,3... | collective-permute-start | bytes 196616 | tf_op jit(solution)/shard_map/ppermute | solution.py:21
  33.8 1.5 %shard_map.70 = f32[384,1024]{1,0:T(8,128)} custom-call(bf16[512,384]{1,0:T(8,128)(2,1)S(1)} %get-tuple-element.15.grads_ref, bf16[512,1024]{1,0:T(8,128)(2,1)S(1)} %get-tuple-element.16.window_ref), custom_call_target="tpu_custom_call" | custom-call | flops 402653184 | bytes 3014656 | tf_op jit(solution)/shard_map/pallas_call | solution.py:211
  35.6 1.2 %collective-permute-done.18 = bf16[32,1024]{1,0:T(8,128)(2,1)S(1)} collective-permute-done((bf16[32,1024]{1,0:T(8,128)(2,1)S(1)}, bf16[32,1024]{1,0:T(8,128)(2,1)S(1)}, u32[]{:S(2)}, u32[]{:S(2)}) %collective-permute-start.18) | collective-permute-done | bytes 65568 | tf_op jit(solution)/shard_map/ppermute | solution.py:21
  36.9 0.7 %fusion.11 = f32[32,1024]{1,0:T(8,128)} fusion(f32[2,32,1024]{2,1,0:T(8,128)S(1)} %convert_add_fusion.3, bf16[32,1024]{1,0:T(8,128)(2,1)S(1)} %collective-permute-done.19, bf16[32,1024]{1,0:T(8,128)(2,1)S(1)} %collective-permute-done.18, bf16[32,1024]{1,0:T(8,128)(2,1)S(1)} %collective-permute-done.16, bf16[32,1024]{1,0:T(8,128)(2,1)S(1)} %collective-permute-done.14), kind=kLoop, calls=%fused_computation.24 | loop fusion | flops 262144 | bytes 524288 | tf_op jit(solution)/shard_map/add | solution.py:247
  (39 shorter events, 2.1 us)
Async XLA Ops:
  0.6 8.5 %copy-start.1 = (bf16[32,1024]{1,0:T(8,128)(2,1)S(1)}, bf16[32,1024]{1,0:T(8,128)(2,1)}, u32[]{:S(2)}) copy-start(bf16[32,1024]{1,0:T(8,128)(2,1)} %param.6) | copy-start | bytes 196612
  0.6 17.8 %copy-start.2 = (f32[384]{0:T(512)S(1)}, f32[384]{0:T(512)}, u32[]{:S(2)}) copy-start(f32[384]{0:T(512)} %param.9) | copy-start | bytes 4612
  0.7 17.8 %copy-start = (s32[3,4]{1,0:T(4,128)S(1)}, s32[3,4]{1,0:T(4,128)}, u32[]{:S(2)}) copy-start(s32[3,4]{1,0:T(4,128)} %mask_ref.1) | copy-start | bytes 148
  0.7 8.5 %collective-permute-start = (bf16[32,1024]{1,0:T(8,128)(2,1)}, bf16[32,1024]{1,0:T(8,128)(2,1)S(1)}, u32[]{:S(2)}, u32[]{:S(2)}) collective-permute-start(bf16[32,1024]{1,0:T(8,128)(2,1)} %param.6), channel_id=1, source_target_pairs={{0,8},{1,9},{2,10},{3,11},{4,12},{5,13},{6,14},{7,15},{8,16},{9,17... | collective-permute-start | bytes 196616 | tf_op jit(solution)/shard_map/ppermute | solution.py:21
  3.7 8.2 %collective-permute-start.5 = (bf16[32,1024]{1,0:T(8,128)(2,1)}, bf16[32,1024]{1,0:T(8,128)(2,1)S(1)}, u32[]{:S(2)}, u32[]{:S(2)}) collective-permute-start(bf16[32,1024]{1,0:T(8,128)(2,1)} %param.6), channel_id=1, source_target_pairs={{0,4},{1,5},{2,6},{3,7},{4,16},{5,17},{6,18},{7,19},{8,12},{9,13},... | collective-permute-start | bytes 196616 | tf_op jit(solution)/shard_map/ppermute | solution.py:21
  5.3 8.8 %collective-permute-start.3 = (bf16[32,1024]{1,0:T(8,128)(2,1)}, bf16[32,1024]{1,0:T(8,128)(2,1)S(1)}, u32[]{:S(2)}, u32[]{:S(2)}) collective-permute-start(bf16[32,1024]{1,0:T(8,128)(2,1)} %param.6), channel_id=1, source_target_pairs={{0,10},{1,11},{2,8},{3,9},{4,14},{5,15},{6,12},{7,13},{8,18},{9,19... | collective-permute-start | bytes 196616 | tf_op jit(solution)/shard_map/ppermute | solution.py:21
  9.2 5.9 %collective-permute-start.2 = (bf16[32,1024]{1,0:T(8,128)(2,1)S(1)}, bf16[32,1024]{1,0:T(8,128)(2,1)S(1)}, u32[]{:S(2)}, u32[]{:S(2)}) collective-permute-start(bf16[32,1024]{1,0:T(8,128)(2,1)S(1)} %copy-done.1), channel_id=1, source_target_pairs={{0,2},{1,3},{2,0},{3,1},{4,6},{5,7},{6,4},{7,5},{8,10},{9,11},{10,... | collective-permute-start | bytes 196616 | tf_op jit(solution)/shard_map/ppermute | solution.py:21
  9.9 8.4 %collective-permute-start.1 = (bf16[32,1024]{1,0:T(8,128)(2,1)S(1)}, bf16[32,1024]{1,0:T(8,128)(2,1)S(1)}, u32[]{:S(2)}, u32[]{:S(2)}) collective-permute-start(bf16[32,1024]{1,0:T(8,128)(2,1)S(1)} %collective-permute-done), channel_id=1, source_target_pairs={{0,4},{1,5},{2,6},{3,7},{4,0},{5,1},{6,2},{7,3},{8,12},{9,13},{10,... | collective-permute-start | bytes 196616 | tf_op jit(solution)/shard_map/ppermute | solution.py:21
  11.9 4.3 %collective-permute-start.6 = (bf16[32,1024]{1,0:T(8,128)(2,1)S(1)}, bf16[32,1024]{1,0:T(8,128)(2,1)S(1)}, u32[]{:S(2)}, u32[]{:S(2)}) collective-permute-start(bf16[32,1024]{1,0:T(8,128)(2,1)S(1)} %collective-permute-done.5), channel_id=1, source_target_pairs={{0,2},{1,3},{2,0},{3,1},{4,6},{5,7},{6,4},{7,5},{8,10},{9,11},{10,... | collective-permute-start | bytes 196616 | tf_op jit(solution)/shard_map/ppermute | solution.py:21
  14.0 4.3 %collective-permute-start.7 = (bf16[32,1024]{1,0:T(8,128)(2,1)S(1)}, bf16[32,1024]{1,0:T(8,128)(2,1)S(1)}, u32[]{:S(2)}, u32[]{:S(2)}) collective-permute-start(bf16[32,1024]{1,0:T(8,128)(2,1)S(1)} %collective-permute-done.3), channel_id=1, source_target_pairs={{0,4},{1,5},{2,6},{3,7},{4,0},{5,1},{6,2},{7,3},{8,12},{9,13},{10,... | collective-permute-start | bytes 196616 | tf_op jit(solution)/shard_map/ppermute | solution.py:21
  15.1 3.8 %collective-permute-start.4 = (bf16[4,32,1024]{2,1,0:T(8,128)(2,1)S(1)}, bf16[4,32,1024]{2,1,0:T(8,128)(2,1)S(1)}, u32[]{:S(2)}, u32[]{:S(2)}) collective-permute-start(bf16[4,32,1024]{2,1,0:T(8,128)(2,1)S(1)} %pad_maximum_fusion.refs_0_), channel_id=1, source_target_pairs={{0,1},{1,0},{2,3},{3,2},{4,5},{5,4},{6,7},{7,6},{8,9},{9,8},{10,11... | collective-permute-start | bytes 786440 | tf_op jit(solution)/shard_map/ppermute | solution.py:21
  18.3 1.6 %collective-permute-start.8 = (bf16[4,32,1024]{2,1,0:T(8,128)(2,1)S(1)}, bf16[4,32,1024]{2,1,0:T(8,128)(2,1)S(1)}, u32[]{:S(2)}, u32[]{:S(2)}) collective-permute-start(bf16[4,32,1024]{2,1,0:T(8,128)(2,1)S(1)} %pad_maximum_fusion.1.refs_2_), channel_id=1, source_target_pairs={{0,1},{1,0},{2,3},{3,2},{4,5},{5,4},{6,7},{7,6},{8,9},{9,8},{10,11... | collective-permute-start | bytes 786440 | tf_op jit(solution)/shard_map/ppermute | solution.py:21
  21.8 1.4 %collective-permute-start.11 = (bf16[2,32,1024]{2,1,0:T(8,128)(2,1)S(1)}, bf16[2,32,1024]{2,1,0:T(8,128)(2,1)S(1)}, u32[]{:S(2)}, u32[]{:S(2)}) collective-permute-start(bf16[2,32,1024]{2,1,0:T(8,128)(2,1)S(1)} %get-tuple-element.25), channel_id=1, source_target_pairs={{0,1},{1,0},{2,3},{3,2},{4,5},{5,4},{6,7},{7,6},{8,9},{9,8},{10,11... | collective-permute-start | bytes 393224 | tf_op jit(solution)/shard_map/ppermute | solution.py:21
  22.0 1.4 %collective-permute-start.12 = (bf16[2,32,1024]{2,1,0:T(8,128)(2,1)S(1)}, bf16[2,32,1024]{2,1,0:T(8,128)(2,1)S(1)}, u32[]{:S(2)}, u32[]{:S(2)}) collective-permute-start(bf16[2,32,1024]{2,1,0:T(8,128)(2,1)S(1)} %get-tuple-element.24), channel_id=1, source_target_pairs={{0,1},{1,0},{2,3},{3,2},{4,5},{5,4},{6,7},{7,6},{8,9},{9,8},{10,11... | collective-permute-start | bytes 393224 | tf_op jit(solution)/shard_map/ppermute | solution.py:21
  22.3 3.9 %collective-permute-start.10 = (bf16[2,32,1024]{2,1,0:T(8,128)(2,1)S(1)}, bf16[2,32,1024]{2,1,0:T(8,128)(2,1)S(1)}, u32[]{:S(2)}, u32[]{:S(2)}) collective-permute-start(bf16[2,32,1024]{2,1,0:T(8,128)(2,1)S(1)} %get-tuple-element.26), channel_id=1, source_target_pairs={{0,1},{1,0},{2,3},{3,2},{4,5},{5,4},{6,7},{7,6},{8,9},{9,8},{10,11... | collective-permute-start | bytes 393224 | tf_op jit(solution)/shard_map/ppermute | solution.py:21
  22.5 3.8 %collective-permute-start.9 = (bf16[2,32,1024]{2,1,0:T(8,128)(2,1)S(1)}, bf16[2,32,1024]{2,1,0:T(8,128)(2,1)S(1)}, u32[]{:S(2)}, u32[]{:S(2)}) collective-permute-start(bf16[2,32,1024]{2,1,0:T(8,128)(2,1)S(1)} %get-tuple-element.27), channel_id=1, source_target_pairs={{0,1},{1,0},{2,3},{3,2},{4,5},{5,4},{6,7},{7,6},{8,9},{9,8},{10,11... | collective-permute-start | bytes 393224 | tf_op jit(solution)/shard_map/ppermute | solution.py:21
  23.4 4.4 %collective-permute-start.13 = (bf16[32,1024]{1,0:T(8,128)(2,1)S(1)}, bf16[32,1024]{1,0:T(8,128)(2,1)S(1)}, u32[]{:S(2)}, u32[]{:S(2)}) collective-permute-start(bf16[32,1024]{1,0:T(8,128)(2,1)S(1)} %fusion.12), channel_id=1, source_target_pairs={{0,2},{1,3},{2,0},{3,1},{4,6},{5,7},{6,4},{7,5},{8,10},{9,11},{10,... | collective-permute-start | bytes 196616 | tf_op jit(solution)/shard_map/ppermute | solution.py:21
  24.0 5.2 %collective-permute-start.15 = (bf16[32,1024]{1,0:T(8,128)(2,1)S(1)}, bf16[32,1024]{1,0:T(8,128)(2,1)S(1)}, u32[]{:S(2)}, u32[]{:S(2)}) collective-permute-start(bf16[32,1024]{1,0:T(8,128)(2,1)S(1)} %get-tuple-element.30), channel_id=1, source_target_pairs={{0,4},{1,5},{2,6},{3,7},{4,0},{5,1},{6,2},{7,3},{8,12},{9,13},{10,... | collective-permute-start | bytes 196616 | tf_op jit(solution)/shard_map/ppermute | solution.py:21
  26.1 4.6 %collective-permute-start.17 = (bf16[32,1024]{1,0:T(8,128)(2,1)S(1)}, bf16[32,1024]{1,0:T(8,128)(2,1)S(1)}, u32[]{:S(2)}, u32[]{:S(2)}) collective-permute-start(bf16[32,1024]{1,0:T(8,128)(2,1)S(1)} %get-tuple-element.31), channel_id=1, source_target_pairs={{0,4},{1,5},{2,6},{3,7},{4,0},{5,1},{6,2},{7,3},{8,12},{9,13},{10,... | collective-permute-start | bytes 196616 | tf_op jit(solution)/shard_map/ppermute | solution.py:21
  26.3 9.0 %collective-permute-start.19 = (bf16[32,1024]{1,0:T(8,128)(2,1)S(1)}, bf16[32,1024]{1,0:T(8,128)(2,1)S(1)}, u32[]{:S(2)}, u32[]{:S(2)}) collective-permute-start(bf16[32,1024]{1,0:T(8,128)(2,1)S(1)} %fusion.13), channel_id=1, source_target_pairs={{0,2},{1,3},{2,0},{3,1},{4,6},{5,7},{6,4},{7,5},{8,10},{9,11},{10,... | collective-permute-start | bytes 196616 | tf_op jit(solution)/shard_map/ppermute | solution.py:21
  27.8 7.5 %collective-permute-start.14 = (bf16[32,1024]{1,0:T(8,128)(2,1)S(1)}, bf16[32,1024]{1,0:T(8,128)(2,1)S(1)}, u32[]{:S(2)}, u32[]{:S(2)}) collective-permute-start(bf16[32,1024]{1,0:T(8,128)(2,1)S(1)} %fusion.7), channel_id=1, source_target_pairs={{0,20},{1,21},{2,22},{3,23},{4,0},{5,1},{6,2},{7,3},{8,28},{9,29},... | collective-permute-start | bytes 196616 | tf_op jit(solution)/shard_map/ppermute | solution.py:21
  30.8 4.9 %collective-permute-start.16 = (bf16[32,1024]{1,0:T(8,128)(2,1)S(1)}, bf16[32,1024]{1,0:T(8,128)(2,1)S(1)}, u32[]{:S(2)}, u32[]{:S(2)}) collective-permute-start(bf16[32,1024]{1,0:T(8,128)(2,1)S(1)} %get-tuple-element.28), channel_id=1, source_target_pairs={{0,24},{1,25},{2,26},{3,27},{4,28},{5,29},{6,30},{7,31},{8,0},{9,1... | collective-permute-start | bytes 196616 | tf_op jit(solution)/shard_map/ppermute | solution.py:21
  31.7 5.2 %collective-permute-start.18 = (bf16[32,1024]{1,0:T(8,128)(2,1)S(1)}, bf16[32,1024]{1,0:T(8,128)(2,1)S(1)}, u32[]{:S(2)}, u32[]{:S(2)}) collective-permute-start(bf16[32,1024]{1,0:T(8,128)(2,1)S(1)} %get-tuple-element.29), channel_id=1, source_target_pairs={{0,26},{1,27},{2,24},{3,25},{4,30},{5,31},{6,28},{7,29},{8,2},{9,3... | collective-permute-start | bytes 196616 | tf_op jit(solution)/shard_map/ppermute | solution.py:21

commit v5 on v4

--- a/solution.py
+++ b/solution.py
@@ -66,7 +66,7 @@
     pieces = refs[:-5]
     own_rows, width = pieces[0].shape[1:]
     count_rows = grads_ref.shape[1]
-    lanes = 128 if count_rows % 128 == 0 else count_rows
+    lanes = count_rows
     slots, halves = send_ref.shape[:2]
     for number in range(slots * 2 * halves):
         slot, offset = divmod(number, 2 * halves)
@@ -142,6 +142,9 @@
     def across(offset):
         return lambda p, c: ((p + 1 + 2 * (p % 2)) % count_pb, c ^ offset)
 
+    def slant(offset):
+        return lambda p, c: ((p + 3 - 2 * (p % 2)) % count_pb, c ^ offset)
+
     def beside(p, c):
         return (p ^ 1, c)
 
@@ -239,12 +242,16 @@
     third = sums[2][0]
     for offset in evens[1:]:
         third = third + arrived(sums[2][offset // 2], own(offset))
-    seconds = [part + arrived(fourth, beside) for part, fourth in zip(sums[1], sums[3])]
-    group_grad = sums[0][0] + arrived(third, reverse(across(0)))
-    for offset in evens:
-        group_grad = group_grad + arrived(seconds[offset // 2], reverse(ahead(offset)))
+    group_grad = sums[0][0]
+    group_grad = group_grad + arrived(third, reverse(across(0)))
     for offset in evens[1:]:
         group_grad = group_grad + arrived(sums[0][offset // 2], own(offset))
+    group_grad = group_grad + arrived(sums[1][0], reverse(ahead(0)))
+    for offset in evens[1:]:
+        group_grad = group_grad + arrived(sums[1][offset // 2], reverse(ahead(offset)))
+    group_grad = group_grad + arrived(sums[3][0], reverse(slant(0)))
+    for offset in evens[1:]:
+        group_grad = group_grad + arrived(sums[3][offset // 2], reverse(slant(offset)))
     return (query_grad, group_grad)
 
 

time: 37.7 us -> 37.6 us (level)
  waiting for transfers between devices: 7.76 us -> 5.93 us
  starting transfers between devices: 22.8 us -> 24.5 us
    ppermute x20, waiting for transfers between devices: 7.76 us -> 5.93 us  [moved_to(): return lax.ppermute(block, ('pb', 'col'), pairs)]
    ppermute x20, starting transfers between devices: 22.8 us -> 24.5 us  [moved_to(): return lax.ppermute(block, ('pb', 'col'), pairs)]
  transfers between devices with their start and end apart: 20 -> 20, of which waited for: 8 -> 6; matrix products, arithmetic and copies ran while one was open for 4% -> 4% of each run, Pallas kernels for 5% -> 5%
where the time goes in v5:
time: 37.6 us; the launch traced here: 37.4 us
  starting transfers between devices  24.5 us (65%)
  waiting for transfers between devices  5.93 us (16%)
  Pallas kernels  3.74 us (10%)
  other arithmetic  2.34 us (6%)
  between operations  0.85 us (2%)
    ppermute x20, starting transfers between devices, moved_to(): return lax.ppermute(block, ('pb', 'col'), pairs)  24.5 us
    ppermute x20, waiting for transfers between devices, moved_to(): return lax.ppermute(block, ('pb', 'col'), pairs)  5.93 us
    pallas_call x1, Pallas kernels, on_device(): pl.pallas_call(functools.partial(grads_kernel, score_scale, places), out_...  1.75 us
    pallas_call x1, Pallas kernels, on_device(): pl.pallas_call(query_grad_kernel, out_shape=jax.ShapeDtypeStruct((count_r...  1.5 us
    concatenate x1, other arithmetic, on_device(): jnp.concatenate([jnp.concatenate([queries, teacher], axis=1), jnp.pad(gro...  1.37 us
  transfers between devices with their start and end apart: 20, of which 6 were waited for; matrix products, arithmetic and copies ran while one was open for 4% of the time, Pallas kernels for 5%

profile of v5, /device:TPU:0, one launch (start us, length us, event | category | flops | bytes accessed | tf_op | source)
XLA Modules:
  0.0 37.4 jit_solution(1018334264865297999)
XLA Ops:
  0.7 3.1 %collective-permute-start = (bf16[32,1024]{1,0:T(8,128)(2,1)}, bf16[32,1024]{1,0:T(8,128)(2,1)S(1)}, u32[]{:S(2)}, u32[]{:S(2)}) collective-permute-start(bf16[32,1024]{1,0:T(8,128)(2,1)} %param.6), channel_id=1, source_target_pairs={{0,8},{1,9},{2,10},{3,11},{4,12},{5,13},{6,14},{7,15},{8,16},{9,17... | collective-permute-start | bytes 196616 | tf_op jit(solution)/shard_map/ppermute | solution.py:21
  3.7 1.5 %collective-permute-start.5 = (bf16[32,1024]{1,0:T(8,128)(2,1)}, bf16[32,1024]{1,0:T(8,128)(2,1)S(1)}, u32[]{:S(2)}, u32[]{:S(2)}) collective-permute-start(bf16[32,1024]{1,0:T(8,128)(2,1)} %param.6), channel_id=1, source_target_pairs={{0,4},{1,5},{2,6},{3,7},{4,16},{5,17},{6,18},{7,19},{8,12},{9,13},... | collective-permute-start | bytes 196616 | tf_op jit(solution)/shard_map/ppermute | solution.py:21
  5.3 2.5 %collective-permute-start.3 = (bf16[32,1024]{1,0:T(8,128)(2,1)}, bf16[32,1024]{1,0:T(8,128)(2,1)S(1)}, u32[]{:S(2)}, u32[]{:S(2)}) collective-permute-start(bf16[32,1024]{1,0:T(8,128)(2,1)} %param.6), channel_id=1, source_target_pairs={{0,10},{1,11},{2,8},{3,9},{4,14},{5,15},{6,12},{7,13},{8,18},{9,19... | collective-permute-start | bytes 196616 | tf_op jit(solution)/shard_map/ppermute | solution.py:21
  7.8 1.4 %fusion.1.packed_ref = bf16[416,1536]{1,0:T(8,128)(2,1)S(1)} fusion(bf16[32,1024]{1,0:T(8,128)(2,1)} %param.6, bf16[384,512]{1,0:T(8,128)(2,1)} %param.7, bf16[384,1024]{1,0:T(8,128)(2,1)} %param.5), kind=kLoop, calls=%fused_computation.2 | loop fusion | flops 5111808 | bytes 2523136 | tf_op jit(solution)/shard_map/concatenate | solution.py:160
  9.2 0.8 %collective-permute-start.2 = (bf16[32,1024]{1,0:T(8,128)(2,1)S(1)}, bf16[32,1024]{1,0:T(8,128)(2,1)S(1)}, u32[]{:S(2)}, u32[]{:S(2)}) collective-permute-start(bf16[32,1024]{1,0:T(8,128)(2,1)S(1)} %copy-done.1), channel_id=1, source_target_pairs={{0,2},{1,3},{2,0},{3,1},{4,6},{5,7},{6,4},{7,5},{8,10},{9,11},{10,... | collective-permute-start | bytes 196616 | tf_op jit(solution)/shard_map/ppermute | solution.py:21
  9.9 2.0 %collective-permute-start.1 = (bf16[32,1024]{1,0:T(8,128)(2,1)S(1)}, bf16[32,1024]{1,0:T(8,128)(2,1)S(1)}, u32[]{:S(2)}, u32[]{:S(2)}) collective-permute-start(bf16[32,1024]{1,0:T(8,128)(2,1)S(1)} %collective-permute-done), channel_id=1, source_target_pairs={{0,4},{1,5},{2,6},{3,7},{4,0},{5,1},{6,2},{7,3},{8,12},{9,13},{10,... | collective-permute-start | bytes 196616 | tf_op jit(solution)/shard_map/ppermute | solution.py:21
  11.9 2.1 %collective-permute-start.6 = (bf16[32,1024]{1,0:T(8,128)(2,1)S(1)}, bf16[32,1024]{1,0:T(8,128)(2,1)S(1)}, u32[]{:S(2)}, u32[]{:S(2)}) collective-permute-start(bf16[32,1024]{1,0:T(8,128)(2,1)S(1)} %collective-permute-done.5), channel_id=1, source_target_pairs={{0,2},{1,3},{2,0},{3,1},{4,6},{5,7},{6,4},{7,5},{8,10},{9,11},{10,... | collective-permute-start | bytes 196616 | tf_op jit(solution)/shard_map/ppermute | solution.py:21
  14.0 1.0 %collective-permute-start.7 = (bf16[32,1024]{1,0:T(8,128)(2,1)S(1)}, bf16[32,1024]{1,0:T(8,128)(2,1)S(1)}, u32[]{:S(2)}, u32[]{:S(2)}) collective-permute-start(bf16[32,1024]{1,0:T(8,128)(2,1)S(1)} %collective-permute-done.3), channel_id=1, source_target_pairs={{0,4},{1,5},{2,6},{3,7},{4,0},{5,1},{6,2},{7,3},{8,12},{9,13},{10,... | collective-permute-start | bytes 196616 | tf_op jit(solution)/shard_map/ppermute | solution.py:21
  15.2 1.1 %collective-permute-done.6 = bf16[32,1024]{1,0:T(8,128)(2,1)S(1)} collective-permute-done((bf16[32,1024]{1,0:T(8,128)(2,1)S(1)}, bf16[32,1024]{1,0:T(8,128)(2,1)S(1)}, u32[]{:S(2)}, u32[]{:S(2)}) %collective-permute-start.6) | collective-permute-done | bytes 65568 | tf_op jit(solution)/shard_map/ppermute | solution.py:21
  16.3 2.0 %collective-permute-done.7 = bf16[32,1024]{1,0:T(8,128)(2,1)S(1)} collective-permute-done((bf16[32,1024]{1,0:T(8,128)(2,1)S(1)}, bf16[32,1024]{1,0:T(8,128)(2,1)S(1)}, u32[]{:S(2)}, u32[]{:S(2)}) %collective-permute-start.7) | collective-permute-done | bytes 65568 | tf_op jit(solution)/shard_map/ppermute | solution.py:21
  18.4 0.5 %shard_map.68.target_ref = f32[512,384]{1,0:T(8,128)S(1)} custom-call(s32[3,4]{1,0:T(4,128)S(1)} %copy-done, bf16[416,1536]{1,0:T(8,128)(2,1)S(1)} %fusion.1.packed_ref), custom_call_target="tpu_custom_call" | custom-call | flops 1572864 | bytes 1179648 | tf_op jit(solution)/shard_map/pallas_call | solution.py:170
  19.0 1.0 %collective-permute-done.8.refs_3_ = bf16[4,32,1024]{2,1,0:T(8,128)(2,1)S(1)} collective-permute-done((bf16[4,32,1024]{2,1,0:T(8,128)(2,1)S(1)}, bf16[4,32,1024]{2,1,0:T(8,128)(2,1)S(1)}, u32[]{:S(2)}, u32[]{:S(2)}) %collective-permute-start.8) | collective-permute-done | bytes 262176 | tf_op jit(solution)/shard_map/ppermute | solution.py:21
  19.9 1.8 %shard_map.69 = (bf16[512,384]{1,0:T(8,128)(2,1)S(1)}, bf16[512,1024]{1,0:T(8,128)(2,1)S(1)}, bf16[4,2,32,1024]{3,2,1,0:T(8,128)(2,1)S(1)}, bf16[4,2,32,1024]{3,2,1,0:T(8,128)(2,1)S(1)}) custom-call(bf16[416,1536]{1,0:T(8,128)(2,1)S(1)} %fusion.1.packed_ref, f32[512,384]{1,0:T(8,128)S(1)} %shard_map.68.target_ref, f32[1,384]{1,0:T(1,128)S(1)} %broadcast_in_dim.3.weights_ref, ...), custom_call_target="tpu_custom_call" | custom-call | flops 805306368 | bytes 4063232 | tf_op jit(solution)/shard_map/pallas_call | solution.py:194
  22.0 0.4 collective-permute-start.12
  23.2 0.6 %collective-permute-start.13 = (bf16[32,1024]{1,0:T(8,128)(2,1)S(1)}, bf16[32,1024]{1,0:T(8,128)(2,1)S(1)}, u32[]{:S(2)}, u32[]{:S(2)}) collective-permute-start(bf16[32,1024]{1,0:T(8,128)(2,1)S(1)} %fusion.10), channel_id=1, source_target_pairs={{0,2},{1,3},{2,0},{3,1},{4,6},{5,7},{6,4},{7,5},{8,10},{9,11},{10,... | collective-permute-start | bytes 196616 | tf_op jit(solution)/shard_map/ppermute | solution.py:21
  24.0 1.5 %collective-permute-start.15 = (bf16[32,1024]{1,0:T(8,128)(2,1)S(1)}, bf16[32,1024]{1,0:T(8,128)(2,1)S(1)}, u32[]{:S(2)}, u32[]{:S(2)}) collective-permute-start(bf16[32,1024]{1,0:T(8,128)(2,1)S(1)} %fusion.11), channel_id=1, source_target_pairs={{0,2},{1,3},{2,0},{3,1},{4,6},{5,7},{6,4},{7,5},{8,10},{9,11},{10,... | collective-permute-start | bytes 196616 | tf_op jit(solution)/shard_map/ppermute | solution.py:21
  25.5 2.1 %collective-permute-start.16 = (bf16[32,1024]{1,0:T(8,128)(2,1)S(1)}, bf16[32,1024]{1,0:T(8,128)(2,1)S(1)}, u32[]{:S(2)}, u32[]{:S(2)}) collective-permute-start(bf16[32,1024]{1,0:T(8,128)(2,1)S(1)} %get-tuple-element.29), channel_id=1, source_target_pairs={{0,24},{1,25},{2,26},{3,27},{4,28},{5,29},{6,30},{7,31},{8,0},{9,1... | collective-permute-start | bytes 196616 | tf_op jit(solution)/shard_map/ppermute | solution.py:21
  27.6 0.5 %collective-permute-start.17 = (bf16[32,1024]{1,0:T(8,128)(2,1)S(1)}, bf16[32,1024]{1,0:T(8,128)(2,1)S(1)}, u32[]{:S(2)}, u32[]{:S(2)}) collective-permute-start(bf16[32,1024]{1,0:T(8,128)(2,1)S(1)} %get-tuple-element.30), channel_id=1, source_target_pairs={{0,26},{1,27},{2,24},{3,25},{4,30},{5,31},{6,28},{7,29},{8,2},{9,3... | collective-permute-start | bytes 196616 | tf_op jit(solution)/shard_map/ppermute | solution.py:21
  28.1 0.7 %collective-permute-start.18 = (bf16[32,1024]{1,0:T(8,128)(2,1)S(1)}, bf16[32,1024]{1,0:T(8,128)(2,1)S(1)}, u32[]{:S(2)}, u32[]{:S(2)}) collective-permute-start(bf16[32,1024]{1,0:T(8,128)(2,1)S(1)} %get-tuple-element.31), channel_id=1, source_target_pairs={{0,28},{1,29},{2,30},{3,31},{4,24},{5,25},{6,26},{7,27},{8,4},{9,5... | collective-permute-start | bytes 196616 | tf_op jit(solution)/shard_map/ppermute | solution.py:21
  28.8 3.5 %collective-permute-start.19 = (bf16[32,1024]{1,0:T(8,128)(2,1)S(1)}, bf16[32,1024]{1,0:T(8,128)(2,1)S(1)}, u32[]{:S(2)}, u32[]{:S(2)}) collective-permute-start(bf16[32,1024]{1,0:T(8,128)(2,1)S(1)} %get-tuple-element.32), channel_id=1, source_target_pairs={{0,30},{1,31},{2,28},{3,29},{4,26},{5,27},{6,24},{7,25},{8,6},{9,7... | collective-permute-start | bytes 196616 | tf_op jit(solution)/shard_map/ppermute | solution.py:21
  32.4 1.3 %collective-permute-start.14 = (bf16[32,1024]{1,0:T(8,128)(2,1)S(1)}, bf16[32,1024]{1,0:T(8,128)(2,1)S(1)}, u32[]{:S(2)}, u32[]{:S(2)}) collective-permute-start(bf16[32,1024]{1,0:T(8,128)(2,1)S(1)} %fusion.3), channel_id=1, source_target_pairs={{0,20},{1,21},{2,22},{3,23},{4,0},{5,1},{6,2},{7,3},{8,28},{9,29},... | collective-permute-start | bytes 196616 | tf_op jit(solution)/shard_map/ppermute | solution.py:21
  33.7 1.5 %shard_map.70 = f32[384,1024]{1,0:T(8,128)} custom-call(bf16[512,384]{1,0:T(8,128)(2,1)S(1)} %get-tuple-element.15.grads_ref, bf16[512,1024]{1,0:T(8,128)(2,1)S(1)} %get-tuple-element.16.window_ref), custom_call_target="tpu_custom_call" | custom-call | flops 402653184 | bytes 3014656 | tf_op jit(solution)/shard_map/pallas_call | solution.py:214
  35.3 1.4 %collective-permute-done.14 = bf16[32,1024]{1,0:T(8,128)(2,1)S(1)} collective-permute-done((bf16[32,1024]{1,0:T(8,128)(2,1)S(1)}, bf16[32,1024]{1,0:T(8,128)(2,1)S(1)}, u32[]{:S(2)}, u32[]{:S(2)}) %collective-permute-start.14) | collective-permute-done | bytes 65568 | tf_op jit(solution)/shard_map/ppermute | solution.py:21
  36.7 0.7 %fusion.9 = f32[32,1024]{1,0:T(8,128)} fusion(f32[2,32,1024]{2,1,0:T(8,128)S(1)} %get-tuple-element.24, bf16[32,1024]{1,0:T(8,128)(2,1)S(1)} %collective-permute-done.19, bf16[32,1024]{1,0:T(8,128)(2,1)S(1)} %collective-permute-done.18, bf16[32,1024]{1,0:T(8,128)(2,1)S(1)} %collective-permute-done.17, bf16[32,1024]{1,0:T(8,128)(2,1)S(1)} %collective-permute-done.16, ...), kind=kLoop, calls=%fused_computation.20 | loop fusion | flops 393216 | bytes 655360 | tf_op jit(solution)/shard_map/add | solution.py:254
  (38 shorter events, 1.6 us)
Async XLA Ops:
  0.6 8.5 %copy-start.1 = (bf16[32,1024]{1,0:T(8,128)(2,1)S(1)}, bf16[32,1024]{1,0:T(8,128)(2,1)}, u32[]{:S(2)}) copy-start(bf16[32,1024]{1,0:T(8,128)(2,1)} %param.6) | copy-start | bytes 196612
  0.6 17.8 %copy-start.2 = (f32[384]{0:T(512)S(1)}, f32[384]{0:T(512)}, u32[]{:S(2)}) copy-start(f32[384]{0:T(512)} %param.9) | copy-start | bytes 4612
  0.7 17.8 %copy-start = (s32[3,4]{1,0:T(4,128)S(1)}, s32[3,4]{1,0:T(4,128)}, u32[]{:S(2)}) copy-start(s32[3,4]{1,0:T(4,128)} %mask_ref.1) | copy-start | bytes 148
  0.7 8.5 %collective-permute-start = (bf16[32,1024]{1,0:T(8,128)(2,1)}, bf16[32,1024]{1,0:T(8,128)(2,1)S(1)}, u32[]{:S(2)}, u32[]{:S(2)}) collective-permute-start(bf16[32,1024]{1,0:T(8,128)(2,1)} %param.6), channel_id=1, source_target_pairs={{0,8},{1,9},{2,10},{3,11},{4,12},{5,13},{6,14},{7,15},{8,16},{9,17... | collective-permute-start | bytes 196616 | tf_op jit(solution)/shard_map/ppermute | solution.py:21
  3.7 8.2 %collective-permute-start.5 = (bf16[32,1024]{1,0:T(8,128)(2,1)}, bf16[32,1024]{1,0:T(8,128)(2,1)S(1)}, u32[]{:S(2)}, u32[]{:S(2)}) collective-permute-start(bf16[32,1024]{1,0:T(8,128)(2,1)} %param.6), channel_id=1, source_target_pairs={{0,4},{1,5},{2,6},{3,7},{4,16},{5,17},{6,18},{7,19},{8,12},{9,13},... | collective-permute-start | bytes 196616 | tf_op jit(solution)/shard_map/ppermute | solution.py:21
  5.3 8.8 %collective-permute-start.3 = (bf16[32,1024]{1,0:T(8,128)(2,1)}, bf16[32,1024]{1,0:T(8,128)(2,1)S(1)}, u32[]{:S(2)}, u32[]{:S(2)}) collective-permute-start(bf16[32,1024]{1,0:T(8,128)(2,1)} %param.6), channel_id=1, source_target_pairs={{0,10},{1,11},{2,8},{3,9},{4,14},{5,15},{6,12},{7,13},{8,18},{9,19... | collective-permute-start | bytes 196616 | tf_op jit(solution)/shard_map/ppermute | solution.py:21
  9.2 5.9 %collective-permute-start.2 = (bf16[32,1024]{1,0:T(8,128)(2,1)S(1)}, bf16[32,1024]{1,0:T(8,128)(2,1)S(1)}, u32[]{:S(2)}, u32[]{:S(2)}) collective-permute-start(bf16[32,1024]{1,0:T(8,128)(2,1)S(1)} %copy-done.1), channel_id=1, source_target_pairs={{0,2},{1,3},{2,0},{3,1},{4,6},{5,7},{6,4},{7,5},{8,10},{9,11},{10,... | collective-permute-start | bytes 196616 | tf_op jit(solution)/shard_map/ppermute | solution.py:21
  9.9 8.4 %collective-permute-start.1 = (bf16[32,1024]{1,0:T(8,128)(2,1)S(1)}, bf16[32,1024]{1,0:T(8,128)(2,1)S(1)}, u32[]{:S(2)}, u32[]{:S(2)}) collective-permute-start(bf16[32,1024]{1,0:T(8,128)(2,1)S(1)} %collective-permute-done), channel_id=1, source_target_pairs={{0,4},{1,5},{2,6},{3,7},{4,0},{5,1},{6,2},{7,3},{8,12},{9,13},{10,... | collective-permute-start | bytes 196616 | tf_op jit(solution)/shard_map/ppermute | solution.py:21
  11.9 4.3 %collective-permute-start.6 = (bf16[32,1024]{1,0:T(8,128)(2,1)S(1)}, bf16[32,1024]{1,0:T(8,128)(2,1)S(1)}, u32[]{:S(2)}, u32[]{:S(2)}) collective-permute-start(bf16[32,1024]{1,0:T(8,128)(2,1)S(1)} %collective-permute-done.5), channel_id=1, source_target_pairs={{0,2},{1,3},{2,0},{3,1},{4,6},{5,7},{6,4},{7,5},{8,10},{9,11},{10,... | collective-permute-start | bytes 196616 | tf_op jit(solution)/shard_map/ppermute | solution.py:21
  14.0 4.3 %collective-permute-start.7 = (bf16[32,1024]{1,0:T(8,128)(2,1)S(1)}, bf16[32,1024]{1,0:T(8,128)(2,1)S(1)}, u32[]{:S(2)}, u32[]{:S(2)}) collective-permute-start(bf16[32,1024]{1,0:T(8,128)(2,1)S(1)} %collective-permute-done.3), channel_id=1, source_target_pairs={{0,4},{1,5},{2,6},{3,7},{4,0},{5,1},{6,2},{7,3},{8,12},{9,13},{10,... | collective-permute-start | bytes 196616 | tf_op jit(solution)/shard_map/ppermute | solution.py:21
  15.1 3.8 %collective-permute-start.4 = (bf16[4,32,1024]{2,1,0:T(8,128)(2,1)S(1)}, bf16[4,32,1024]{2,1,0:T(8,128)(2,1)S(1)}, u32[]{:S(2)}, u32[]{:S(2)}) collective-permute-start(bf16[4,32,1024]{2,1,0:T(8,128)(2,1)S(1)} %pad_maximum_fusion.refs_0_), channel_id=1, source_target_pairs={{0,1},{1,0},{2,3},{3,2},{4,5},{5,4},{6,7},{7,6},{8,9},{9,8},{10,11... | collective-permute-start | bytes 786440 | tf_op jit(solution)/shard_map/ppermute | solution.py:21
  18.3 1.6 %collective-permute-start.8 = (bf16[4,32,1024]{2,1,0:T(8,128)(2,1)S(1)}, bf16[4,32,1024]{2,1,0:T(8,128)(2,1)S(1)}, u32[]{:S(2)}, u32[]{:S(2)}) collective-permute-start(bf16[4,32,1024]{2,1,0:T(8,128)(2,1)S(1)} %pad_maximum_fusion.1.refs_2_), channel_id=1, source_target_pairs={{0,1},{1,0},{2,3},{3,2},{4,5},{5,4},{6,7},{7,6},{8,9},{9,8},{10,11... | collective-permute-start | bytes 786440 | tf_op jit(solution)/shard_map/ppermute | solution.py:21
  21.7 1.4 %collective-permute-start.11 = (bf16[2,32,1024]{2,1,0:T(8,128)(2,1)S(1)}, bf16[2,32,1024]{2,1,0:T(8,128)(2,1)S(1)}, u32[]{:S(2)}, u32[]{:S(2)}) collective-permute-start(bf16[2,32,1024]{2,1,0:T(8,128)(2,1)S(1)} %get-tuple-element.25), channel_id=1, source_target_pairs={{0,1},{1,0},{2,3},{3,2},{4,5},{5,4},{6,7},{7,6},{8,9},{9,8},{10,11... | collective-permute-start | bytes 393224 | tf_op jit(solution)/shard_map/ppermute | solution.py:21
  22.0 1.9 %collective-permute-start.12 = (bf16[2,32,1024]{2,1,0:T(8,128)(2,1)S(1)}, bf16[2,32,1024]{2,1,0:T(8,128)(2,1)S(1)}, u32[]{:S(2)}, u32[]{:S(2)}) collective-permute-start(bf16[2,32,1024]{2,1,0:T(8,128)(2,1)S(1)} %get-tuple-element.26), channel_id=1, source_target_pairs={{0,1},{1,0},{2,3},{3,2},{4,5},{5,4},{6,7},{7,6},{8,9},{9,8},{10,11... | collective-permute-start | bytes 393224 | tf_op jit(solution)/shard_map/ppermute | solution.py:21
  22.3 1.5 %collective-permute-start.10 = (bf16[2,32,1024]{2,1,0:T(8,128)(2,1)S(1)}, bf16[2,32,1024]{2,1,0:T(8,128)(2,1)S(1)}, u32[]{:S(2)}, u32[]{:S(2)}) collective-permute-start(bf16[2,32,1024]{2,1,0:T(8,128)(2,1)S(1)} %get-tuple-element.27), channel_id=1, source_target_pairs={{0,1},{1,0},{2,3},{3,2},{4,5},{5,4},{6,7},{7,6},{8,9},{9,8},{10,11... | collective-permute-start | bytes 393224 | tf_op jit(solution)/shard_map/ppermute | solution.py:21
  22.5 1.4 %collective-permute-start.9 = (bf16[2,32,1024]{2,1,0:T(8,128)(2,1)S(1)}, bf16[2,32,1024]{2,1,0:T(8,128)(2,1)S(1)}, u32[]{:S(2)}, u32[]{:S(2)}) collective-permute-start(bf16[2,32,1024]{2,1,0:T(8,128)(2,1)S(1)} %get-tuple-element.28), channel_id=1, source_target_pairs={{0,1},{1,0},{2,3},{3,2},{4,5},{5,4},{6,7},{7,6},{8,9},{9,8},{10,11... | collective-permute-start | bytes 393224 | tf_op jit(solution)/shard_map/ppermute | solution.py:21
  23.2 5.6 %collective-permute-start.13 = (bf16[32,1024]{1,0:T(8,128)(2,1)S(1)}, bf16[32,1024]{1,0:T(8,128)(2,1)S(1)}, u32[]{:S(2)}, u32[]{:S(2)}) collective-permute-start(bf16[32,1024]{1,0:T(8,128)(2,1)S(1)} %fusion.10), channel_id=1, source_target_pairs={{0,2},{1,3},{2,0},{3,1},{4,6},{5,7},{6,4},{7,5},{8,10},{9,11},{10,... | collective-permute-start | bytes 196616 | tf_op jit(solution)/shard_map/ppermute | solution.py:21
  24.0 8.4 %collective-permute-start.15 = (bf16[32,1024]{1,0:T(8,128)(2,1)S(1)}, bf16[32,1024]{1,0:T(8,128)(2,1)S(1)}, u32[]{:S(2)}, u32[]{:S(2)}) collective-permute-start(bf16[32,1024]{1,0:T(8,128)(2,1)S(1)} %fusion.11), channel_id=1, source_target_pairs={{0,2},{1,3},{2,0},{3,1},{4,6},{5,7},{6,4},{7,5},{8,10},{9,11},{10,... | collective-permute-start | bytes 196616 | tf_op jit(solution)/shard_map/ppermute | solution.py:21
  25.5 9.7 %collective-permute-start.16 = (bf16[32,1024]{1,0:T(8,128)(2,1)S(1)}, bf16[32,1024]{1,0:T(8,128)(2,1)S(1)}, u32[]{:S(2)}, u32[]{:S(2)}) collective-permute-start(bf16[32,1024]{1,0:T(8,128)(2,1)S(1)} %get-tuple-element.29), channel_id=1, source_target_pairs={{0,24},{1,25},{2,26},{3,27},{4,28},{5,29},{6,30},{7,31},{8,0},{9,1... | collective-permute-start | bytes 196616 | tf_op jit(solution)/shard_map/ppermute | solution.py:21
  27.6 7.7 %collective-permute-start.17 = (bf16[32,1024]{1,0:T(8,128)(2,1)S(1)}, bf16[32,1024]{1,0:T(8,128)(2,1)S(1)}, u32[]{:S(2)}, u32[]{:S(2)}) collective-permute-start(bf16[32,1024]{1,0:T(8,128)(2,1)S(1)} %get-tuple-element.30), channel_id=1, source_target_pairs={{0,26},{1,27},{2,24},{3,25},{4,30},{5,31},{6,28},{7,29},{8,2},{9,3... | collective-permute-start | bytes 196616 | tf_op jit(solution)/shard_map/ppermute | solution.py:21
  28.1 7.2 %collective-permute-start.18 = (bf16[32,1024]{1,0:T(8,128)(2,1)S(1)}, bf16[32,1024]{1,0:T(8,128)(2,1)S(1)}, u32[]{:S(2)}, u32[]{:S(2)}) collective-permute-start(bf16[32,1024]{1,0:T(8,128)(2,1)S(1)} %get-tuple-element.31), channel_id=1, source_target_pairs={{0,28},{1,29},{2,30},{3,31},{4,24},{5,25},{6,26},{7,27},{8,4},{9,5... | collective-permute-start | bytes 196616 | tf_op jit(solution)/shard_map/ppermute | solution.py:21
  28.8 6.5 %collective-permute-start.19 = (bf16[32,1024]{1,0:T(8,128)(2,1)S(1)}, bf16[32,1024]{1,0:T(8,128)(2,1)S(1)}, u32[]{:S(2)}, u32[]{:S(2)}) collective-permute-start(bf16[32,1024]{1,0:T(8,128)(2,1)S(1)} %get-tuple-element.32), channel_id=1, source_target_pairs={{0,30},{1,31},{2,28},{3,29},{4,26},{5,27},{6,24},{7,25},{8,6},{9,7... | collective-permute-start | bytes 196616 | tf_op jit(solution)/shard_map/ppermute | solution.py:21
  32.4 4.3 %collective-permute-start.14 = (bf16[32,1024]{1,0:T(8,128)(2,1)S(1)}, bf16[32,1024]{1,0:T(8,128)(2,1)S(1)}, u32[]{:S(2)}, u32[]{:S(2)}) collective-permute-start(bf16[32,1024]{1,0:T(8,128)(2,1)S(1)} %fusion.3), channel_id=1, source_target_pairs={{0,20},{1,21},{2,22},{3,23},{4,0},{5,1},{6,2},{7,3},{8,28},{9,29},... | collective-permute-start | bytes 196616 | tf_op jit(solution)/shard_map/ppermute | solution.py:21

commit v6 on v5

--- a/solution.py
+++ b/solution.py
@@ -233,7 +233,7 @@
 
     sums = {}
     last = None
-    for slot in (3, 2, 1, 0):
+    for slot in (2, 0, 3, 1):
         other = moved_to(send[slot], own(1))
         if last is not None:
             other = after(other, last)
@@ -242,16 +242,17 @@
     third = sums[2][0]
     for offset in evens[1:]:
         third = third + arrived(sums[2][offset // 2], own(offset))
+    sums[1][1:] = [after(block, third) for block in sums[1][1:]]
     group_grad = sums[0][0]
     group_grad = group_grad + arrived(third, reverse(across(0)))
+    group_grad = group_grad + arrived(sums[3][0], reverse(slant(0)))
+    for offset in evens[1:]:
+        group_grad = group_grad + arrived(sums[3][offset // 2], reverse(slant(offset)))
+    group_grad = group_grad + arrived(sums[1][0], reverse(ahead(0)))
+    for offset in evens[1:]:
+        group_grad = group_grad + arrived(sums[1][offset // 2], reverse(ahead(offset)))
     for offset in evens[1:]:
         group_grad = group_grad + arrived(sums[0][offset // 2], own(offset))
-    group_grad = group_grad + arrived(sums[1][0], reverse(ahead(0)))
-    for offset in evens[1:]:
-        group_grad = group_grad + arrived(sums[1][offset // 2], reverse(ahead(offset)))
-    group_grad = group_grad + arrived(sums[3][0], reverse(slant(0)))
-    for offset in evens[1:]:
-        group_grad = group_grad + arrived(sums[3][offset // 2], reverse(slant(offset)))
     return (query_grad, group_grad)
 
 

time: 37.6 us -> 37.6 us (level)
  starting transfers between devices: 24.5 us -> 24 us
  waiting for transfers between devices: 5.93 us -> 6.43 us
    ppermute x20, starting transfers between devices: 24.5 us -> 24 us  [moved_to(): return lax.ppermute(block, ('pb', 'col'), pairs)]
    ppermute x20, waiting for transfers between devices: 5.93 us -> 6.43 us  [moved_to(): return lax.ppermute(block, ('pb', 'col'), pairs)]
where the time goes in v6:
time: 37.6 us; the launch traced here: 37.4 us
  starting transfers between devices  24 us (64%)
  waiting for transfers between devices  6.43 us (17%)
  Pallas kernels  3.74 us (10%)
  other arithmetic  2.31 us (6%)
  between operations  0.87 us (2%)
    ppermute x20, starting transfers between devices, moved_to(): return lax.ppermute(block, ('pb', 'col'), pairs)  24 us
    ppermute x20, waiting for transfers between devices, moved_to(): return lax.ppermute(block, ('pb', 'col'), pairs)  6.43 us
    pallas_call x1, Pallas kernels, on_device(): pl.pallas_call(functools.partial(grads_kernel, score_scale, places), out_...  1.75 us
    pallas_call x1, Pallas kernels, on_device(): pl.pallas_call(query_grad_kernel, out_shape=jax.ShapeDtypeStruct((count_r...  1.5 us
    concatenate x1, other arithmetic, on_device(): jnp.concatenate([jnp.concatenate([queries, teacher], axis=1), jnp.pad(gro...  1.37 us
  transfers between devices with their start and end apart: 20, of which 6 were waited for; matrix products, arithmetic and copies ran while one was open for 4% of the time, Pallas kernels for 5%

profile of v6, /device:TPU:0, one launch (start us, length us, event | category | flops | bytes accessed | tf_op | source)
XLA Modules:
  0.0 37.4 jit_solution(6275116342141712042)
XLA Ops:
  0.7 3.1 %collective-permute-start = (bf16[32,1024]{1,0:T(8,128)(2,1)}, bf16[32,1024]{1,0:T(8,128)(2,1)S(1)}, u32[]{:S(2)}, u32[]{:S(2)}) collective-permute-start(bf16[32,1024]{1,0:T(8,128)(2,1)} %param.6), channel_id=1, source_target_pairs={{0,8},{1,9},{2,10},{3,11},{4,12},{5,13},{6,14},{7,15},{8,16},{9,17... | collective-permute-start | bytes 196616 | tf_op jit(solution)/shard_map/ppermute | solution.py:21
  3.7 1.5 %collective-permute-start.5 = (bf16[32,1024]{1,0:T(8,128)(2,1)}, bf16[32,1024]{1,0:T(8,128)(2,1)S(1)}, u32[]{:S(2)}, u32[]{:S(2)}) collective-permute-start(bf16[32,1024]{1,0:T(8,128)(2,1)} %param.6), channel_id=1, source_target_pairs={{0,4},{1,5},{2,6},{3,7},{4,16},{5,17},{6,18},{7,19},{8,12},{9,13},... | collective-permute-start | bytes 196616 | tf_op jit(solution)/shard_map/ppermute | solution.py:21
  5.3 2.5 %collective-permute-start.3 = (bf16[32,1024]{1,0:T(8,128)(2,1)}, bf16[32,1024]{1,0:T(8,128)(2,1)S(1)}, u32[]{:S(2)}, u32[]{:S(2)}) collective-permute-start(bf16[32,1024]{1,0:T(8,128)(2,1)} %param.6), channel_id=1, source_target_pairs={{0,10},{1,11},{2,8},{3,9},{4,14},{5,15},{6,12},{7,13},{8,18},{9,19... | collective-permute-start | bytes 196616 | tf_op jit(solution)/shard_map/ppermute | solution.py:21
  7.8 1.4 %fusion.1.packed_ref = bf16[416,1536]{1,0:T(8,128)(2,1)S(1)} fusion(bf16[32,1024]{1,0:T(8,128)(2,1)} %param.6, bf16[384,512]{1,0:T(8,128)(2,1)} %param.7, bf16[384,1024]{1,0:T(8,128)(2,1)} %param.5), kind=kLoop, calls=%fused_computation.2 | loop fusion | flops 5111808 | bytes 2523136 | tf_op jit(solution)/shard_map/concatenate | solution.py:160
  9.2 0.8 %collective-permute-start.2 = (bf16[32,1024]{1,0:T(8,128)(2,1)S(1)}, bf16[32,1024]{1,0:T(8,128)(2,1)S(1)}, u32[]{:S(2)}, u32[]{:S(2)}) collective-permute-start(bf16[32,1024]{1,0:T(8,128)(2,1)S(1)} %copy-done.1), channel_id=1, source_target_pairs={{0,2},{1,3},{2,0},{3,1},{4,6},{5,7},{6,4},{7,5},{8,10},{9,11},{10,... | collective-permute-start | bytes 196616 | tf_op jit(solution)/shard_map/ppermute | solution.py:21
  9.9 2.0 %collective-permute-start.1 = (bf16[32,1024]{1,0:T(8,128)(2,1)S(1)}, bf16[32,1024]{1,0:T(8,128)(2,1)S(1)}, u32[]{:S(2)}, u32[]{:S(2)}) collective-permute-start(bf16[32,1024]{1,0:T(8,128)(2,1)S(1)} %collective-permute-done), channel_id=1, source_target_pairs={{0,4},{1,5},{2,6},{3,7},{4,0},{5,1},{6,2},{7,3},{8,12},{9,13},{10,... | collective-permute-start | bytes 196616 | tf_op jit(solution)/shard_map/ppermute | solution.py:21
  11.9 2.1 %collective-permute-start.6 = (bf16[32,1024]{1,0:T(8,128)(2,1)S(1)}, bf16[32,1024]{1,0:T(8,128)(2,1)S(1)}, u32[]{:S(2)}, u32[]{:S(2)}) collective-permute-start(bf16[32,1024]{1,0:T(8,128)(2,1)S(1)} %collective-permute-done.5), channel_id=1, source_target_pairs={{0,2},{1,3},{2,0},{3,1},{4,6},{5,7},{6,4},{7,5},{8,10},{9,11},{10,... | collective-permute-start | bytes 196616 | tf_op jit(solution)/shard_map/ppermute | solution.py:21
  14.0 1.0 %collective-permute-start.7 = (bf16[32,1024]{1,0:T(8,128)(2,1)S(1)}, bf16[32,1024]{1,0:T(8,128)(2,1)S(1)}, u32[]{:S(2)}, u32[]{:S(2)}) collective-permute-start(bf16[32,1024]{1,0:T(8,128)(2,1)S(1)} %collective-permute-done.3), channel_id=1, source_target_pairs={{0,4},{1,5},{2,6},{3,7},{4,0},{5,1},{6,2},{7,3},{8,12},{9,13},{10,... | collective-permute-start | bytes 196616 | tf_op jit(solution)/shard_map/ppermute | solution.py:21
  15.2 1.1 %collective-permute-done.6 = bf16[32,1024]{1,0:T(8,128)(2,1)S(1)} collective-permute-done((bf16[32,1024]{1,0:T(8,128)(2,1)S(1)}, bf16[32,1024]{1,0:T(8,128)(2,1)S(1)}, u32[]{:S(2)}, u32[]{:S(2)}) %collective-permute-start.6) | collective-permute-done | bytes 65568 | tf_op jit(solution)/shard_map/ppermute | solution.py:21
  16.3 2.0 %collective-permute-done.7 = bf16[32,1024]{1,0:T(8,128)(2,1)S(1)} collective-permute-done((bf16[32,1024]{1,0:T(8,128)(2,1)S(1)}, bf16[32,1024]{1,0:T(8,128)(2,1)S(1)}, u32[]{:S(2)}, u32[]{:S(2)}) %collective-permute-start.7) | collective-permute-done | bytes 65568 | tf_op jit(solution)/shard_map/ppermute | solution.py:21
  18.4 0.5 %shard_map.68.target_ref = f32[512,384]{1,0:T(8,128)S(1)} custom-call(s32[3,4]{1,0:T(4,128)S(1)} %copy-done, bf16[416,1536]{1,0:T(8,128)(2,1)S(1)} %fusion.1.packed_ref), custom_call_target="tpu_custom_call" | custom-call | flops 1572864 | bytes 1179648 | tf_op jit(solution)/shard_map/pallas_call | solution.py:170
  19.0 1.0 %collective-permute-done.8.refs_3_ = bf16[4,32,1024]{2,1,0:T(8,128)(2,1)S(1)} collective-permute-done((bf16[4,32,1024]{2,1,0:T(8,128)(2,1)S(1)}, bf16[4,32,1024]{2,1,0:T(8,128)(2,1)S(1)}, u32[]{:S(2)}, u32[]{:S(2)}) %collective-permute-start.8) | collective-permute-done | bytes 262176 | tf_op jit(solution)/shard_map/ppermute | solution.py:21
  19.9 1.8 %shard_map.69 = (bf16[512,384]{1,0:T(8,128)(2,1)S(1)}, bf16[512,1024]{1,0:T(8,128)(2,1)S(1)}, bf16[4,2,32,1024]{3,2,1,0:T(8,128)(2,1)S(1)}, bf16[4,2,32,1024]{3,2,1,0:T(8,128)(2,1)S(1)}) custom-call(bf16[416,1536]{1,0:T(8,128)(2,1)S(1)} %fusion.1.packed_ref, f32[512,384]{1,0:T(8,128)S(1)} %shard_map.68.target_ref, f32[1,384]{1,0:T(1,128)S(1)} %broadcast_in_dim.3.weights_ref, ...), custom_call_target="tpu_custom_call" | custom-call | flops 805306368 | bytes 4063232 | tf_op jit(solution)/shard_map/pallas_call | solution.py:194
  23.2 2.1 %collective-permute-start.17 = (bf16[32,1024]{1,0:T(8,128)(2,1)S(1)}, bf16[32,1024]{1,0:T(8,128)(2,1)S(1)}, u32[]{:S(2)}, u32[]{:S(2)}) collective-permute-start(bf16[32,1024]{1,0:T(8,128)(2,1)S(1)} %get-tuple-element.30), channel_id=1, source_target_pairs={{0,24},{1,25},{2,26},{3,27},{4,28},{5,29},{6,30},{7,31},{8,0},{9,1... | collective-permute-start | bytes 196616 | tf_op jit(solution)/shard_map/ppermute | solution.py:21
  25.4 0.6 %collective-permute-start.11 = (bf16[32,1024]{1,0:T(8,128)(2,1)S(1)}, bf16[32,1024]{1,0:T(8,128)(2,1)S(1)}, u32[]{:S(2)}, u32[]{:S(2)}) collective-permute-start(bf16[32,1024]{1,0:T(8,128)(2,1)S(1)} %fusion.9), channel_id=1, source_target_pairs={{0,2},{1,3},{2,0},{3,1},{4,6},{5,7},{6,4},{7,5},{8,10},{9,11},{10,... | collective-permute-start | bytes 196616 | tf_op jit(solution)/shard_map/ppermute | solution.py:21
  26.1 1.6 %collective-permute-start.19 = (bf16[32,1024]{1,0:T(8,128)(2,1)S(1)}, bf16[32,1024]{1,0:T(8,128)(2,1)S(1)}, u32[]{:S(2)}, u32[]{:S(2)}) collective-permute-start(bf16[32,1024]{1,0:T(8,128)(2,1)S(1)} %fusion.11), channel_id=1, source_target_pairs={{0,2},{1,3},{2,0},{3,1},{4,6},{5,7},{6,4},{7,5},{8,10},{9,11},{10,... | collective-permute-start | bytes 196616 | tf_op jit(solution)/shard_map/ppermute | solution.py:21
  27.7 0.7 %collective-permute-start.14 = (bf16[32,1024]{1,0:T(8,128)(2,1)S(1)}, bf16[32,1024]{1,0:T(8,128)(2,1)S(1)}, u32[]{:S(2)}, u32[]{:S(2)}) collective-permute-start(bf16[32,1024]{1,0:T(8,128)(2,1)S(1)} %get-tuple-element.28), channel_id=1, source_target_pairs={{0,28},{1,29},{2,30},{3,31},{4,24},{5,25},{6,26},{7,27},{8,4},{9,5... | collective-permute-start | bytes 196616 | tf_op jit(solution)/shard_map/ppermute | solution.py:21
  28.4 1.1 %collective-permute-start.15 = (bf16[32,1024]{1,0:T(8,128)(2,1)S(1)}, bf16[32,1024]{1,0:T(8,128)(2,1)S(1)}, u32[]{:S(2)}, u32[]{:S(2)}) collective-permute-start(bf16[32,1024]{1,0:T(8,128)(2,1)S(1)} %get-tuple-element.29), channel_id=1, source_target_pairs={{0,30},{1,31},{2,28},{3,29},{4,26},{5,27},{6,24},{7,25},{8,6},{9,7... | collective-permute-start | bytes 196616 | tf_op jit(solution)/shard_map/ppermute | solution.py:21
  29.5 0.6 %collective-permute-done.11 = bf16[32,1024]{1,0:T(8,128)(2,1)S(1)} collective-permute-done((bf16[32,1024]{1,0:T(8,128)(2,1)S(1)}, bf16[32,1024]{1,0:T(8,128)(2,1)S(1)}, u32[]{:S(2)}, u32[]{:S(2)}) %collective-permute-start.11) | collective-permute-done | bytes 65568 | tf_op jit(solution)/shard_map/ppermute | solution.py:21
  30.0 2.4 %collective-permute-start.18 = (bf16[32,1024]{1,0:T(8,128)(2,1)S(1)}, bf16[32,1024]{1,0:T(8,128)(2,1)S(1)}, u32[]{:S(2)}, u32[]{:S(2)}) collective-permute-start(bf16[32,1024]{1,0:T(8,128)(2,1)S(1)} %get-tuple-element.23), channel_id=1, source_target_pairs={{0,26},{1,27},{2,24},{3,25},{4,30},{5,31},{6,28},{7,29},{8,2},{9,3... | collective-permute-start | bytes 196616 | tf_op jit(solution)/shard_map/ppermute | solution.py:21
  32.4 1.3 %collective-permute-start.12 = (bf16[32,1024]{1,0:T(8,128)(2,1)S(1)}, bf16[32,1024]{1,0:T(8,128)(2,1)S(1)}, u32[]{:S(2)}, u32[]{:S(2)}) collective-permute-start(bf16[32,1024]{1,0:T(8,128)(2,1)S(1)} %fusion.2), channel_id=1, source_target_pairs={{0,20},{1,21},{2,22},{3,23},{4,0},{5,1},{6,2},{7,3},{8,28},{9,29},... | collective-permute-start | bytes 196616 | tf_op jit(solution)/shard_map/ppermute | solution.py:21
  33.7 1.5 %shard_map.70 = f32[384,1024]{1,0:T(8,128)} custom-call(bf16[512,384]{1,0:T(8,128)(2,1)S(1)} %get-tuple-element.16.grads_ref, bf16[512,1024]{1,0:T(8,128)(2,1)S(1)} %get-tuple-element.17.window_ref), custom_call_target="tpu_custom_call" | custom-call | flops 402653184 | bytes 3014656 | tf_op jit(solution)/shard_map/pallas_call | solution.py:214
  35.3 1.4 %collective-permute-done.12 = bf16[32,1024]{1,0:T(8,128)(2,1)S(1)} collective-permute-done((bf16[32,1024]{1,0:T(8,128)(2,1)S(1)}, bf16[32,1024]{1,0:T(8,128)(2,1)S(1)}, u32[]{:S(2)}, u32[]{:S(2)}) %collective-permute-start.12) | collective-permute-done | bytes 65568 | tf_op jit(solution)/shard_map/ppermute | solution.py:21
  36.7 0.7 %fusion.8 = f32[32,1024]{1,0:T(8,128)} fusion(f32[2,32,1024]{2,1,0:T(8,128)S(1)} %convert_add_fusion.3, bf16[32,1024]{1,0:T(8,128)(2,1)S(1)} %collective-permute-done.19, bf16[32,1024]{1,0:T(8,128)(2,1)S(1)} %collective-permute-done.18, bf16[32,1024]{1,0:T(8,128)(2,1)S(1)} %collective-permute-done.17, bf16[32,1024]{1,0:T(8,128)(2,1)S(1)} %collective-permute-done.15, ...), kind=kLoop, calls=%fused_computation.21 | loop fusion | flops 393216 | bytes 655360 | tf_op jit(solution)/shard_map/add | solution.py:255
  (40 shorter events, 1.9 us)
Async XLA Ops:
  0.6 8.5 %copy-start.1 = (bf16[32,1024]{1,0:T(8,128)(2,1)S(1)}, bf16[32,1024]{1,0:T(8,128)(2,1)}, u32[]{:S(2)}) copy-start(bf16[32,1024]{1,0:T(8,128)(2,1)} %param.6) | copy-start | bytes 196612
  0.6 17.8 %copy-start.2 = (f32[384]{0:T(512)S(1)}, f32[384]{0:T(512)}, u32[]{:S(2)}) copy-start(f32[384]{0:T(512)} %param.9) | copy-start | bytes 4612
  0.7 17.8 %copy-start = (s32[3,4]{1,0:T(4,128)S(1)}, s32[3,4]{1,0:T(4,128)}, u32[]{:S(2)}) copy-start(s32[3,4]{1,0:T(4,128)} %mask_ref.1) | copy-start | bytes 148
  0.7 8.5 %collective-permute-start = (bf16[32,1024]{1,0:T(8,128)(2,1)}, bf16[32,1024]{1,0:T(8,128)(2,1)S(1)}, u32[]{:S(2)}, u32[]{:S(2)}) collective-permute-start(bf16[32,1024]{1,0:T(8,128)(2,1)} %param.6), channel_id=1, source_target_pairs={{0,8},{1,9},{2,10},{3,11},{4,12},{5,13},{6,14},{7,15},{8,16},{9,17... | collective-permute-start | bytes 196616 | tf_op jit(solution)/shard_map/ppermute | solution.py:21
  3.7 8.2 %collective-permute-start.5 = (bf16[32,1024]{1,0:T(8,128)(2,1)}, bf16[32,1024]{1,0:T(8,128)(2,1)S(1)}, u32[]{:S(2)}, u32[]{:S(2)}) collective-permute-start(bf16[32,1024]{1,0:T(8,128)(2,1)} %param.6), channel_id=1, source_target_pairs={{0,4},{1,5},{2,6},{3,7},{4,16},{5,17},{6,18},{7,19},{8,12},{9,13},... | collective-permute-start | bytes 196616 | tf_op jit(solution)/shard_map/ppermute | solution.py:21
  5.3 8.8 %collective-permute-start.3 = (bf16[32,1024]{1,0:T(8,128)(2,1)}, bf16[32,1024]{1,0:T(8,128)(2,1)S(1)}, u32[]{:S(2)}, u32[]{:S(2)}) collective-permute-start(bf16[32,1024]{1,0:T(8,128)(2,1)} %param.6), channel_id=1, source_target_pairs={{0,10},{1,11},{2,8},{3,9},{4,14},{5,15},{6,12},{7,13},{8,18},{9,19... | collective-permute-start | bytes 196616 | tf_op jit(solution)/shard_map/ppermute | solution.py:21
  9.2 5.9 %collective-permute-start.2 = (bf16[32,1024]{1,0:T(8,128)(2,1)S(1)}, bf16[32,1024]{1,0:T(8,128)(2,1)S(1)}, u32[]{:S(2)}, u32[]{:S(2)}) collective-permute-start(bf16[32,1024]{1,0:T(8,128)(2,1)S(1)} %copy-done.1), channel_id=1, source_target_pairs={{0,2},{1,3},{2,0},{3,1},{4,6},{5,7},{6,4},{7,5},{8,10},{9,11},{10,... | collective-permute-start | bytes 196616 | tf_op jit(solution)/shard_map/ppermute | solution.py:21
  9.9 8.4 %collective-permute-start.1 = (bf16[32,1024]{1,0:T(8,128)(2,1)S(1)}, bf16[32,1024]{1,0:T(8,128)(2,1)S(1)}, u32[]{:S(2)}, u32[]{:S(2)}) collective-permute-start(bf16[32,1024]{1,0:T(8,128)(2,1)S(1)} %collective-permute-done), channel_id=1, source_target_pairs={{0,4},{1,5},{2,6},{3,7},{4,0},{5,1},{6,2},{7,3},{8,12},{9,13},{10,... | collective-permute-start | bytes 196616 | tf_op jit(solution)/shard_map/ppermute | solution.py:21
  11.9 4.3 %collective-permute-start.6 = (bf16[32,1024]{1,0:T(8,128)(2,1)S(1)}, bf16[32,1024]{1,0:T(8,128)(2,1)S(1)}, u32[]{:S(2)}, u32[]{:S(2)}) collective-permute-start(bf16[32,1024]{1,0:T(8,128)(2,1)S(1)} %collective-permute-done.5), channel_id=1, source_target_pairs={{0,2},{1,3},{2,0},{3,1},{4,6},{5,7},{6,4},{7,5},{8,10},{9,11},{10,... | collective-permute-start | bytes 196616 | tf_op jit(solution)/shard_map/ppermute | solution.py:21
  14.0 4.3 %collective-permute-start.7 = (bf16[32,1024]{1,0:T(8,128)(2,1)S(1)}, bf16[32,1024]{1,0:T(8,128)(2,1)S(1)}, u32[]{:S(2)}, u32[]{:S(2)}) collective-permute-start(bf16[32,1024]{1,0:T(8,128)(2,1)S(1)} %collective-permute-done.3), channel_id=1, source_target_pairs={{0,4},{1,5},{2,6},{3,7},{4,0},{5,1},{6,2},{7,3},{8,12},{9,13},{10,... | collective-permute-start | bytes 196616 | tf_op jit(solution)/shard_map/ppermute | solution.py:21
  15.1 3.8 %collective-permute-start.4 = (bf16[4,32,1024]{2,1,0:T(8,128)(2,1)S(1)}, bf16[4,32,1024]{2,1,0:T(8,128)(2,1)S(1)}, u32[]{:S(2)}, u32[]{:S(2)}) collective-permute-start(bf16[4,32,1024]{2,1,0:T(8,128)(2,1)S(1)} %pad_maximum_fusion.refs_0_), channel_id=1, source_target_pairs={{0,1},{1,0},{2,3},{3,2},{4,5},{5,4},{6,7},{7,6},{8,9},{9,8},{10,11... | collective-permute-start | bytes 786440 | tf_op jit(solution)/shard_map/ppermute | solution.py:21
  18.3 1.6 %collective-permute-start.8 = (bf16[4,32,1024]{2,1,0:T(8,128)(2,1)S(1)}, bf16[4,32,1024]{2,1,0:T(8,128)(2,1)S(1)}, u32[]{:S(2)}, u32[]{:S(2)}) collective-permute-start(bf16[4,32,1024]{2,1,0:T(8,128)(2,1)S(1)} %pad_maximum_fusion.1.refs_2_), channel_id=1, source_target_pairs={{0,1},{1,0},{2,3},{3,2},{4,5},{5,4},{6,7},{7,6},{8,9},{9,8},{10,11... | collective-permute-start | bytes 786440 | tf_op jit(solution)/shard_map/ppermute | solution.py:21
  21.7 1.4 %collective-permute-start.16 = (bf16[2,32,1024]{2,1,0:T(8,128)(2,1)S(1)}, bf16[2,32,1024]{2,1,0:T(8,128)(2,1)S(1)}, u32[]{:S(2)}, u32[]{:S(2)}) collective-permute-start(bf16[2,32,1024]{2,1,0:T(8,128)(2,1)S(1)} %get-tuple-element.25), channel_id=1, source_target_pairs={{0,1},{1,0},{2,3},{3,2},{4,5},{5,4},{6,7},{7,6},{8,9},{9,8},{10,11... | collective-permute-start | bytes 393224 | tf_op jit(solution)/shard_map/ppermute | solution.py:21
  22.0 4.1 %collective-permute-start.13 = (bf16[2,32,1024]{2,1,0:T(8,128)(2,1)S(1)}, bf16[2,32,1024]{2,1,0:T(8,128)(2,1)S(1)}, u32[]{:S(2)}, u32[]{:S(2)}) collective-permute-start(bf16[2,32,1024]{2,1,0:T(8,128)(2,1)S(1)} %get-tuple-element.24), channel_id=1, source_target_pairs={{0,1},{1,0},{2,3},{3,2},{4,5},{5,4},{6,7},{7,6},{8,9},{9,8},{10,11... | collective-permute-start | bytes 393224 | tf_op jit(solution)/shard_map/ppermute | solution.py:21
  22.3 3.0 %collective-permute-start.10 = (bf16[2,32,1024]{2,1,0:T(8,128)(2,1)S(1)}, bf16[2,32,1024]{2,1,0:T(8,128)(2,1)S(1)}, u32[]{:S(2)}, u32[]{:S(2)}) collective-permute-start(bf16[2,32,1024]{2,1,0:T(8,128)(2,1)S(1)} %get-tuple-element.26), channel_id=1, source_target_pairs={{0,1},{1,0},{2,3},{3,2},{4,5},{5,4},{6,7},{7,6},{8,9},{9,8},{10,11... | collective-permute-start | bytes 393224 | tf_op jit(solution)/shard_map/ppermute | solution.py:21
  22.5 3.5 %collective-permute-start.9 = (bf16[2,32,1024]{2,1,0:T(8,128)(2,1)S(1)}, bf16[2,32,1024]{2,1,0:T(8,128)(2,1)S(1)}, u32[]{:S(2)}, u32[]{:S(2)}) collective-permute-start(bf16[2,32,1024]{2,1,0:T(8,128)(2,1)S(1)} %get-tuple-element.27), channel_id=1, source_target_pairs={{0,1},{1,0},{2,3},{3,2},{4,5},{5,4},{6,7},{7,6},{8,9},{9,8},{10,11... | collective-permute-start | bytes 393224 | tf_op jit(solution)/shard_map/ppermute | solution.py:21
  23.2 9.2 %collective-permute-start.17 = (bf16[32,1024]{1,0:T(8,128)(2,1)S(1)}, bf16[32,1024]{1,0:T(8,128)(2,1)S(1)}, u32[]{:S(2)}, u32[]{:S(2)}) collective-permute-start(bf16[32,1024]{1,0:T(8,128)(2,1)S(1)} %get-tuple-element.30), channel_id=1, source_target_pairs={{0,24},{1,25},{2,26},{3,27},{4,28},{5,29},{6,30},{7,31},{8,0},{9,1... | collective-permute-start | bytes 196616 | tf_op jit(solution)/shard_map/ppermute | solution.py:21
  25.4 4.6 %collective-permute-start.11 = (bf16[32,1024]{1,0:T(8,128)(2,1)S(1)}, bf16[32,1024]{1,0:T(8,128)(2,1)S(1)}, u32[]{:S(2)}, u32[]{:S(2)}) collective-permute-start(bf16[32,1024]{1,0:T(8,128)(2,1)S(1)} %fusion.9), channel_id=1, source_target_pairs={{0,2},{1,3},{2,0},{3,1},{4,6},{5,7},{6,4},{7,5},{8,10},{9,11},{10,... | collective-permute-start | bytes 196616 | tf_op jit(solution)/shard_map/ppermute | solution.py:21
  26.1 9.1 %collective-permute-start.19 = (bf16[32,1024]{1,0:T(8,128)(2,1)S(1)}, bf16[32,1024]{1,0:T(8,128)(2,1)S(1)}, u32[]{:S(2)}, u32[]{:S(2)}) collective-permute-start(bf16[32,1024]{1,0:T(8,128)(2,1)S(1)} %fusion.11), channel_id=1, source_target_pairs={{0,2},{1,3},{2,0},{3,1},{4,6},{5,7},{6,4},{7,5},{8,10},{9,11},{10,... | collective-permute-start | bytes 196616 | tf_op jit(solution)/shard_map/ppermute | solution.py:21
  27.7 7.6 %collective-permute-start.14 = (bf16[32,1024]{1,0:T(8,128)(2,1)S(1)}, bf16[32,1024]{1,0:T(8,128)(2,1)S(1)}, u32[]{:S(2)}, u32[]{:S(2)}) collective-permute-start(bf16[32,1024]{1,0:T(8,128)(2,1)S(1)} %get-tuple-element.28), channel_id=1, source_target_pairs={{0,28},{1,29},{2,30},{3,31},{4,24},{5,25},{6,26},{7,27},{8,4},{9,5... | collective-permute-start | bytes 196616 | tf_op jit(solution)/shard_map/ppermute | solution.py:21
  28.4 6.9 %collective-permute-start.15 = (bf16[32,1024]{1,0:T(8,128)(2,1)S(1)}, bf16[32,1024]{1,0:T(8,128)(2,1)S(1)}, u32[]{:S(2)}, u32[]{:S(2)}) collective-permute-start(bf16[32,1024]{1,0:T(8,128)(2,1)S(1)} %get-tuple-element.29), channel_id=1, source_target_pairs={{0,30},{1,31},{2,28},{3,29},{4,26},{5,27},{6,24},{7,25},{8,6},{9,7... | collective-permute-start | bytes 196616 | tf_op jit(solution)/shard_map/ppermute | solution.py:21
  30.0 5.2 %collective-permute-start.18 = (bf16[32,1024]{1,0:T(8,128)(2,1)S(1)}, bf16[32,1024]{1,0:T(8,128)(2,1)S(1)}, u32[]{:S(2)}, u32[]{:S(2)}) collective-permute-start(bf16[32,1024]{1,0:T(8,128)(2,1)S(1)} %get-tuple-element.23), channel_id=1, source_target_pairs={{0,26},{1,27},{2,24},{3,25},{4,30},{5,31},{6,28},{7,29},{8,2},{9,3... | collective-permute-start | bytes 196616 | tf_op jit(solution)/shard_map/ppermute | solution.py:21
  32.4 4.3 %collective-permute-start.12 = (bf16[32,1024]{1,0:T(8,128)(2,1)S(1)}, bf16[32,1024]{1,0:T(8,128)(2,1)S(1)}, u32[]{:S(2)}, u32[]{:S(2)}) collective-permute-start(bf16[32,1024]{1,0:T(8,128)(2,1)S(1)} %fusion.2), channel_id=1, source_target_pairs={{0,20},{1,21},{2,22},{3,23},{4,0},{5,1},{6,2},{7,3},{8,28},{9,29},... | collective-permute-start | bytes 196616 | tf_op jit(solution)/shard_map/ppermute | solution.py:21
